TPU v7x, 32 devices: a whole 2x2x4 slice. The times are simulated.
32 devices in a mesh: dp: 4 (over y, x), ctx: 8 (over z, core).
Axes of the slice: x: 2, y: 2, z: 4, core: 2. Of those that a mesh axis runs over, the one named last changes fastest.
Arguments:
- tokens: bfloat16 [16, 1024, 1024], P('dp', 'ctx'), may hold values from -6 to 6
- cotangent: bfloat16 [16, 1024, 1024], P('dp', 'ctx'), may hold values from -6 to 6
- lengths: int32 [16], P('dp'), may hold values from 256 to 1024, as said below
- weights: float32 [12288, 1024], P('ctx'), may hold values from -1 to 1
- vectors: float32 [12288], P('ctx'), may hold values from -1.2 to 1.5
- first_weights: float32 [12288, 1024], P('ctx'), may hold values from -384 to 384
- second_weights: float32 [12288, 1024], P('ctx'), may hold values from 0.8192 to 81.92
- first_vectors: float32 [12288], P('ctx'), may hold values from -384 to 384
- second_vectors: float32 [12288], P('ctx'), may hold values from 0.8192 to 81.92
Outputs:
- layer_out: bfloat16 [16, 1024, 1024], P('dp', 'ctx')
- grad_tokens: bfloat16 [16, 1024, 1024], P('dp', 'ctx')
- grad_weights: float32 [12288, 1024], P('ctx')
- grad_vectors: float32 [12288], P('ctx')
- weight_change: float32 [12288, 1024], P('ctx')
- vector_change: float32 [12288], P('ctx')
- new_first_weights: float32 [12288, 1024], P('ctx')
- new_second_weights: float32 [12288, 1024], P('ctx')
- new_first_vectors: float32 [12288], P('ctx')
- new_second_vectors: float32 [12288], P('ctx')
Inputs may be any that keep to these rules, and one draw needn't show every extreme that they name: `lengths`: in each run of 4 sequences that share an index of dp, one, drawn, has length 1024.
All inputs are finite; a program needn't handle non-finite values.
Results may differ from a plain program's by a relative error of at most 0.018.
Values may be sent and summed in bfloat16 or wider, within the bound.
No kernel may reach another device: no remote copies, remote signals or barrier semaphores. Data moves between devices by JAX's collectives and lax.ppermute only.
A program may use at most 320 MiB of HBM per device.

v0:
```python
import math

import jax
import jax.numpy as jnp
from jax import lax
from jax.sharding import PartitionSpec as P

D = 1024
FF = 4096
H = 16
HD = 64
STEP = 10


EPSILON = 1e-05
LEARN_RATE = 0.003


def times_rows(operand, matrix):
    return lax.dot_general(
        operand, matrix, (((1,), (1,)), ((), ())), preferred_element_type=jnp.float32
    )


def times_cols(operand, matrix):
    return lax.dot_general(
        operand, matrix, (((0,), (0,)), ((), ())), preferred_element_type=jnp.float32
    )


def exact_gelu(inputs):
    return jax.nn.gelu(inputs, approximate=False)


def layer_norm(inputs, gain_vec, shift_vec):
    centre = jnp.mean(inputs, axis=-1, keepdims=True)
    shifted = inputs - centre
    inverse = lax.rsqrt(jnp.mean(shifted * shifted, axis=-1, keepdims=True) + EPSILON)
    normed = shifted * inverse
    return (normed * gain_vec + shift_vec, normed, inverse)


def norm_back(grad_out, normed, inverse, gain_vec):
    scaled = grad_out * gain_vec
    inner_term = (
        scaled
        - jnp.mean(scaled, axis=-1, keepdims=True)
        - normed * jnp.mean(scaled * normed, axis=-1, keepdims=True)
    )
    return (inverse * inner_term, jnp.sum(grad_out * normed, axis=0), jnp.sum(grad_out, axis=0))


def split_matrices(packed):
    return (
        packed[: 3 * D],
        packed[3 * D : 4 * D],
        packed[4 * D : 4 * D + FF],
        packed[4 * D + FF :],
    )


def split_vectors(packed):
    bounds = [
        0,
        D,
        2 * D,
        3 * D,
        3 * D + FF,
        4 * D + FF,
        5 * D + FF,
        6 * D + FF,
        7 * D + FF,
        8 * D + FF,
    ]
    return [packed[bounds[number] : bounds[number + 1]] for number in range(9)]


def attention_scores(queries_h, keys_h, allowed):
    scores = jnp.einsum(
        "bqhd,bkhd->bhqk", queries_h, keys_h, preferred_element_type=jnp.float32
    ) / math.sqrt(HD)
    return jnp.where(allowed, scores, -1e30)


def forward(tokens, lengths, matrix_set, vector_set):
    groups, per_device, width = tokens.shape
    wqkv_rows, wout_rows, wup_rows, wdown_rows = matrix_set
    bias_q, bias_v, bias_o, bias_up, bias_down, gain_one, shift_one, gain_two, shift_two = (
        vector_set
    )
    flat_rows = tokens.reshape(groups * per_device, width)
    merged = times_rows(flat_rows, wqkv_rows)
    queries = (merged[:, :width] + bias_q).astype(jnp.bfloat16)
    keys_local = (
        merged[:, width : 2 * width].astype(jnp.bfloat16).reshape(groups, per_device, width)
    )
    values_local = (
        (merged[:, 2 * width :] + bias_v).astype(jnp.bfloat16).reshape(groups, per_device, width)
    )
    keys_all, values_all = (
        lax.all_gather(keys_local, "ctx", axis=1, tiled=True),
        lax.all_gather(values_local, "ctx", axis=1, tiled=True),
    )
    span = keys_all.shape[1]
    queries_h = queries.reshape(groups, per_device, H, HD)
    keys_h = keys_all.reshape(groups, span, H, HD)
    values_h = values_all.reshape(groups, span, H, HD)
    allowed = (jnp.arange(span, dtype=jnp.int32)[None, :] < lengths[:, None])[:, None, None, :]
    scores = attention_scores(queries_h, keys_h, allowed)
    highest = jnp.max(scores, axis=-1, keepdims=True)
    expo_terms = jnp.exp(scores - highest)
    denominator = jnp.sum(expo_terms, axis=-1, keepdims=True)
    probs_low = (expo_terms / denominator).astype(jnp.bfloat16)
    log_total = highest + jnp.log(denominator)
    attended = jnp.einsum(
        "bhqk,bkhd->bqhd", probs_low, values_h, preferred_element_type=jnp.float32
    )
    heads_out = attended.reshape(groups * per_device, width).astype(jnp.bfloat16)
    branch = times_rows(heads_out, wout_rows) + bias_o
    normed_in, normed_one, inverse_one = layer_norm(
        flat_rows.astype(jnp.float32) + branch, gain_one, shift_one
    )
    upper_low = normed_in.astype(jnp.bfloat16)
    gate_in = times_rows(upper_low, wup_rows) + bias_up
    hidden_low = exact_gelu(gate_in).astype(jnp.bfloat16)
    feed_out = jnp.dot(hidden_low, wdown_rows, preferred_element_type=jnp.float32) + bias_down
    result, normed_two, inverse_two = layer_norm(
        upper_low.astype(jnp.float32) + feed_out, gain_two, shift_two
    )
    saved = (
        flat_rows,
        queries_h,
        keys_h,
        values_h,
        allowed,
        log_total,
        heads_out,
        normed_one,
        inverse_one,
        upper_low,
        gate_in,
        hidden_low,
        normed_two,
        inverse_two,
    )
    return (result.astype(jnp.bfloat16).reshape(tokens.shape), saved)


def backward(grad_out, saved, matrix_set, vector_set):
    (
        flat_rows,
        queries_h,
        keys_h,
        values_h,
        allowed,
        log_total,
        heads_out,
        normed_one,
        inverse_one,
        upper_low,
        gate_in,
        hidden_low,
        normed_two,
        inverse_two,
    ) = saved
    wqkv_rows, wout_rows, wup_rows, wdown_rows = matrix_set
    gain_one = vector_set[5]
    gain_two = vector_set[7]
    grad_two, grad_gain_two, grad_shift_two = norm_back(grad_out, normed_two, inverse_two, gain_two)
    feed_low = grad_two.astype(jnp.bfloat16)
    grad_down = times_cols(hidden_low, feed_low)
    grad_bias_down = jnp.sum(feed_low.astype(jnp.float32), axis=0)
    grad_hidden = times_rows(feed_low, wdown_rows)
    gate_pull = jax.vjp(exact_gelu, gate_in)[1]
    gate_low = gate_pull(grad_hidden)[0].astype(jnp.bfloat16)
    grad_up = times_cols(gate_low, upper_low)
    grad_bias_up = jnp.sum(gate_low.astype(jnp.float32), axis=0)
    grad_upper = jnp.dot(gate_low, wup_rows, preferred_element_type=jnp.float32) + grad_two
    grad_one, grad_gain_one, grad_shift_one = norm_back(
        grad_upper, normed_one, inverse_one, gain_one
    )
    branch_low = grad_one.astype(jnp.bfloat16)
    grad_out_proj = times_cols(branch_low, heads_out)
    grad_bias_o = jnp.sum(branch_low.astype(jnp.float32), axis=0)
    heads_grad = jnp.dot(branch_low, wout_rows, preferred_element_type=jnp.float32).astype(
        jnp.bfloat16
    )
    groups, span = (keys_h.shape[0], keys_h.shape[1])
    per_device = queries_h.shape[1]
    scale_factor = 1.0 / math.sqrt(HD)
    grad_heads = heads_grad.reshape(groups, per_device, H, HD)
    probs = jnp.exp(attention_scores(queries_h, keys_h, allowed) - log_total)
    grad_probs = jnp.einsum(
        "bqhd,bkhd->bhqk", grad_heads, values_h, preferred_element_type=jnp.float32
    )
    row_sums = jnp.sum(grad_probs * probs, axis=-1, keepdims=True)
    grad_scores = (probs * (grad_probs - row_sums)).astype(jnp.bfloat16)
    grad_queries = (
        jnp.einsum("bhqk,bkhd->bqhd", grad_scores, keys_h, preferred_element_type=jnp.float32)
        * scale_factor
    ).astype(jnp.bfloat16)
    probs_low = probs.astype(jnp.bfloat16)
    grad_values = jnp.einsum(
        "bhqk,bqhd->bkhd", probs_low, grad_heads, preferred_element_type=jnp.float32
    )
    grad_keys = (
        jnp.einsum("bhqk,bqhd->bkhd", grad_scores, queries_h, preferred_element_type=jnp.float32)
        * scale_factor
    )
    grad_keys, grad_values = (
        lax.psum_scatter(
            grad_keys.reshape(groups, span, D).astype(jnp.bfloat16),
            "ctx",
            scatter_dimension=1,
            tiled=True,
        ).astype(jnp.float32),
        lax.psum_scatter(
            grad_values.reshape(groups, span, D).astype(jnp.bfloat16),
            "ctx",
            scatter_dimension=1,
            tiled=True,
        ).astype(jnp.float32),
    )
    flat_q = grad_queries.reshape(groups * per_device, D)
    flat_k = grad_keys.astype(jnp.bfloat16).reshape(groups * per_device, D)
    flat_v = grad_values.astype(jnp.bfloat16).reshape(groups * per_device, D)
    grad_merged = jnp.concatenate([flat_q, flat_k, flat_v], axis=1)
    grad_qkv = times_cols(grad_merged, flat_rows)
    grad_rows = grad_one + jnp.dot(grad_merged, wqkv_rows, preferred_element_type=jnp.float32)
    grad_bias_q = jnp.sum(flat_q.astype(jnp.float32), axis=0)
    grad_bias_v = jnp.sum(flat_v.astype(jnp.float32), axis=0)
    matrix_grad = jnp.concatenate([grad_qkv, grad_out_proj, grad_up, grad_down], axis=0)
    vector_grad = jnp.concatenate(
        [
            grad_bias_q,
            grad_bias_v,
            grad_bias_o,
            grad_bias_up,
            grad_bias_down,
            grad_gain_one,
            grad_shift_one,
            grad_gain_two,
            grad_shift_two,
        ]
    )
    return (grad_rows, matrix_grad, vector_grad)


def adamw_update(parameter, gradient, first_old, second_old, decay_rate):
    step_float = float(STEP)
    first_new = 0.9 * first_old + 0.1 * gradient
    second_new = 0.999 * second_old + 0.001 * gradient * gradient
    first_fix = first_new / (1.0 - 0.9**step_float)
    second_fix = second_new / (1.0 - 0.999**step_float)
    update = first_fix / (jnp.sqrt(second_fix) + 1e-08)
    return (-LEARN_RATE * (update + decay_rate * parameter), first_new, second_new)


def shards(
    tokens,
    cotangent,
    lengths,
    weights,
    vectors,
    first_weights,
    second_weights,
    first_vectors,
    second_vectors,
):
    gathered_w, gathered_v = (
        lax.all_gather(weights.astype(jnp.bfloat16), "ctx", axis=0, tiled=True),
        lax.all_gather(vectors.astype(jnp.bfloat16), "ctx", axis=0, tiled=True),
    )
    matrix_set = split_matrices(gathered_w)
    vector_set = split_vectors(gathered_v.astype(jnp.float32))
    layer_out, saved = forward(tokens, lengths, matrix_set, vector_set)
    again = lax.optimization_barrier((tokens, gathered_w, gathered_v, layer_out))
    matrix_set = split_matrices(again[1])
    vector_set = split_vectors(again[2].astype(jnp.float32))
    saved = forward(again[0], lengths, matrix_set, vector_set)[1]
    groups, per_device, width = tokens.shape
    positions = lax.axis_index("ctx") * per_device + jnp.arange(per_device, dtype=jnp.int32)
    live_rows = (positions[None, :] < lengths[:, None]).astype(jnp.float32)
    grad_out = (cotangent.astype(jnp.float32) * live_rows[:, :, None]).reshape(
        groups * per_device, width
    )
    grad_rows, matrix_grad, vector_grad = backward(grad_out, saved, matrix_set, vector_set)
    grad_tokens = grad_rows.astype(jnp.bfloat16).reshape(tokens.shape)
    ctx_count = lax.axis_size("ctx")
    dp_count = lax.axis_size("dp")
    ordered_w = (
        matrix_grad.reshape(ctx_count, dp_count, -1, width).swapaxes(0, 1).reshape(-1, width)
    )
    ordered_v = vector_grad.reshape(ctx_count, dp_count, -1).swapaxes(0, 1).reshape(-1)
    piece_w, piece_v = (
        lax.psum_scatter(ordered_w, ("dp", "ctx"), scatter_dimension=0, tiled=True),
        lax.psum_scatter(ordered_v, ("dp", "ctx"), scatter_dimension=0, tiled=True),
    )
    shard_w, shard_v = (
        lax.all_gather(piece_w.astype(jnp.bfloat16), "dp", axis=0, tiled=True).astype(
            piece_w.dtype
        ),
        lax.all_gather(piece_v.astype(jnp.bfloat16), "dp", axis=0, tiled=True).astype(
            piece_v.dtype
        ),
    )
    weight_change, new_first_weights, new_second_weights = adamw_update(
        weights, shard_w, first_weights, second_weights, 0.01
    )
    vector_change, new_first_vectors, new_second_vectors = adamw_update(
        vectors, shard_v, first_vectors, second_vectors, 0.0
    )
    return (
        layer_out,
        grad_tokens,
        shard_w,
        shard_v,
        weight_change,
        vector_change,
        new_first_weights,
        new_second_weights,
        new_first_vectors,
        new_second_vectors,
    )


def solution(mesh):
    placed = (
        P("dp", "ctx", None),
        P("dp", "ctx", None),
        P("dp"),
        P("ctx", None),
        P("ctx"),
        P("ctx", None),
        P("ctx", None),
        P("ctx"),
        P("ctx"),
    )
    return jax.shard_map(
        shards,
        mesh=mesh,
        in_specs=placed,
        out_specs=(
            P("dp", "ctx", None),
            P("dp", "ctx", None),
            P("ctx", None),
            P("ctx"),
            P("ctx", None),
            P("ctx"),
            P("ctx", None),
            P("ctx", None),
            P("ctx"),
            P("ctx"),
        ),
        check_vma=False,
    )
```

profile of v0, /device:TPU:0, one launch (start us, length us, event | category | flops | bytes accessed | tf_op | source)
XLA Modules:
  0.0 1602.9 jit_solution(777068153721569664)
XLA Ops:
  12.3 222.7 %all-gather.9.cloned.1.call-done = bf16[12288,1024]{1,0:T(8,128)(2,1)} async-done(((bf16[1536,1024]{1,0:T(8,128)(2,1)}), bf16[12288,1024]{1,0:T(8,128)(2,1)}) %all-gather.9.cloned.1.call-update) | async-done | bytes 25165840 | tf_op jit(solution)/shard_map/all_gather | solution.py:271
  244.6 14.0 all-gather
  264.3 60.6 %all-gather.13.cloned.1.call-done = bf16[4,1024,1024]{2,1,0:T(8,128)(2,1)} async-done(((bf16[4,128,1024]{2,1,0:T(8,128)(2,1)}), bf16[4,1024,1024]{2,1,0:T(8,128)(2,1)}) %all-gather.13.cloned.1.call-update) | async-done | bytes 8388624 | tf_op jit(solution)/shard_map/all_gather | solution.py:101
  324.9 11.6 copy.72
  336.5 19.3 %fusion.169 = (f32[4,16,128]{2,1,0:T(8,128)S(1)}, f32[4,16,128,1024]{3,2,1,0:T(8,128)}) fusion(pred[4,1024]{1,0:T(4,128)(4,1)S(1)} %iota_compare_fusion, bf16[4,1024,16,64]{1,3,2,0:T(8,128)(2,1)} %bitcast.98, bf16[4,128,16,64]{3,2,1,0:T(8,128)(2,1)S(1)} %reshape.278), kind=kOutput, calls=%fused_computation.234 | convolution fusion | flops 1107297280 | bytes 43028480 | tf_op jit(solution)/shard_map/sub | solution.py:111
  355.7 52.0 %all-gather.11.cloned.1.call-done = bf16[4,1024,1024]{2,1,0:T(8,128)(2,1)} async-done(((bf16[4,128,1024]{2,1,0:T(8,128)(2,1)}), bf16[4,1024,1024]{2,1,0:T(8,128)(2,1)}) %all-gather.11.cloned.1.call-update) | async-done | bytes 8388624 | tf_op jit(solution)/shard_map/all_gather | solution.py:102
  407.8 11.4 copy.70
  419.1 15.7 fusion.101
  439.2 25.0 %fusion.15.clone.3.clone.5 = bf16[512,4096]{1,0:T(8,128)(2,1)S(1)} fusion(bf16[12288,1024]{1,0:T(8,128)(2,1)} %all-gather.9.cloned.1.call-done, f32[4096]{0:T(1024)S(1)} %slice.137, f32[512,1024]{1,0:T(8,128)S(1)} %get-tuple-element.60, f32[1024]{0:T(1024)S(1)} %get-tuple-element.52, ...), kind=kOutput, calls=%fused_computation.28.clone.clone.clone.clone.clone.clone.clone.2 | convolution fusion | flops 4436000768 | bytes 14708736 | tf_op jit(solution)/shard_map/dot_general | solution.py:20
  494.7 68.9 %all-gather.17.cloned.1.call-done = bf16[4,1024,1024]{2,1,0:T(8,128)(2,1)} async-done(((bf16[4,128,1024]{2,1,0:T(8,128)(2,1)}), bf16[4,1024,1024]{2,1,0:T(8,128)(2,1)}) %all-gather.17.cloned.1.call-update) | async-done | bytes 8388624 | tf_op jit(solution)/shard_map/all_gather | solution.py:101
  563.6 11.6 copy.77
  575.2 15.7 fusion.12
  590.9 14.7 fusion.1
  606.2 40.0 %all-gather.15.cloned.1.call-done = bf16[4,1024,1024]{2,1,0:T(8,128)(2,1)} async-done(((bf16[4,128,1024]{2,1,0:T(8,128)(2,1)}), bf16[4,1024,1024]{2,1,0:T(8,128)(2,1)}) %all-gather.15.cloned.1.call-update) | async-done | bytes 8388624 | tf_op jit(solution)/shard_map/all_gather | solution.py:102
  646.3 11.4 copy.75
  657.7 15.8 fusion.102
  678.8 26.4 %multiply_convert_fusion.2 = (bf16[512,4096]{1,0:T(8,128)(2,1)S(1)}, f32[512,4096]{1,0:T(8,128)}, f32[512,4096]{1,0:T(8,128)}) fusion(f32[4096]{0:T(1024)S(1)} %slice.150, bf16[12288,1024]{1,0:T(8,128)(2,1)} %all-gather.9.cloned.1.call-done, f32[512,1024]{1,0:T(8,128)S(1)} %get-tuple-element.66, f32[1024]{0:T(1024)S(1)} %get-tuple-element.45, ...), kind=kOutput, calls=%fused_computation.36 | convolution fusion | flops 4436000768 | bytes 31485952 | tf_op jit(solution)/shard_map/dot_general | solution.py:20
  716.8 14.8 convert_reduce_fusion
  750.7 25.9 %multiply_reduce_fusion = (f32[4,16,128]{2,1,0:T(8,128)S(1)}, f32[4,16,128,1024]{3,2,1,0:T(8,128)}) fusion(f32[4,16,128]{2,1,0:T(8,128)S(1)} %copy-done.17, f32[4,16,128,1024]{3,2,1,0:T(8,128)} %get-tuple-element.64, pred[4,1024]{1,0:T(4,128)(4,1)S(1)} %iota_compare_fusion, bf16[4,128,16,64]{1,3,2,0:T(8,128)(2,1)S(1)} %copy.81, ...), kind=kOutput, calls=%fused_computation.3 | convolution fusion | flops 1115676672 | bytes 76615680 | tf_op jit(solution)/shard_map/bqhd,bkhd->bhqk/dot_general | solution.py:193
  776.7 28.1 %multiply_convert_fusion = bf16[4,16,128,1024]{3,2,1,0:T(8,128)(2,1)} fusion(f32[4,16,128,1024]{3,2,1,0:T(8,128)} %get-tuple-element.72, f32[4,16,128]{2,1,0:T(8,128)S(1)} %get-tuple-element.71, f32[4,16,128]{2,1,0:T(8,128)S(1)} %copy-done.17, f32[4,16,128,1024]{3,2,1,0:T(8,128)} %get-tuple-element.64, pred[4,1024]{1,0:T(4,128)(4,1)S(1)} %iota_compare_fusion), kind=kLoop, calls=%fused_computation.2 | loop fusion | flops 50331648 | bytes 83955712 | tf_op jit(solution)/shard_map/convert_element_type | solution.py:197
  804.8 11.4 multiply_convert_fusion.1
  816.2 11.4 copy.84
  828.9 17.3 %fusion.41 = bf16[4,16,64,1024]{3,2,1,0:T(8,128)(2,1)} fusion(bf16[4,128,16,64]{1,3,2,0:T(8,128)(2,1)S(1)} %copy-done.8, f32[4,16,128]{2,1,0:T(8,128)S(1)} %copy-done.17, f32[4,16,128,1024]{3,2,1,0:T(8,128)} %get-tuple-element.64, pred[4,1024]{1,0:T(4,128)(4,1)S(1)} %iota_compare_fusion), kind=kOutput, calls=%fused_computation.73 | convolution fusion | flops 1111490560 | bytes 43028480 | tf_op jit(solution)/shard_map/bhqk,bqhd->bkhd/dot_general | solution.py:203
  846.2 11.4 copy.86
  857.7 12.0 convert_reduce_fusion.4
  892.0 23.9 %reduce-scatter.4.cloned.1.call-done = bf16[4,128,1024]{2,1,0:T(8,128)(2,1)} async-done(((bf16[4,1024,1024]{2,1,0:T(8,128)(2,1)}), bf16[4,128,1024]{2,1,0:T(8,128)(2,1)}) %reduce-scatter.4.cloned.1.call-update) | async-done | bytes 1048592 | tf_op jit(solution)/shard_map/reduce_scatter | solution.py:211
  918.2 88.0 %reduce-scatter.6.cloned.1.call-done = bf16[4,128,1024]{2,1,0:T(8,128)(2,1)} async-done(((bf16[4,1024,1024]{2,1,0:T(8,128)(2,1)}), bf16[4,128,1024]{2,1,0:T(8,128)(2,1)}) %reduce-scatter.6.cloned.1.call-update) | async-done | bytes 1048592 | tf_op jit(solution)/shard_map/reduce_scatter | solution.py:217
  1018.5 35.9 %pad_maximum_fusion = f32[12288,1024]{1,0:T(8,128)} fusion(f32[4096,1024]{1,0:T(8,128)} %fusion.125, f32[4096,1024]{1,0:T(8,128)} %fusion.180, f32[1024,1024]{1,0:T(8,128)} %fusion.104, f32[3072,1024]{1,0:T(8,128)} %fusion.103), kind=kLoop, calls=%fused_computation.1 | loop fusion | flops 37748736 | bytes 100663296 | tf_op jit(solution)/shard_map/concatenate | solution.py:232
  1054.4 35.0 %copy.89 = f32[4,8,384,1024]{3,2,1,0:T(8,128)} copy(f32[4,8,384,1024]{3,2,0,1:T(8,128)} %bitcast.92) | data formatting | bytes 100663296 | tf_op jit(solution)/shard_map/transpose | solution.py:292
  1089.6 430.3 %reduce-scatter.8.cloned.1.call-done = f32[384,1024]{1,0:T(8,128)} async-done(((f32[12288,1024]{1,0:T(8,128)}), f32[384,1024]{1,0:T(8,128)}) %reduce-scatter.8.cloned.1.call-update) | async-done | bytes 1572880 | tf_op jit(solution)/shard_map/reduce_scatter | solution.py:296
  1522.8 39.9 %all-reduce = bf16[12288]{0:T(1024)(128)(2,1)S(1)} all-reduce(f32[12288]{0:T(1024)S(1)} %reshape.272), channel_id=5, replica_groups=mesh['dp'=4,'ctx'=8] {'dp','ctx'}, use_global_device_ids=true, to_apply=%region_29.30.clone | all-reduce | flops 12288 | bytes 73728
  1580.4 15.6 add_multiply_fusion
  (185 shorter events, 150.3 us)
Async XLA Ops:
  7.2 227.8 %copy-start.35 = (bf16[4,128,1024]{2,1,0:T(8,128)(2,1)S(1)}, bf16[4,128,1024]{2,1,0:T(8,128)(2,1)}, u32[]{:S(2)}) copy-start(bf16[4,128,1024]{2,1,0:T(8,128)(2,1)} %param.9) | copy-start | bytes 3145732
  7.2 227.8 %all-gather.9.cloned.1.call-start = ((), (), s32[]{:S(2)}) async-start(), calls=%async_computation.3 | async-start | bytes 28311552 | tf_op jit(solution)/shard_map/all_gather | solution.py:271
  12.3 312.6 %all-gather.13.cloned.1.call-start = ((), (), s32[]{:S(2)}) async-start(), calls=%async_computation.5 | async-start | bytes 9437184 | tf_op jit(solution)/shard_map/all_gather | solution.py:101
  243.3 19.6 %copy-start.33 = (s32[4]{0:T(128)S(1)}, s32[4]{0:T(128)}, u32[]{:S(2)}) copy-start(s32[4]{0:T(128)} %param.11) | copy-start | bytes 52
  244.5 163.3 %all-gather.11.cloned.1.call-start = ((), (), s32[]{:S(2)}) async-start(), calls=%async_computation.4 | async-start | bytes 9437184 | tf_op jit(solution)/shard_map/all_gather | solution.py:102
  262.7 300.9 %all-gather.17.cloned.1.call-start = ((), (), s32[]{:S(2)}) async-start(), calls=%async_computation.7 | async-start | bytes 9437184 | tf_op jit(solution)/shard_map/all_gather | solution.py:101
  419.1 16.6 %copy-start.36 = (bf16[4,128,1024]{2,1,0:T(8,128)(2,1)S(1)}, bf16[4,128,1024]{2,1,0:T(8,128)(2,1)}, u32[]{:S(2)}) copy-start(bf16[4,128,1024]{2,1,0:T(8,128)(2,1)} %param.9) | copy-start | bytes 3145732
  482.8 163.4 %all-gather.15.cloned.1.call-start = ((), (), s32[]{:S(2)}) async-start(), calls=%async_computation.6 | async-start | bytes 9437184 | tf_op jit(solution)/shard_map/all_gather | solution.py:102
  482.9 11.2 copy-start.18
  486.8 429.2 %reduce-scatter.4.cloned.1.call-start = ((), (), s32[]{:S(2)}) async-start(), calls=%async_computation.8 | async-start | bytes 9437184 | tf_op jit(solution)/shard_map/reduce_scatter | solution.py:211
  490.0 85.2 %copy-start.1 = (bf16[4,128,16,64]{1,3,2,0:T(8,128)(2,1)}, bf16[4,128,16,64]{1,3,2,0:T(8,128)(2,1)S(1)}, u32[]{:S(2)}) copy-start(bf16[4,128,16,64]{1,3,2,0:T(8,128)(2,1)S(1)} %copy.78) | copy-start | bytes 3145732
  657.7 17.7 %copy-start.37 = (bf16[4,128,1024]{2,1,0:T(8,128)(2,1)S(1)}, bf16[4,128,1024]{2,1,0:T(8,128)(2,1)}, u32[]{:S(2)}) copy-start(bf16[4,128,1024]{2,1,0:T(8,128)(2,1)} %param.9) | copy-start | bytes 3145732
  678.4 63.0 %copy-start.3 = (f32[512,1024]{1,0:T(8,128)}, f32[512,1024]{1,0:T(8,128)S(1)}, u32[]{:S(2)}) copy-start(f32[512,1024]{1,0:T(8,128)S(1)} %get-tuple-element.66) | copy-start | bytes 6291460
  716.8 14.8 copy-start.12
  750.7 26.0 %copy-start.7 = (bf16[4,128,16,64]{1,3,2,0:T(8,128)(2,1)}, bf16[4,128,16,64]{1,3,2,0:T(8,128)(2,1)S(1)}, u32[]{:S(2)}) copy-start(bf16[4,128,16,64]{1,3,2,0:T(8,128)(2,1)S(1)} %copy.81) | copy-start | bytes 3145732
  776.7 28.2 %copy-start.2 = (bf16[4,128,16,64]{1,3,2,0:T(8,128)(2,1)S(1)}, bf16[4,128,16,64]{1,3,2,0:T(8,128)(2,1)}, u32[]{:S(2)}) copy-start(bf16[4,128,16,64]{1,3,2,0:T(8,128)(2,1)} %copy-done.1) | copy-start | bytes 3145732
  827.7 178.6 %reduce-scatter.6.cloned.1.call-start = ((), (), s32[]{:S(2)}) async-start(), calls=%async_computation.9 | async-start | bytes 9437184 | tf_op jit(solution)/shard_map/reduce_scatter | solution.py:217
  857.6 14.2 copy-start.10
  857.6 662.2 %reduce-scatter.8.cloned.1.call-start = ((), (), s32[]{:S(2)}) async-start(), calls=%async_computation.10 | async-start | bytes 51904512 | tf_op jit(solution)/shard_map/reduce_scatter | solution.py:296
  883.5 125.3 %copy-start.14 = (bf16[128,8,4,128]{3,1,2,0:T(8,128)(2,1)S(1)}, bf16[128,8,4,128]{3,1,2,0:T(8,128)(2,1)}, u32[]{:S(2)}) copy-start(bf16[128,8,4,128]{3,1,2,0:T(8,128)(2,1)} %copy.129) | copy-start | bytes 3145732
  1089.4 432.9 %copy-start.11 = (bf16[4,128,1024]{2,1,0:T(8,128)(2,1)S(1)}, bf16[4,128,1024]{2,1,0:T(8,128)(2,1)}, u32[]{:S(2)}) copy-start(bf16[4,128,1024]{2,1,0:T(8,128)(2,1)} %reduce-scatter.6.cloned.1.call-done) | copy-start | bytes 3145732
  1089.4 433.1 %copy-start.26 = (f32[1024]{0:T(1024)S(1)}, f32[1024]{0:T(1024)}, u32[]{:S(2)}) copy-start(f32[1024]{0:T(1024)} %get-tuple-element.33) | copy-start | bytes 12292
  1089.4 433.2 %copy-start.27 = (f32[4096]{0:T(1024)S(1)}, f32[4096]{0:T(1024)}, u32[]{:S(2)}) copy-start(f32[4096]{0:T(1024)} %get-tuple-element.75) | copy-start | bytes 49156
  1089.4 433.2 %copy-start.25 = (f32[1024]{0:T(1024)S(1)}, f32[1024]{0:T(1024)}, u32[]{:S(2)}) copy-start(f32[1024]{0:T(1024)} %get-tuple-element.31) | copy-start | bytes 12292
  1089.4 433.2 %copy-start.32 = (f32[1024]{0:T(1024)S(1)}, f32[1024]{0:T(1024)}, u32[]{:S(2)}) copy-start(f32[1024]{0:T(1024)} %get-tuple-element.18) | copy-start | bytes 12292
  1089.4 433.2 %copy-start.31 = (f32[1024]{0:T(1024)S(1)}, f32[1024]{0:T(1024)}, u32[]{:S(2)}) copy-start(f32[1024]{0:T(1024)} %get-tuple-element.21) | copy-start | bytes 12292
  1089.4 433.2 %copy-start.24 = (f32[1024]{0:T(1024)S(1)}, f32[1024]{0:T(1024)}, u32[]{:S(2)}) copy-start(f32[1024]{0:T(1024)} %get-tuple-element.16) | copy-start | bytes 12292
  1089.5 433.2 %copy-start.23 = (f32[1024]{0:T(1024)S(1)}, f32[1024]{0:T(1024)}, u32[]{:S(2)}) copy-start(f32[1024]{0:T(1024)} %get-tuple-element.22) | copy-start | bytes 12292
  1089.5 482.2 %copy-start.22 = (f32[1536]{0:T(1024)S(1)}, f32[1536]{0:T(1024)}, u32[]{:S(2)}) copy-start(f32[1536]{0:T(1024)} %param.13) | copy-start | bytes 18436
  1089.5 482.2 %copy-start.29 = (f32[1536]{0:T(1024)S(1)}, f32[1536]{0:T(1024)}, u32[]{:S(2)}) copy-start(f32[1536]{0:T(1024)} %param.16) | copy-start | bytes 18436
  1089.5 482.2 %copy-start.30 = (f32[1536]{0:T(1024)S(1)}, f32[1536]{0:T(1024)}, u32[]{:S(2)}) copy-start(f32[1536]{0:T(1024)} %param.17) | copy-start | bytes 18436
  1089.5 490.9 %all-gather.19.cloned.1.call-start = ((), (), s32[]{:S(2)}) async-start(), calls=%async_computation.11 | async-start | bytes 3932160 | tf_op jit(solution)/shard_map/all_gather | solution.py:300
  (19 other events, 127.6 us)
Sparse Core Ops, SparseCore 0:
  12.4 222.5 all-gather.8
  244.6 80.2 all-gather.12
  327.1 80.5 all-gather.10
  483.0 80.5 all-gather.16
  565.6 80.5 all-gather.14
  827.8 88.1 reduce-scatter.3
  918.3 87.9 reduce-scatter.5
  1089.7 430.1 reduce-scatter.7
  1522.4 43.8 all-gather.18
where the time goes:
time: 1610 us; the launch traced here: 1600 us
  waiting for transfers between devices  987 us (61%)
  matrix products  284 us (18%)
  local copies, waits for them, and re-layouts  132 us (8%)
  other arithmetic  122 us (8%)
  blocking collectives  62.8 us (4%)
    reduce_scatter x1, waiting for transfers between devices, shards(): lax.psum_scatter(ordered_w, ('dp', 'ctx'), scatter_dimension=0, tiled=True)  430 us
    all_gather x1, waiting for transfers between devices, shards(): lax.all_gather(weights.astype(jnp.bfloat16), 'ctx', axis=0, tiled=True)  223 us
    all_gather x2, waiting for transfers between devices, forward(): lax.all_gather(keys_local, 'ctx', axis=1, tiled=True)  129 us
    all_gather x2, waiting for transfers between devices, forward(): lax.all_gather(values_local, 'ctx', axis=1, tiled=True)  92 us
    reduce_scatter x1, waiting for transfers between devices, backward(): lax.psum_scatter(grad_values.reshape(groups, span, D).astype(jnp.bfloat16...  88 us
    dot_general x7, matrix products, times_rows(): lax.dot_general(operand, matrix, (((1,), (1,)), ((), ())), preferred_elem...  83.4 us
    unnamed x1, blocking collectives  39.9 us
    concatenate x1, other arithmetic, backward(): jnp.concatenate([grad_qkv, grad_out_proj, grad_up, grad_down], axis=0)  35.9 us
  transfers between devices with their start and end apart: 9, of which 8 were waited for; matrix products, arithmetic and copies ran while one was open for 10% of the time, Pallas kernels for 0%

commit v1 on v0

v1 whole, which is shorter than its diff:
```python
import math

import jax
import jax.numpy as jnp
from jax import lax
from jax.sharding import Mesh
from jax.sharding import PartitionSpec as P

D = 1024
FF = 4096
H = 16
HD = 64
STEP = 10
EPSILON = 1e-05
LEARN_RATE = 0.003
BF = jnp.bfloat16
F32 = jnp.float32
HALF = D // 2
BLOCK = 512


def rows_dot(operand, matrix):
    return lax.dot_general(operand, matrix, (((1,), (1,)), ((), ())), preferred_element_type=F32)


def cols_dot(operand, matrix):
    return lax.dot_general(operand, matrix, (((0,), (0,)), ((), ())), preferred_element_type=F32)


def plain_dot(operand, matrix):
    return lax.dot_general(operand, matrix, (((1,), (0,)), ((), ())), preferred_element_type=F32)


def swap(value):
    return lax.ppermute(value, "core", [(0, 1), (1, 0)])


def exchange(axis, bit, value):
    count = lax.axis_size(axis)
    return lax.ppermute(value, axis, [(i, i ^ bit) for i in range(count)])


def sum_all(value):
    for axis in ("core", "z", "dp"):
        bit = 1
        while bit < lax.axis_size(axis):
            value = value + exchange(axis, bit, value)
            bit *= 2
    return value


def layer_norm(inputs, gain_vec, shift_vec):
    centre = jnp.mean(inputs, axis=-1, keepdims=True)
    shifted = inputs - centre
    inverse = lax.rsqrt(jnp.mean(shifted * shifted, axis=-1, keepdims=True) + EPSILON)
    normed = shifted * inverse
    return (normed * gain_vec + shift_vec, normed, inverse)


def norm_back(grad_out, normed, inverse, gain_vec):
    scaled = grad_out * gain_vec
    inner_term = (
        scaled
        - jnp.mean(scaled, axis=-1, keepdims=True)
        - normed * jnp.mean(scaled * normed, axis=-1, keepdims=True)
    )
    return (inverse * inner_term, jnp.sum(grad_out * normed, axis=0), jnp.sum(grad_out, axis=0))


def to_chips(blocks, z):
    count = lax.axis_size("z")
    parts = []
    for shift in range(count):
        part = lax.dynamic_index_in_dim(blocks, (z + shift) % count, 0, keepdims=False)
        if shift:
            part = lax.ppermute(part, "z", [(i, (i + shift) % count) for i in range(count)])
        parts.append(part)
    return jnp.concatenate(parts, axis=0)


def from_chips(rows, z):
    count = lax.axis_size("z")
    blocks = rows.reshape(count, -1, rows.shape[-1])
    result = jnp.zeros_like(blocks)
    for shift in range(count):
        part = blocks[shift]
        if shift:
            part = lax.ppermute(part, "z", [(i, (i - shift) % count) for i in range(count)])
        result = lax.dynamic_update_index_in_dim(result, part, (z + shift) % count, 0)
    return result


def quadrants(matrix):
    half = matrix.shape[0] // 2
    return jnp.concatenate(
        [
            jnp.concatenate([matrix[:half, :half], matrix[half:, :half]], axis=1),
            jnp.concatenate([matrix[:half, half:], matrix[half:, half:]], axis=1),
        ],
        axis=0,
    )


def is_out_projection(z, core):
    return jnp.logical_and(z == 1, core == 0)


def pack_weights(weights, z, core):
    low = weights.astype(BF)
    top = jnp.where(is_out_projection(z, core), quadrants(low[:D]), low[:D])
    first, middle, last = top[:BLOCK], top[BLOCK:], low[D:]
    other = swap(middle)
    return jnp.where(
        core == 0,
        jnp.concatenate([first, last, other], axis=0),
        jnp.concatenate([other, first, last], axis=0),
    )


def unpack_grads(packed, z, core):
    a, b, c = packed[:BLOCK], packed[BLOCK : 2 * BLOCK], packed[2 * BLOCK :]
    middle = swap(jnp.where(core == 0, c, a))
    first, last = jnp.where(core == 0, a, b), jnp.where(core == 0, b, c)
    top = jnp.concatenate([first, middle], axis=0)
    top = jnp.where(is_out_projection(z, core), quadrants(top), top)
    return jnp.concatenate([top, last], axis=0).astype(F32)


def gather_weights(packed):
    count = lax.axis_size("dp")
    rows = packed.shape[0] // count
    piece = lax.dynamic_slice_in_dim(packed, lax.axis_index("dp") * rows, rows, 0)
    return lax.all_gather(piece, ("z", "dp"), axis=0, tiled=True)


def reduce_grads(blocks):
    whole = jnp.concatenate(blocks, axis=0)
    piece = lax.psum_scatter(whole, ("z", "dp"), scatter_dimension=0, tiled=True)
    return lax.all_gather(piece, "dp", axis=0, tiled=True)


def attention_scores(queries, keys, allowed):
    scores = jnp.einsum("qhd,khd->hqk", queries, keys, preferred_element_type=F32) / math.sqrt(HD)
    return jnp.where(allowed[None, None, :], scores, -1e30)


def attention_forward(queries, keys, values, allowed):
    rows, width = queries.shape
    heads = width // HD
    scores = attention_scores(queries.reshape(rows, heads, HD), keys.reshape(rows, heads, HD), allowed)
    highest = jnp.max(scores, axis=-1, keepdims=True)
    terms = jnp.exp(scores - highest)
    total = jnp.sum(terms, axis=-1, keepdims=True)
    probs = (terms / total).astype(BF)
    out = jnp.einsum(
        "hqk,khd->qhd", probs, values.reshape(rows, heads, HD), preferred_element_type=F32
    )
    return out.astype(BF).reshape(rows, width), highest + jnp.log(total)


def attention_backward(queries, keys, values, allowed, log_total, grad_out):
    rows, width = queries.shape
    heads = width // HD
    shape = (rows, heads, HD)
    queries, keys, values, grad_out = (
        item.reshape(shape) for item in (queries, keys, values, grad_out)
    )
    factor = 1.0 / math.sqrt(HD)
    probs = jnp.exp(attention_scores(queries, keys, allowed) - log_total)
    grad_probs = jnp.einsum("qhd,khd->hqk", grad_out, values, preferred_element_type=F32)
    row_sums = jnp.sum(grad_probs * probs, axis=-1, keepdims=True)
    grad_scores = (probs * (grad_probs - row_sums)).astype(BF)
    dq = jnp.einsum("hqk,khd->qhd", grad_scores, keys, preferred_element_type=F32) * factor
    dk = jnp.einsum("hqk,qhd->khd", grad_scores, queries, preferred_element_type=F32) * factor
    dv = jnp.einsum("hqk,qhd->khd", probs.astype(BF), grad_out, preferred_element_type=F32)
    return jnp.concatenate([item.astype(BF).reshape(rows, width) for item in (dq, dk, dv)], axis=1)


def adamw_update(parameter, gradient, first_old, second_old, decay_rate):
    step_float = float(STEP)
    first_new = 0.9 * first_old + 0.1 * gradient
    second_new = 0.999 * second_old + 0.001 * gradient * gradient
    first_fix = first_new / (1.0 - 0.9**step_float)
    second_fix = second_new / (1.0 - 0.999**step_float)
    update = first_fix / (jnp.sqrt(second_fix) + 1e-08)
    return (-LEARN_RATE * (update + decay_rate * parameter), first_new, second_new)


def share(partial):
    return partial[:HALF] + swap(partial[HALF:].astype(BF)).astype(F32)


def both(rows):
    return jnp.concatenate([rows, swap(rows)], axis=0)


def core_part(vector, core, pieces):
    return vector.reshape(pieces, 2, -1)[:, core].reshape(-1)


def spread_part(vector, core, pieces):
    parts = vector.reshape(pieces, 1, -1)
    mine = (jnp.arange(2) == core)[None, :, None]
    return jnp.where(mine, parts, 0.0).reshape(-1)


def shards(
    tokens,
    cotangent,
    lengths,
    weights,
    vectors,
    first_weights,
    second_weights,
    first_vectors,
    second_vectors,
):
    z, core = lax.axis_index("z"), lax.axis_index("core")
    count = lax.axis_size("z")
    per_device = tokens.shape[1]
    rows = count * per_device
    length = lengths[z]
    block = jnp.arange(count, dtype=jnp.int32)[:, None]
    inner = jnp.arange(per_device, dtype=jnp.int32)[None, :]
    chip_of = (z - block) % count
    here = ((chip_of * 2 + core) * per_device + inner).reshape(rows)
    there = ((chip_of * 2 + 1 - core) * per_device + inner).reshape(rows)
    allowed = jnp.concatenate([here, there]) < length
    live = (here < length).astype(F32)[:, None]

    vec = lax.all_gather(vectors.astype(BF), ("z", "core"), axis=0, tiled=True).astype(F32)
    bounds = [0, D, 2 * D, 3 * D, 3 * D + FF] + [(n + 4) * D + FF for n in range(6)]
    bias_q, bias_v, bias_o, bias_up, bias_down, gain_one, shift_one, gain_two, shift_two = (
        vec[bounds[n] : bounds[n + 1]] for n in range(9)
    )
    bias_q, bias_v = core_part(bias_q, core, 1), core_part(bias_v, core, 1)
    bias_up = core_part(bias_up, core, FF // (2 * BLOCK))

    whole = gather_weights(pack_weights(weights, z, core))
    w_qkv = whole[: 3 * HALF]
    w_out = whole[3 * HALF : 4 * HALF]
    w_up = whole[4 * HALF : 4 * HALF + FF // 2]
    w_down = whole[4 * HALF + FF // 2 :]

    x_mine = to_chips(tokens, z)
    x = both(x_mine)
    merged = rows_dot(x, w_qkv)
    queries = (merged[:, :HALF] + bias_q).astype(BF)
    keys = merged[:, HALF : 2 * HALF].astype(BF)
    values = (merged[:, 2 * HALF :] + bias_v).astype(BF)
    heads_out, log_total = attention_forward(queries, keys, values, allowed)

    branch = jnp.concatenate(
        [rows_dot(heads_out, w_out[:, :HALF]), rows_dot(heads_out, w_out[:, HALF:])], axis=1
    )
    normed_in, normed_one, inverse_one = layer_norm(
        x_mine.astype(F32) + share(branch) + bias_o, gain_one, shift_one
    )
    u_mine = normed_in.astype(BF)
    u = both(u_mine)
    gate_in = rows_dot(u, w_up) + bias_up
    cdf = 0.5 * (1.0 + lax.erf(gate_in * (1.0 / math.sqrt(2.0))))
    slope = cdf + gate_in * jnp.exp(-0.5 * gate_in * gate_in) * (1.0 / math.sqrt(2.0 * math.pi))
    hidden = (gate_in * cdf).astype(BF)
    feed = share(plain_dot(hidden, w_down)) + bias_down
    result, normed_two, inverse_two = layer_norm(u_mine.astype(F32) + feed, gain_two, shift_two)
    layer_out = from_chips(result.astype(BF), z)

    grad_out = to_chips(cotangent, z).astype(F32) * live
    grad_two, grad_gain_two, grad_shift_two = norm_back(grad_out, normed_two, inverse_two, gain_two)
    df_mine = grad_two.astype(BF)
    df = both(df_mine)
    grad_bias_down = jnp.sum(df_mine.astype(F32), axis=0)
    dz = (rows_dot(df, w_down) * slope).astype(BF)
    grad_down = cols_dot(hidden, df).astype(BF)
    grad_up = cols_dot(dz, u).astype(BF)
    grad_bias_up = jnp.sum(dz.astype(F32), axis=0)
    du = share(plain_dot(dz, w_up)) + grad_two
    grad_one, grad_gain_one, grad_shift_one = norm_back(du, normed_one, inverse_one, gain_one)
    da_mine = grad_one.astype(BF)
    da = both(da_mine)
    grad_bias_o = jnp.sum(da_mine.astype(F32), axis=0)
    do = (plain_dot(da[:, :HALF], w_out[:, :HALF]) + plain_dot(da[:, HALF:], w_out[:, HALF:])).astype(BF)
    grad_wo = jnp.concatenate(
        [cols_dot(da[:, :HALF], heads_out), cols_dot(da[:, HALF:], heads_out)], axis=1
    ).astype(BF)
    d_merged = attention_backward(queries, keys, values, allowed, log_total, do)
    grad_qkv = cols_dot(d_merged, x).astype(BF)
    column_sums = jnp.sum(d_merged.astype(F32), axis=0)
    grad_rows = share(plain_dot(d_merged, w_qkv)) + grad_one
    grad_tokens = from_chips(grad_rows.astype(BF), z)

    vector_grad = jnp.concatenate(
        [
            spread_part(column_sums[:HALF], core, 1),
            spread_part(column_sums[2 * HALF :], core, 1),
            grad_bias_o,
            spread_part(grad_bias_up, core, FF // (2 * BLOCK)),
            grad_bias_down,
            grad_gain_one,
            grad_shift_one,
            grad_gain_two,
            grad_shift_two,
        ]
    )
    vector_sum = sum_all(vector_grad)
    shard_v = lax.dynamic_slice_in_dim(
        vector_sum, (z * 2 + core) * vectors.shape[0], vectors.shape[0], 0
    )
    shard_w = unpack_grads(reduce_grads([grad_qkv, grad_wo, grad_up, grad_down]), z, core)

    weight_change, new_first_weights, new_second_weights = adamw_update(
        weights, shard_w, first_weights, second_weights, 0.01
    )
    vector_change, new_first_vectors, new_second_vectors = adamw_update(
        vectors, shard_v, first_vectors, second_vectors, 0.0
    )
    return (
        layer_out,
        grad_tokens,
        shard_w,
        shard_v,
        weight_change,
        vector_change,
        new_first_weights,
        new_second_weights,
        new_first_vectors,
        new_second_vectors,
    )


def solution(mesh):
    chips = Mesh(
        mesh.devices.reshape(mesh.shape["dp"], mesh.shape["ctx"] // 2, 2), ("dp", "z", "core")
    )
    ctx = ("z", "core")
    activations, matrix, vector = P("dp", ctx, None), P(ctx, None), P(ctx)
    return jax.shard_map(
        shards,
        mesh=chips,
        in_specs=(activations, activations, P("dp"), matrix, vector, matrix, matrix, vector, vector),
        out_specs=(
            activations,
            activations,
            matrix,
            vector,
            matrix,
            vector,
            matrix,
            matrix,
            vector,
            vector,
        ),
        check_vma=False,
    )
```

time: 1610 us -> 812 us (0.50)
  waiting for transfers between devices: 987 us -> 363 us
  matrix products: 284 us -> 159 us
  local copies, waits for them, and re-layouts: 132 us -> 45.9 us
  starting transfers between devices: 0.55 us -> 34.7 us
  blocking collectives: 62.8 us -> 44.9 us
  other arithmetic: 122 us -> 139 us
    reduce_scatter x3 -> x1, waiting for transfers between devices: 542 us -> 206 us  [reduce_grads(): lax.psum_scatter(whole, ('z', 'dp'), scatter_dimension=0, tiled=True)]
    all_gather x6 -> x2, waiting for transfers between devices: 444 us -> 110 us  [the longest x1 110 us: gather_weights(): return lax.all_gather(piece, ('z', 'dp'), axis=0, tiled=True)]
    dot_general x23 -> x21, matrix products: 264 us -> 159 us  [the longest x5 28.2 us: rows_dot(): lax.dot_general(operand, matrix, (((1,), (1,)), ((), ())), preferred_elem...]
    ppermute x0 -> x27, waiting for transfers between devices: none -> 46.7 us  [the longest x6 17 us: from_chips(): lax.ppermute(part, 'z', [(i, (i - shift) % count) for i in range(count)])]
    all_gather x4 -> x0, local copies, waits for them, and re-layouts: 45.9 us -> none  [the longest x2 23.2 us: forward(): lax.all_gather(keys_local, 'ctx', axis=1, tiled=True)]
    unnamed x1 -> x0, blocking collectives: 39.9 us -> none
    transpose x2 -> x0, local copies, waits for them, and re-layouts: 35 us -> none  [the longest x1 35 us: shards(): matrix_grad.reshape(ctx_count, dp_count, -1, width).swapaxes(0, 1)]
    ppermute x0 -> x27, starting transfers between devices: none -> 34.6 us  [the longest x5 13.5 us: exchange(): return lax.ppermute(value, axis, [(i, i ^ bit) for i in range(count)])]
  transfers between devices with their start and end apart: 9 -> 30, of which waited for: 8 -> 15; matrix products, arithmetic and copies ran while one was open for 10% -> 8% of each run, Pallas kernels for 0% -> 0%
where the time goes in v1:
time: 812 us; the launch traced here: 801 us
  waiting for transfers between devices  363 us (45%)
  matrix products  159 us (20%)
  other arithmetic  139 us (17%)
  local copies, waits for them, and re-layouts  45.9 us (6%)
  blocking collectives  44.9 us (6%)
  starting transfers between devices  34.7 us (4%)
  between operations  15.2 us (2%)
    reduce_scatter x1, waiting for transfers between devices, reduce_grads(): lax.psum_scatter(whole, ('z', 'dp'), scatter_dimension=0, tiled=True)  206 us
    all_gather x1, waiting for transfers between devices, gather_weights(): return lax.all_gather(piece, ('z', 'dp'), axis=0, tiled=True)  110 us
    all_gather x1, blocking collectives, shards(): lax.all_gather(vectors.astype(BF), ('z', 'core'), axis=0, tiled=True)  44.9 us
    concatenate x1, other arithmetic, reduce_grads(): whole = jnp.concatenate(blocks, axis=0)  34.5 us
    convert_element_type x1, other arithmetic, attention_backward(): grad_scores = (probs * (grad_probs - row_sums)).astype(BF)  28.6 us
    dot_general x5, matrix products, rows_dot(): lax.dot_general(operand, matrix, (((1,), (1,)), ((), ())), preferred_elem...  28.2 us
    dot_general x5, matrix products, plain_dot(): lax.dot_general(operand, matrix, (((1,), (0,)), ((), ())), preferred_elem...  23.7 us
    dot_general x1, matrix products, attention_backward(): jnp.einsum('qhd,khd->hqk', grad_out, values, preferred_element_type=F32)  22.3 us
  transfers between devices with their start and end apart: 30, of which 15 were waited for; matrix products, arithmetic and copies ran while one was open for 8% of the time, Pallas kernels for 0%

profile of v1, /device:TPU:0, one launch (start us, length us, event | category | flops | bytes accessed | tf_op | source)
XLA Modules:
  0.0 801.3 jit_solution(12486800304038120248)
XLA Ops:
  18.8 3.7 fusion.46
  24.0 5.0 collective-permute-start.2
  30.6 44.9 %all-gather = bf16[8,1,1536]{2,1,0:T(2,128)(2,1)S(1)} all-gather(bf16[1,1,1536]{2,1,0:T(2,128)(2,1)S(1)} %reshape.273), channel_id=1, replica_groups=mesh['dp'=4,'z'=4,'core'=2] {'z','core'}, dimensions={0}, use_global_device_ids=true | all-gather | bytes 27648 | tf_op jit(solution)/shard_map/all_gather | solution.py:231
  82.2 110.1 %all-gather.4.cloned.1.call-done = bf16[6144,1024]{1,0:T(8,128)(2,1)} async-done(((bf16[384,1024]{1,0:T(8,128)(2,1)}), bf16[6144,1024]{1,0:T(8,128)(2,1)}) %all-gather.4.cloned.1.call-update) | async-done | bytes 12582928 | tf_op jit(solution)/shard_map/all_gather | solution.py:133
  192.3 6.0 fusion.22
  203.4 13.8 %fusion.86 = (f32[8,1024]{1,0:T(8,128)S(1)}, f32[8,1024,1024]{1,2,0:T(8,128)}) fusion(bf16[1024,8,64]{0,2,1:T(8,128)(2,1)S(1)} %bitcast.79, bf16[1024,8,64]{0,2,1:T(8,128)(2,1)S(1)} %bitcast.81, pred[1024]{0:T(1024)(128)(4,1)S(1)} %add_compare_fusion), kind=kOutput, calls=%fused_computation.207 | convolution fusion | flops 1098899456 | bytes 35685376 | tf_op jit(solution)/shard_map/qhd,khd->hqk/dot_general | solution.py:143
  217.2 13.0 %fusion = f32[8,1024]{1,0:T(8,128)S(1)} fusion(f32[8,1024,1024]{1,2,0:T(8,128)} %get-tuple-element.78, f32[8,1024]{1,0:T(8,128)S(1)} %get-tuple-element.77), kind=kLoop, calls=%fused_computation.6 | loop fusion | flops 16769024 | bytes 33619968 | tf_op jit(solution)/shard_map/reduce_sum | solution.py:153
  230.3 13.6 %fusion.42 = bf16[8,64,1024]{2,1,0:T(8,128)(2,1)S(1)} fusion(bf16[1024,8,64]{0,2,1:T(8,128)(2,1)S(1)} %bitcast.85, f32[8,1024,1024]{1,2,0:T(8,128)} %get-tuple-element.78, f32[8,1024]{1,0:T(8,128)S(1)} %fusion, f32[8,1024]{1,0:T(8,128)S(1)} %get-tuple-element.77), kind=kOutput, calls=%fused_computation.102 | convolution fusion | flops 1099431936 | bytes 35717120 | tf_op jit(solution)/shard_map/hqk,khd->qhd/dot_general | solution.py:155
  254.9 9.4 %multiply_convert_fusion.1 = (bf16[1024,2048]{1,0:T(8,128)(2,1)S(1)}, f32[1024,2048]{1,0:T(8,128)}) fusion(f32[2048]{0:T(1024)S(1)} %bitcast.119, bf16[6144,1024]{1,0:T(8,128)(2,1)} %all-gather.4.cloned.1.call-done, bf16[512,1024]{0,1:T(8,128)(2,1)} %collective-permute-done.6, bf16[512,1024]{0,1:T(8,128)(2,1)S(1)} %add_convert_fusion.2), kind=kOutput, calls=%fused_computation.21 | convolution fusion | flops 4311744512 | bytes 18882560 | tf_op jit(solution)/shard_map/dot_general | solution.py:23
  264.2 7.9 fusion.14
  285.4 6.0 collective-permute-done.12
  291.4 6.9 collective-permute-done.13
  304.1 8.9 %convert_reduce_fusion = (f32[2048]{0:T(1024)S(1)}, bf16[1024,2048]{1,0:T(8,128)(2,1)S(1)}) fusion(f32[1024,2048]{1,0:T(8,128)S(1)} %bitcast.122, f32[2048]{0:T(1024)S(1)} %bitcast.120, bf16[6144,1024]{1,0:T(8,128)(2,1)} %all-gather.4.cloned.1.call-done, bf16[512,1024]{0,1:T(8,128)(2,1)S(1)} %collective-permute-done.14, ...), kind=kOutput, calls=%fused_computation.20 | convolution fusion | flops 4326422528 | bytes 18890752 | tf_op jit(solution)/shard_map/dot_general | solution.py:23
  313.0 6.4 fusion.16
  328.7 6.4 convolution_convert_fusion.1
  335.1 7.3 convolution_convert_fusion.2
  346.4 14.3 %fusion.39 = bf16[8,64,1024]{2,1,0:T(8,128)(2,1)} fusion(bf16[1024,8,64]{0,2,1:T(8,128)(2,1)S(1)} %bitcast.83, f32[8,1024,1024]{1,2,0:T(8,128)} %get-tuple-element.78, f32[8,1024]{1,0:T(8,128)S(1)} %log_add_fusion), kind=kOutput, calls=%fused_computation.101 | convolution fusion | flops 1091043328 | bytes 35684352 | tf_op jit(solution)/shard_map/hqk,qhd->khd/dot_general | solution.py:175
  360.7 22.3 %multiply_reduce_fusion = (f32[8,1024]{1,0:T(8,128)S(1)}, f32[8,1024,1024]{1,2,0:T(8,128)}) fusion(f32[8,1024,1024]{1,2,0:T(8,128)} %get-tuple-element.78, f32[8,1024]{1,0:T(8,128)S(1)} %log_add_fusion, bf16[1024,8,64]{0,2,1:T(8,128)(2,1)S(1)} %bitcast.84, bf16[1024,8,64]{0,2,1:T(8,128)(2,1)} %bitcast.86), kind=kOutput, calls=%fused_computation.1 | convolution fusion | flops 1098899456 | bytes 69271552 | tf_op jit(solution)/shard_map/qhd,khd->hqk/dot_general | solution.py:170
  383.0 28.6 %multiply_convert_fusion = bf16[8,1024,1024]{1,2,0:T(8,128)(2,1)} fusion(f32[8,1024,1024]{1,2,0:T(8,128)} %get-tuple-element.82, f32[8,1024,1024]{1,2,0:T(8,128)} %get-tuple-element.78, f32[8,1024]{1,0:T(8,128)S(1)} %get-tuple-element.81, f32[8,1024]{1,0:T(8,128)S(1)} %log_add_fusion), kind=kLoop, calls=%fused_computation | loop fusion | flops 33554432 | bytes 83951616 | tf_op jit(solution)/shard_map/convert_element_type | solution.py:172
  411.7 11.9 %multiply_convert_fusion.2 = bf16[8,64,1024]{2,1,0:T(8,128)(2,1)} fusion(bf16[1024,8,64]{0,2,1:T(8,128)(2,1)S(1)} %bitcast.80, bf16[8,1024,1024]{1,2,0:T(8,128)(2,1)} %multiply_convert_fusion), kind=kOutput, calls=%fused_computation.83 | convolution fusion | flops 1074790400 | bytes 18874368 | tf_op jit(solution)/shard_map/hqk,qhd->khd/dot_general | solution.py:174
  423.6 10.2 %multiply_convert_fusion.3 = bf16[8,64,1024]{2,1,0:T(8,128)(2,1)} fusion(bf16[1024,8,64]{0,2,1:T(8,128)(2,1)} %bitcast.82, bf16[8,1024,1024]{1,2,0:T(8,128)(2,1)} %multiply_convert_fusion), kind=kOutput, calls=%fused_computation.84 | convolution fusion | flops 1074790400 | bytes 18874368 | tf_op jit(solution)/shard_map/hqk,khd->qhd/dot_general | solution.py:173
  438.8 5.8 convolution_convert_fusion
  444.6 34.5 %pad_maximum_fusion = bf16[6144,1024]{1,0:T(8,128)(2,1)} fusion(bf16[2048,1024]{1,0:T(8,128)(2,1)S(1)} %copy-done.15, bf16[2048,1024]{1,0:T(8,128)(2,1)S(1)} %copy-done.16, bf16[512,1024]{1,0:T(8,128)(2,1)S(1)} %copy-done.14, bf16[1536,1024]{1,0:T(8,128)(2,1)S(1)} %convolution_convert_fusion), kind=kLoop, calls=%fused_computation.11 | loop fusion | flops 50331648 | bytes 25165824 | tf_op jit(solution)/shard_map/concatenate | solution.py:137
  479.3 205.9 %reduce-scatter.2.cloned.1.call-done = bf16[384,1024]{1,0:T(8,128)(2,1)} async-done(((bf16[6144,1024]{1,0:T(8,128)(2,1)}), bf16[384,1024]{1,0:T(8,128)(2,1)}) %reduce-scatter.2.cloned.1.call-update) | async-done | bytes 786448 | tf_op jit(solution)/shard_map/reduce_scatter | solution.py:138
  695.9 5.5 fusion.20
  709.9 8.9 %collective-permute-start.23 = (f32[12288]{0:T(1024)S(1)}, f32[12288]{0:T(1024)}, u32[]{:S(2)}, u32[]{:S(2)}) collective-permute-start(f32[12288]{0:T(1024)S(1)} %add.388), channel_id=1, source_target_pairs={{0,2},{2,0},{4,6},{6,4},{1,3},{3,1},{5,7},{7,5},{8,10},{10,8},{12,... | collective-permute-start | bytes 147464 | tf_op jit(solution)/shard_map/ppermute | solution.py:40
  733.6 3.9 fusion.29
  737.5 3.7 broadcast_select_fusion.2
  748.0 5.6 collective-permute-done.20
  754.8 9.6 %collective-permute-done.19 = bf16[128,1024]{0,1:T(8,128)(2,1)S(1)} collective-permute-done((bf16[128,1024]{0,1:T(8,128)(2,1)}, bf16[128,1024]{0,1:T(8,128)(2,1)S(1)}, u32[]{:S(2)}, u32[]{:S(2)}) %collective-permute-start.19) | collective-permute-done | bytes 262176 | tf_op jit(solution)/shard_map/ppermute | solution.py:88
  769.9 10.5 %maximum_select_fusion = bf16[1024,1024]{1,0:T(8,128)(2,1)} fusion(bf16[512,512]{1,0:T(8,128)(2,1)S(1)} %get-tuple-element.50, bf16[512,512]{1,0:T(8,128)(2,1)S(1)} %get-tuple-element.48, bf16[512,512]{1,0:T(8,128)(2,1)S(1)} %get-tuple-element.49, bf16[512,512]{1,0:T(8,128)(2,1)S(1)} %get-tuple-element.47, bf16[512,1024]{1,0:T(8,128)(2,1)} %collective-permute-done.21, ...), kind=kLoop, calls=%fused_computation.78 | loop fusion | flops 13631488 | bytes 6291457 | tf_op jit(solution)/shard_map/jit(_where)/select_n | solution.py:125
  780.5 14.0 %add_multiply_fusion.1 = (f32[1536,1024]{1,0:T(8,128)}, f32[1536,1024]{1,0:T(8,128)}, f32[1536,1024]{1,0:T(8,128)}, f32[1536,1024]{1,0:T(8,128)}) fusion(f32[1536,1024]{1,0:T(8,128)S(1)} %bitcast.78, f32[1536,1024]{1,0:T(8,128)} %param.14, f32[1536,1024]{1,0:T(8,128)} %param.15, bf16[512,1024]{1,0:T(8,128)(2,1)} %get-tuple-element.38, ...), kind=kLoop, calls=%fused_computation.24 | loop fusion | flops 28311552 | bytes 47185920 | tf_op jit(solution)/shard_map/mul | solution.py:186
  (296 shorter events, 121.2 us)
Async XLA Ops:
  7.2 185.1 %all-gather.4.cloned.1.call-start = ((), (), s32[]{:S(2)}) async-start(), calls=%async_computation.1 | async-start | bytes 13369344 | tf_op jit(solution)/shard_map/all_gather | solution.py:133
  15.7 3.1 collective-permute-start.4
  22.6 662.6 %reduce-scatter.2.cloned.1.call-start = ((), (), s32[]{:S(2)}) async-start(), calls=%async_computation.2 | async-start | bytes 13369344 | tf_op jit(solution)/shard_map/reduce_scatter | solution.py:138
  24.0 52.9 %copy-start.53 = (s32[4]{0:T(128)S(1)}, s32[4]{0:T(128)}, u32[]{:S(2)}) copy-start(s32[4]{0:T(128)} %param.11) | copy-start | bytes 52
  24.0 52.3 %collective-permute-start.2 = (bf16[128,1024]{0,1:T(8,128)(2,1)S(1)}, bf16[128,1024]{0,1:T(8,128)(2,1)S(1)}, u32[]{:S(2)}, u32[]{:S(2)}) collective-permute-start(bf16[128,1024]{0,1:T(8,128)(2,1)S(1)} %bitcast.107), channel_id=1, source_target_pairs={{0,6},{2,0},{4,2},{6,4},{1,7},{3,1},{5,3},{7,5},{8,14},{10,8},{12,... | collective-permute-start | bytes 786440 | tf_op jit(solution)/shard_map/ppermute | solution.py:76
  29.2 47.1 %collective-permute-start = (bf16[128,1024]{0,1:T(8,128)(2,1)S(1)}, bf16[128,1024]{0,1:T(8,128)(2,1)S(1)}, u32[]{:S(2)}, u32[]{:S(2)}) collective-permute-start(bf16[128,1024]{0,1:T(8,128)(2,1)S(1)} %bitcast.110), channel_id=1, source_target_pairs={{0,2},{2,4},{4,6},{6,0},{1,3},{3,5},{5,7},{7,1},{8,10},{10,12},{12... | collective-permute-start | bytes 786440 | tf_op jit(solution)/shard_map/ppermute | solution.py:76
  29.5 46.9 %collective-permute-start.1 = (bf16[128,1024]{0,1:T(8,128)(2,1)S(1)}, bf16[128,1024]{0,1:T(8,128)(2,1)S(1)}, u32[]{:S(2)}, u32[]{:S(2)}) collective-permute-start(bf16[128,1024]{0,1:T(8,128)(2,1)S(1)} %bitcast.111), channel_id=1, source_target_pairs={{0,4},{2,6},{4,0},{6,2},{1,5},{3,7},{5,1},{7,3},{8,12},{10,14},{12... | collective-permute-start | bytes 786440 | tf_op jit(solution)/shard_map/ppermute | solution.py:76
  76.3 175.3 %copy-start.38 = (f32[1024]{0:T(1024)}, f32[1024]{0:T(1024)S(1)}, u32[]{:S(2)}) copy-start(f32[1024]{0:T(1024)S(1)} %get-tuple-element.70) | copy-start | bytes 12292
  76.5 4.7 collective-permute-start.3
  248.1 2.7 collective-permute-start.5
  252.0 2.9 collective-permute-start.6
  275.3 7.1 collective-permute-start.7
  276.3 15.1 %collective-permute-start.12 = (bf16[128,1024]{0,1:T(8,128)(2,1)}, bf16[128,1024]{0,1:T(8,128)(2,1)S(1)}, u32[]{:S(2)}, u32[]{:S(2)}) collective-permute-start(bf16[128,1024]{0,1:T(8,128)(2,1)} %bitcast.23), channel_id=1, source_target_pairs={{0,4},{2,6},{4,0},{6,2},{1,5},{3,7},{5,1},{7,3},{8,12},{10,14},{12... | collective-permute-start | bytes 786440 | tf_op jit(solution)/shard_map/ppermute | solution.py:76
  278.7 19.6 %collective-permute-start.13 = (bf16[128,1024]{0,1:T(8,128)(2,1)}, bf16[128,1024]{0,1:T(8,128)(2,1)S(1)}, u32[]{:S(2)}, u32[]{:S(2)}) collective-permute-start(bf16[128,1024]{0,1:T(8,128)(2,1)} %bitcast.24), channel_id=1, source_target_pairs={{0,6},{2,0},{4,2},{6,4},{1,7},{3,1},{5,3},{7,5},{8,14},{10,8},{12,... | collective-permute-start | bytes 786440 | tf_op jit(solution)/shard_map/ppermute | solution.py:76
  280.0 18.3 %collective-permute-start.11 = (bf16[128,1024]{0,1:T(8,128)(2,1)}, bf16[128,1024]{0,1:T(8,128)(2,1)S(1)}, u32[]{:S(2)}, u32[]{:S(2)}) collective-permute-start(bf16[128,1024]{0,1:T(8,128)(2,1)} %bitcast.108), channel_id=1, source_target_pairs={{0,2},{2,4},{4,6},{6,0},{1,3},{3,5},{5,7},{7,1},{8,10},{10,12},{12... | collective-permute-start | bytes 786440 | tf_op jit(solution)/shard_map/ppermute | solution.py:76
  301.4 2.7 collective-permute-start.14
  319.6 2.7 collective-permute-start.15
  326.6 15.8 %collective-permute-start.16 = (bf16[512,1024]{0,1:T(8,128)(2,1)S(1)}, bf16[512,1024]{0,1:T(8,128)(2,1)S(1)}, u32[]{:S(2)}, u32[]{:S(2)}) collective-permute-start(bf16[512,1024]{0,1:T(8,128)(2,1)S(1)} %get-tuple-element.28), channel_id=1, source_target_pairs={{0,1},{1,0},{2,3},{3,2},{4,5},{5,4},{6,7},{7,6},{8,9},{9,8},{10,11... | collective-permute-start | bytes 3145736 | tf_op jit(solution)/shard_map/ppermute | solution.py:35
  479.2 258.3 %all-gather.6.cloned.1.call-start = ((), (), s32[]{:S(2)}) async-start(), calls=%async_computation.3 | async-start | bytes 3932160 | tf_op jit(solution)/shard_map/all_gather | solution.py:139
  688.7 34.9 %collective-permute-start.10 = (bf16[128,1024]{0,1:T(8,128)(2,1)}, bf16[128,1024]{0,1:T(8,128)(2,1)}, u32[]{:S(2)}, u32[]{:S(2)}) collective-permute-start(bf16[128,1024]{0,1:T(8,128)(2,1)} %get-tuple-element.59), channel_id=1, source_target_pairs={{0,2},{2,4},{4,6},{6,0},{1,3},{3,5},{5,7},{7,1},{8,10},{10,12},{12... | collective-permute-start | bytes 786440 | tf_op jit(solution)/shard_map/ppermute | solution.py:88
  690.3 29.2 %collective-permute-start.9 = (bf16[128,1024]{0,1:T(8,128)(2,1)}, bf16[128,1024]{0,1:T(8,128)(2,1)}, u32[]{:S(2)}, u32[]{:S(2)}) collective-permute-start(bf16[128,1024]{0,1:T(8,128)(2,1)} %get-tuple-element.60), channel_id=1, source_target_pairs={{0,4},{2,6},{4,0},{6,2},{1,5},{3,7},{5,1},{7,3},{8,12},{10,14},{12... | collective-permute-start | bytes 786440 | tf_op jit(solution)/shard_map/ppermute | solution.py:88
  691.4 15.9 %collective-permute-start.8 = (bf16[128,1024]{0,1:T(8,128)(2,1)}, bf16[128,1024]{0,1:T(8,128)(2,1)S(1)}, u32[]{:S(2)}, u32[]{:S(2)}) collective-permute-start(bf16[128,1024]{0,1:T(8,128)(2,1)} %get-tuple-element.61), channel_id=1, source_target_pairs={{0,6},{2,0},{4,2},{6,4},{1,7},{3,1},{5,3},{7,5},{8,14},{10,8},{12,... | collective-permute-start | bytes 786440 | tf_op jit(solution)/shard_map/ppermute | solution.py:88
  704.6 29.0 %collective-permute-start.17 = (bf16[512,1024]{0,1:T(8,128)(2,1)}, bf16[512,1024]{0,1:T(8,128)(2,1)S(1)}, u32[]{:S(2)}, u32[]{:S(2)}) collective-permute-start(bf16[512,1024]{0,1:T(8,128)(2,1)} %slice.398), channel_id=1, source_target_pairs={{0,1},{1,0},{2,3},{3,2},{4,5},{5,4},{6,7},{7,6},{8,9},{9,8},{10,11... | collective-permute-start | bytes 3145736 | tf_op jit(solution)/shard_map/ppermute | solution.py:35
  704.7 4.4 collective-permute-start.22
  709.9 11.0 %collective-permute-start.23 = (f32[12288]{0:T(1024)S(1)}, f32[12288]{0:T(1024)}, u32[]{:S(2)}, u32[]{:S(2)}) collective-permute-start(f32[12288]{0:T(1024)S(1)} %add.388), channel_id=1, source_target_pairs={{0,2},{2,0},{4,6},{6,4},{1,3},{3,1},{5,7},{7,5},{8,10},{10,8},{12,... | collective-permute-start | bytes 147464 | tf_op jit(solution)/shard_map/ppermute | solution.py:40
  721.7 5.4 collective-permute-start.24
  727.9 4.1 collective-permute-start.25
  732.0 15.0 %collective-permute-start.26 = (f32[12288]{0:T(1024)S(1)}, f32[12288]{0:T(1024)S(1)}, u32[]{:S(2)}, u32[]{:S(2)}) collective-permute-start(f32[12288]{0:T(1024)S(1)} %add.391), channel_id=1, source_target_pairs={{0,16},{8,24},{16,0},{24,8},{1,17},{9,25},{17,1},{25,9},{2,18},{10... | collective-permute-start | bytes 147464 | tf_op jit(solution)/shard_map/ppermute | solution.py:40
  741.2 27.0 %collective-permute-start.21 = (bf16[512,1024]{1,0:T(8,128)(2,1)}, bf16[512,1024]{1,0:T(8,128)(2,1)}, u32[]{:S(2)}, u32[]{:S(2)}) collective-permute-start(bf16[512,1024]{1,0:T(8,128)(2,1)} %get-tuple-element.37), channel_id=1, source_target_pairs={{0,1},{1,0},{2,3},{3,2},{4,5},{5,4},{6,7},{7,6},{8,9},{9,8},{10,11... | collective-permute-start | bytes 3145736 | tf_op jit(solution)/shard_map/ppermute | solution.py:35
  742.3 11.4 %collective-permute-start.20 = (bf16[128,1024]{0,1:T(8,128)(2,1)}, bf16[128,1024]{0,1:T(8,128)(2,1)}, u32[]{:S(2)}, u32[]{:S(2)}) collective-permute-start(bf16[128,1024]{0,1:T(8,128)(2,1)} %get-tuple-element.51), channel_id=1, source_target_pairs={{0,2},{2,4},{4,6},{6,0},{1,3},{3,5},{5,7},{7,1},{8,10},{10,12},{12... | collective-permute-start | bytes 786440 | tf_op jit(solution)/shard_map/ppermute | solution.py:88
  744.0 20.3 %collective-permute-start.19 = (bf16[128,1024]{0,1:T(8,128)(2,1)}, bf16[128,1024]{0,1:T(8,128)(2,1)S(1)}, u32[]{:S(2)}, u32[]{:S(2)}) collective-permute-start(bf16[128,1024]{0,1:T(8,128)(2,1)} %get-tuple-element.52), channel_id=1, source_target_pairs={{0,4},{2,6},{4,0},{6,2},{1,5},{3,7},{5,1},{7,3},{8,12},{10,14},{12... | collective-permute-start | bytes 786440 | tf_op jit(solution)/shard_map/ppermute | solution.py:88
  745.1 19.4 %collective-permute-start.18 = (bf16[128,1024]{0,1:T(8,128)(2,1)}, bf16[128,1024]{0,1:T(8,128)(2,1)S(1)}, u32[]{:S(2)}, u32[]{:S(2)}) collective-permute-start(bf16[128,1024]{0,1:T(8,128)(2,1)} %get-tuple-element.53), channel_id=1, source_target_pairs={{0,6},{2,0},{4,2},{6,4},{1,7},{3,1},{5,3},{7,5},{8,14},{10,8},{12,... | collective-permute-start | bytes 786440 | tf_op jit(solution)/shard_map/ppermute | solution.py:88
  (58 other events, 493.2 us)
Sparse Core Ops, SparseCore 0:
  22.7 169.5 all-gather.3
  479.3 205.7 reduce-scatter.1
  687.1 44.0 all-gather.5

commit v2 on v1

v2 whole, which is shorter than its diff:
```python
import math

import jax
import jax.numpy as jnp
from jax import lax
from jax.experimental import pallas as pl
from jax.experimental.pallas import tpu as pltpu
from jax.sharding import Mesh
from jax.sharding import PartitionSpec as P

D = 1024
FF = 4096
HD = 64
PAIR = 2 * HD
STEP = 10
EPSILON = 1e-05
LEARN_RATE = 0.003
BF = jnp.bfloat16
F32 = jnp.float32
HALF = D // 2
BLOCK = 512
EXTRA = 16
QUARTERS = 4
PIECE = 3 * PAIR + EXTRA
MIB = 2**20


def rows_dot(operand, matrix):
    return lax.dot_general(operand, matrix, (((1,), (1,)), ((), ())), preferred_element_type=F32)


def cols_dot(operand, matrix):
    return lax.dot_general(operand, matrix, (((0,), (0,)), ((), ())), preferred_element_type=F32)


def plain_dot(operand, matrix):
    return lax.dot_general(operand, matrix, (((1,), (0,)), ((), ())), preferred_element_type=F32)


def swap(value):
    return lax.ppermute(value, "core", [(0, 1), (1, 0)])


def layer_norm(inputs, gain_vec, shift_vec):
    centre = jnp.mean(inputs, axis=-1, keepdims=True)
    shifted = inputs - centre
    inverse = lax.rsqrt(jnp.mean(shifted * shifted, axis=-1, keepdims=True) + EPSILON)
    normed = shifted * inverse
    return (normed * gain_vec + shift_vec, normed, inverse)


def norm_back(grad_out, normed, inverse, gain_vec):
    scaled = grad_out * gain_vec
    inner_term = (
        scaled
        - jnp.mean(scaled, axis=-1, keepdims=True)
        - normed * jnp.mean(scaled * normed, axis=-1, keepdims=True)
    )
    return (inverse * inner_term, jnp.sum(grad_out * normed, axis=0), jnp.sum(grad_out, axis=0))


def to_chips(blocks, z):
    count = lax.axis_size("z")
    parts = []
    for shift in range(count):
        part = lax.dynamic_index_in_dim(blocks, (z + shift) % count, 0, keepdims=False)
        if shift:
            part = lax.ppermute(part, "z", [(i, (i + shift) % count) for i in range(count)])
        parts.append(part)
    return jnp.concatenate(parts, axis=0)


def from_chips(rows, z):
    count = lax.axis_size("z")
    blocks = rows.reshape(count, -1, rows.shape[-1])
    result = blocks
    for shift in range(count):
        part = blocks[shift]
        if shift:
            part = lax.ppermute(part, "z", [(i, (i - shift) % count) for i in range(count)])
        result = lax.dynamic_update_index_in_dim(result, part, (z + shift) % count, 0)
    return result


def is_out_projection(z, core):
    return jnp.logical_and(z == 1, core == 0)


def gather_weights(weights, vectors, z, core):
    count = lax.axis_size("dp")
    rows = BLOCK // count
    low = weights.astype(BF)
    top = jnp.where(is_out_projection(z, core), low[:D].T, low[:D])
    vector = jnp.pad(vectors.astype(BF), (0, 2 * D - vectors.shape[0])).reshape(2, D)
    vector = jnp.pad(vector, ((0, EXTRA - 2), (0, 0)))
    other = swap(jnp.concatenate([top[BLOCK:], vector], axis=0))
    pair = jnp.stack([vector, other[BLOCK:]])
    pair = jnp.where(core == 0, pair, pair[::-1]).reshape(2, -1)[:, : vectors.shape[0]]
    pair = jnp.pad(pair.reshape(-1, D), ((0, EXTRA - 3), (0, 0)))
    start = lax.axis_index("dp") * rows
    if count > QUARTERS:
        spare = EXTRA * QUARTERS // count
        pair = lax.dynamic_slice_in_dim(pair, (start % PAIR) // rows * spare, spare, 0)
    first, last, middle = (
        lax.dynamic_slice_in_dim(item, start, rows, 0) for item in (top, low[D:], other)
    )
    piece = jnp.where(
        core == 0,
        jnp.concatenate([first, last, middle, pair], axis=0),
        jnp.concatenate([middle, first, last, pair], axis=0),
    )
    whole = lax.all_gather(piece, ("z", "dp"), axis=0, tiled=True)
    if count == QUARTERS:
        whole = whole.reshape(-1, PIECE, D)
    else:
        whole = whole.reshape(-1, count // QUARTERS, piece.shape[0], D)
        blocks = whole[:, :, : 3 * rows].reshape(-1, count // QUARTERS, 3, rows, D).swapaxes(1, 2)
        spare = whole[:, :, 3 * rows :].reshape(-1, EXTRA, D)
        whole = jnp.concatenate([blocks.reshape(-1, 3 * PAIR, D), spare], axis=1)
    found = whole.reshape(-1, QUARTERS, PIECE, D)[:, 0, 3 * PAIR : 3 * PAIR + 3]
    return whole, found.reshape(-1).astype(F32)


def sum_over_dp(grads):
    count = lax.axis_size("dp") // QUARTERS
    if count > 1:
        grads = grads.reshape(QUARTERS, -1, count, PAIR // count, D).swapaxes(1, 2)
    return lax.psum_scatter(grads.reshape(-1, D), "dp", scatter_dimension=0, tiled=True)


def by_hand():
    return lax.axis_size("dp") == 4 and lax.axis_size("z") == 4


def plus(first, second):
    return (first.astype(F32) + second.astype(F32)).astype(BF)


def across(bit, value):
    return lax.ppermute(value, "dp", [(i, i ^ bit) for i in range(4)])


def at(value, index, axis):
    return lax.dynamic_index_in_dim(value, index, axis, keepdims=False)


def reduce_late(late, sum_ff):
    d = lax.axis_index("dp")
    x, y = d % 2, d // 2
    late = late.reshape(2, 2, -1, D)
    a, b = late[..., :HALF], late[..., HALF:]
    got_a, got_b = across(1, at(a, 1 - x, 1)), across(2, at(b, 1 - y, 0))
    got_a, got_b, a, b, sum_ff = lax.optimization_barrier((got_a, got_b, a, b, sum_ff))
    a, b = at(a, x, 1), at(b, y, 0)
    far_a = across(2, plus(at(a, 1 - y, 0), at(got_a, 1 - y, 0)))
    far_b = across(1, plus(at(b, 1 - x, 0), at(got_b, 1 - x, 0)))
    far_a, far_b, a, b = lax.optimization_barrier((far_a, far_b, a, b))
    a = plus(plus(at(a, y, 0), at(got_a, y, 0)), far_a)
    b = plus(plus(at(b, x, 0), at(got_b, x, 0)), far_b)
    return jnp.concatenate([a, b], axis=-1), sum_ff


def gather_pieces(piece, grad_tokens):
    d = lax.axis_index("dp")
    a, b = piece[:, :HALF], piece[:, HALF:]
    pair = jnp.stack([a, b])
    got_x, got_y = across(1, pair), across(2, pair)
    got_x, got_y, pair = lax.optimization_barrier((got_x, got_y, pair))
    far_a, far_b = across(2, got_x[0]), across(1, got_y[1])
    far_a, far_b, pair, grad_tokens = lax.optimization_barrier((far_a, far_b, pair, grad_tokens))
    result = jnp.zeros((4, *piece.shape), BF)
    far = jnp.stack([far_a, far_b])
    for index, value in enumerate((pair, got_x, got_y, far)):
        for half in range(2):
            result = lax.dynamic_update_slice(
                result, value[half][None], (d ^ index, 0, half * HALF)
            )
    return result, grad_tokens


def lanes_of(shape, head):
    lane = lax.broadcasted_iota(jnp.int32, shape, 1)
    return (lane >= HD) if head else (lane < HD), lane - HD * (1 - head)


def split_three(value):
    high = value.astype(BF).astype(F32)
    mid = (value - high).astype(BF).astype(F32)
    return high, mid, (value - high - mid).astype(BF).astype(F32)


def spread_lanes(place, values):
    result = jnp.zeros(place.shape, F32)
    for lane, value in enumerate(values):
        result = jnp.where(place == lane, value, result)
    return result


def whole_block(shape):
    return pl.BlockSpec(shape, lambda *_: (0,) * len(shape))


SCALAR = pl.BlockSpec(memory_space=pltpu.SMEM)
NO_COST = pl.CostEstimate(flops=1, bytes_accessed=1, transcendentals=0)


def qkv_kernel(core_ref, x_ref, w_ref, vector_ref, out_ref):
    quarter = pl.program_id(0)
    row = core_ref[0] * QUARTERS + quarter
    bias_q = vector_ref[pl.ds(row, 1), :]
    bias_v = vector_ref[pl.ds(D // PAIR + row, 1), :]
    bias = jnp.concatenate([bias_q, jnp.zeros_like(bias_q), bias_v], axis=1)
    out_ref[...] = (rows_dot(x_ref[...], w_ref[0]) + bias).astype(BF)


def project(core, x, whole, vec):
    rows = x.shape[0]
    return pl.pallas_call(
        qkv_kernel,
        grid=(QUARTERS,),
        in_specs=[
            SCALAR,
            whole_block(x.shape),
            pl.BlockSpec((1, 3 * PAIR, D), lambda quarter: (quarter, 0, 0)),
            whole_block(vec.shape),
        ],
        out_specs=pl.BlockSpec((rows, 3 * PAIR), lambda quarter: (0, quarter)),
        out_shape=jax.ShapeDtypeStruct((rows, 3 * HALF), BF),
        cost_estimate=NO_COST,
        compiler_params=pltpu.CompilerParams(vmem_limit_bytes=40 * MIB),
    )(core, x, whole, vec)


def forward_kernel(q_ref, k_ref, v_ref, key_ref, o_ref, extra_ref):
    q, k, v, key_extra = q_ref[...], k_ref[...], v_ref[...], key_ref[...]
    outs, extras = [], []
    for head in range(2):
        in_q, place_q = lanes_of(q.shape, head)
        in_k, place_k = lanes_of(k.shape, head)
        keys = jnp.where(in_k, k, key_extra)
        queries = jnp.where(in_q, q * BF(0.125), jnp.where(place_q == 0, BF(1), BF(0)))
        values = jnp.where(in_k, v, jnp.where(place_k == 0, BF(1), BF(0)))
        scores = rows_dot(queries, keys)
        highest = jnp.max(scores, axis=1, keepdims=True)
        terms = jnp.exp(scores - highest).astype(BF)
        out = plain_dot(terms, values)
        column = HD * (1 - head)
        total = out[:, column : column + 1]
        outs.append(out * (1.0 / total))
        parts = split_three(-(highest + jnp.log(total)))
        extras.append(spread_lanes(place_q, (1.0, *parts)))
    in_first, _ = lanes_of(q.shape, 0)
    o_ref[...] = jnp.where(in_first, outs[0], outs[1]).astype(BF)
    extra_ref[...] = jnp.where(in_first, extras[1], extras[0]).astype(BF)


def attention_forward(merged, key_extra, step):
    rows = merged.shape[0]
    some = pl.BlockSpec((step, PAIR), lambda pair, part: (part, 3 * pair))
    ours = pl.BlockSpec((step, PAIR), lambda pair, part: (part, pair))
    keys = pl.BlockSpec((rows, PAIR), lambda pair, part: (0, 3 * pair + 1))
    values = pl.BlockSpec((rows, PAIR), lambda pair, part: (0, 3 * pair + 2))
    return pl.pallas_call(
        forward_kernel,
        grid=(HALF // PAIR, rows // step),
        in_specs=[some, keys, values, whole_block(key_extra.shape)],
        out_specs=[ours, ours],
        out_shape=[jax.ShapeDtypeStruct((rows, HALF), BF)] * 2,
        cost_estimate=NO_COST,
        compiler_params=pltpu.CompilerParams(vmem_limit_bytes=48 * MIB),
    )(merged, merged, merged, key_extra)


def backward_kernel(
    q_ref, extra_ref, k_ref, v_ref, key_ref, o_ref, do_ref, out_ref, dk_sum, dv_sum
):
    part = pl.program_id(1)
    q, extra, k, v = q_ref[...], extra_ref[...], k_ref[...], v_ref[...]
    key_extra, do = key_ref[...], do_ref[...]
    product = do.astype(F32) * o_ref[...].astype(F32)
    zero = BF(0)
    dq = dk = dv = 0.0
    for head in range(2):
        in_q, place_q = lanes_of(q.shape, head)
        in_k, place_k = lanes_of(k.shape, head)
        scaled = jnp.where(in_q, q * BF(0.125), zero)
        queries = jnp.where(in_q, scaled, extra)
        keys = jnp.where(in_k, k, key_extra)
        only_k = jnp.where(in_k, k, zero)
        only_do = jnp.where(in_q, do, zero)
        row_sum = jnp.sum(jnp.where(in_q, product, 0.0), axis=1, keepdims=True)
        grads = jnp.where(in_q, do, spread_lanes(place_q, split_three(-row_sum)).astype(BF))
        ones = jnp.where((place_k >= 0) & (place_k < 3), BF(1), zero)
        values = jnp.where(in_k, v, ones)
        probs = jnp.exp(rows_dot(keys, queries))
        grad_scores = (probs * rows_dot(values, grads)).astype(BF)
        dv = dv + plain_dot(probs.astype(BF), only_do)
        dk = dk + plain_dot(grad_scores, scaled)
        dq = dq + cols_dot(grad_scores, only_k)
    step = q.shape[0]
    out_ref[pl.ds(part * step, step), :PAIR] = (dq * 0.125).astype(BF)

    @pl.when(part == 0)
    def _():
        dk_sum[...] = dk
        dv_sum[...] = dv

    @pl.when(part > 0)
    def _():
        dk_sum[...] += dk
        dv_sum[...] += dv

    @pl.when(part == pl.num_programs(1) - 1)
    def _():
        out_ref[:, PAIR : 2 * PAIR] = dk_sum[...].astype(BF)
        out_ref[:, 2 * PAIR :] = dv_sum[...].astype(BF)


def attention_backward(merged, extra, key_extra, heads_out, grad_out, step):
    rows = merged.shape[0]
    some = pl.BlockSpec((step, PAIR), lambda pair, part: (part, 3 * pair))
    ours = pl.BlockSpec((step, PAIR), lambda pair, part: (part, pair))
    keys = pl.BlockSpec((rows, PAIR), lambda pair, part: (0, 3 * pair + 1))
    values = pl.BlockSpec((rows, PAIR), lambda pair, part: (0, 3 * pair + 2))
    return pl.pallas_call(
        backward_kernel,
        grid=(HALF // PAIR, rows // step),
        in_specs=[some, ours, keys, values, whole_block(key_extra.shape), ours, ours],
        out_specs=pl.BlockSpec((rows, 3 * PAIR), lambda pair, part: (0, pair)),
        out_shape=jax.ShapeDtypeStruct((rows, 3 * HALF), BF),
        scratch_shapes=[pltpu.VMEM((rows, PAIR), F32)] * 2,
        cost_estimate=NO_COST,
        compiler_params=pltpu.CompilerParams(vmem_limit_bytes=56 * MIB),
    )(merged, extra, merged, merged, key_extra, heads_out, grad_out)


def key_lanes(allowed):
    lane = jnp.arange(PAIR)[None, :] % HD
    bias = jnp.where(allowed, 0.0, -1e30)[:, None]
    return jnp.where(lane == 0, bias, jnp.where(lane < 4, 1.0, 0.0)).astype(BF)


def weight_block(chip, part, count=1):
    return pl.BlockSpec(
        (1, count * PAIR, D), lambda quarter: (chip * QUARTERS + quarter, part // count, 0)
    )


UP_BLOCKS = (weight_block(1, 1), weight_block(1, 2), weight_block(2, 0, 2))
DOWN_BLOCKS = (weight_block(2, 2), weight_block(3, 0, 3))


def joined(refs):
    return jnp.concatenate([ref[0] for ref in refs], axis=0)


def feed_forward_kernel(
    core_ref, u_ref, up0, up1, up2, down0, down1, vector_ref,
    hidden_ref, slope_ref, mine_ref, other_ref, total,
):
    quarter = pl.program_id(0)
    rows = [
        vector_ref[pl.ds(3 * D // PAIR + (2 * n + core_ref[0]) * QUARTERS + quarter, 1), :]
        for n in range(4)
    ]
    z = rows_dot(u_ref[...], joined((up0, up1, up2))) + jnp.concatenate(rows, axis=1)
    cdf = 0.5 * (1.0 + lax.erf(z * (1.0 / math.sqrt(2.0))))
    slope = cdf + z * jnp.exp(-0.5 * z * z) * (1.0 / math.sqrt(2.0 * math.pi))
    hidden = (z * cdf).astype(BF)
    hidden_ref[...] = hidden
    slope_ref[...] = slope.astype(BF)
    part = plain_dot(hidden, joined((down0, down1)))

    @pl.when(quarter == 0)
    def _():
        total[...] = part

    @pl.when(quarter > 0)
    def _():
        total[...] += part

    @pl.when(quarter == QUARTERS - 1)
    def _():
        half = mine_ref.shape[0]
        mine_ref[...] = total[:half]
        other_ref[...] = total[half:].astype(BF)


def feed_forward(core, u, whole, vec):
    rows = u.shape[0]
    columns = pl.BlockSpec((rows, BLOCK), lambda quarter: (0, quarter))
    half = (rows // 2, D)
    return pl.pallas_call(
        feed_forward_kernel,
        grid=(QUARTERS,),
        in_specs=[SCALAR, whole_block(u.shape), *UP_BLOCKS, *DOWN_BLOCKS, whole_block(vec.shape)],
        out_specs=[columns, columns, whole_block(half), whole_block(half)],
        out_shape=[
            jax.ShapeDtypeStruct((rows, FF // 2), BF),
            jax.ShapeDtypeStruct((rows, FF // 2), BF),
            jax.ShapeDtypeStruct(half, F32),
            jax.ShapeDtypeStruct(half, BF),
        ],
        scratch_shapes=[pltpu.VMEM((rows, D), F32)],
        cost_estimate=NO_COST,
        compiler_params=pltpu.CompilerParams(vmem_limit_bytes=56 * MIB),
    )(core, u, whole, whole, whole, whole, whole, vec)


def feed_backward_kernel(
    df_ref, u_ref, hidden_ref, slope_ref, up0, up1, up2, down0, down1,
    grads_ref, bias_ref, mine_ref, other_ref, total,
):
    quarter = pl.program_id(0)
    df = df_ref[...]
    dz32 = rows_dot(df, joined((down0, down1))) * slope_ref[...].astype(F32)
    dz = dz32.astype(BF)
    bias_ref[...] = jnp.sum(dz.astype(F32), axis=0, keepdims=True)
    grads_ref[0, :BLOCK] = cols_dot(dz, u_ref[...]).astype(BF)
    grads_ref[0, BLOCK:] = cols_dot(hidden_ref[...], df).astype(BF)
    part = plain_dot(dz, joined((up0, up1, up2)))

    @pl.when(quarter == 0)
    def _():
        total[...] = part

    @pl.when(quarter > 0)
    def _():
        total[...] += part

    @pl.when(quarter == QUARTERS - 1)
    def _():
        half = mine_ref.shape[0]
        mine_ref[...] = total[:half]
        other_ref[...] = total[half:].astype(BF)


def feed_backward(df, u, hidden, slope, whole):
    rows = u.shape[0]
    columns = pl.BlockSpec((rows, BLOCK), lambda quarter: (0, quarter))
    half = (rows // 2, D)
    return pl.pallas_call(
        feed_backward_kernel,
        grid=(QUARTERS,),
        in_specs=[
            whole_block(df.shape), whole_block(u.shape), columns, columns, *UP_BLOCKS, *DOWN_BLOCKS
        ],
        out_specs=[
            pl.BlockSpec((1, 2 * BLOCK, D), lambda quarter: (quarter, 0, 0)),
            pl.BlockSpec((1, BLOCK), lambda quarter: (0, quarter)),
            whole_block(half),
            whole_block(half),
        ],
        out_shape=[
            jax.ShapeDtypeStruct((QUARTERS, 2 * BLOCK, D), BF),
            jax.ShapeDtypeStruct((1, FF // 2), F32),
            jax.ShapeDtypeStruct(half, F32),
            jax.ShapeDtypeStruct(half, BF),
        ],
        scratch_shapes=[pltpu.VMEM((rows, D), F32)],
        cost_estimate=NO_COST,
        compiler_params=pltpu.CompilerParams(vmem_limit_bytes=60 * MIB),
    )(df, u, hidden, slope, whole, whole, whole, whole, whole)


def adamw_update(parameter, gradient, first_old, second_old, decay_rate):
    step_float = float(STEP)
    first_new = 0.9 * first_old + 0.1 * gradient
    second_new = 0.999 * second_old + 0.001 * gradient * gradient
    first_fix = first_new / (1.0 - 0.9**step_float)
    second_fix = second_new / (1.0 - 0.999**step_float)
    update = first_fix / (jnp.sqrt(second_fix) + 1e-08)
    return (-LEARN_RATE * (update + decay_rate * parameter), first_new, second_new)


def share(partial):
    half = partial.shape[0] // 2
    return partial[:half] + swap(partial[half:].astype(BF)).astype(F32)


def both(rows):
    return jnp.concatenate([rows, swap(rows)], axis=0)


def spread_part(vector, core, pieces):
    parts = vector.reshape(pieces, 1, -1)
    mine = (jnp.arange(2) == core)[None, :, None]
    return jnp.where(mine, parts, 0.0).reshape(-1)


def shards(
    tokens,
    cotangent,
    lengths,
    weights,
    vectors,
    first_weights,
    second_weights,
    first_vectors,
    second_vectors,
):
    z, core = lax.axis_index("z"), lax.axis_index("core")
    count, dp_count = lax.axis_size("z"), lax.axis_size("dp")
    per_device = tokens.shape[1]
    rows = count * per_device
    length = lengths[z]
    block = jnp.arange(count, dtype=jnp.int32)[:, None]
    inner = jnp.arange(per_device, dtype=jnp.int32)[None, :]
    chip_of = (z - block) % count
    here = ((chip_of * 2 + core) * per_device + inner).reshape(rows)
    there = ((chip_of * 2 + 1 - core) * per_device + inner).reshape(rows)
    key_extra = key_lanes(jnp.concatenate([here, there]) < length)
    live = (here < length).astype(F32)[:, None]
    core_id = core.astype(jnp.int32).reshape(1)

    whole, vec = gather_weights(weights, vectors, z, core)
    x_mine = to_chips(tokens, z)
    x = both(x_mine)
    whole, x, x_mine, cotangent = lax.optimization_barrier((whole, x, x_mine, cotangent))
    grad_out = to_chips(cotangent, z)
    bounds = [0, D, 2 * D, 3 * D, 3 * D + FF] + [(n + 4) * D + FF for n in range(6)]
    _, _, bias_o, _, bias_down, gain_one, shift_one, gain_two, shift_two = (
        vec[bounds[n] : bounds[n + 1]] for n in range(9)
    )
    vec = vec.reshape(-1, PAIR)
    w_out = whole[QUARTERS : 2 * QUARTERS, :PAIR].reshape(HALF, D)

    merged = project(core_id, x, whole, vec)
    heads_out, extra = attention_forward(merged, key_extra, 2 * rows)
    heads_out, extra, grad_out = lax.optimization_barrier((heads_out, extra, grad_out))
    normed_in, normed_one, inverse_one = layer_norm(
        x_mine.astype(F32) + share(plain_dot(heads_out, w_out)) + bias_o, gain_one, shift_one
    )
    u_mine = normed_in.astype(BF)
    u = both(u_mine)
    hidden, slope, feed, feed_other = feed_forward(core_id, u, whole, vec)
    feed = feed + swap(feed_other).astype(F32) + bias_down
    result, normed_two, inverse_two = layer_norm(u_mine.astype(F32) + feed, gain_two, shift_two)
    layer_out = result.astype(BF)

    grad_out = grad_out.astype(F32) * live
    grad_two, grad_gain_two, grad_shift_two = norm_back(grad_out, normed_two, inverse_two, gain_two)
    df_mine = grad_two.astype(BF)
    grad_bias_down = jnp.sum(df_mine.astype(F32), axis=0)
    grads_ff, grad_bias_up, du, du_other = feed_backward(both(df_mine), u, hidden, slope, whole)
    sum_ff = sum_over_dp(grads_ff)
    du = du + swap(du_other).astype(F32) + grad_two
    grad_one, grad_gain_one, grad_shift_one = norm_back(du, normed_one, inverse_one, gain_one)
    da_mine = grad_one.astype(BF)
    da = both(da_mine)
    grad_bias_o = jnp.sum(da_mine.astype(F32), axis=0)
    do = rows_dot(da, w_out).astype(BF)
    grad_wo = cols_dot(heads_out, da).astype(BF)
    do, layer_out = lax.optimization_barrier((do, layer_out))
    layer_out = from_chips(layer_out, z)
    d_merged = attention_backward(merged, extra, key_extra, heads_out, do, rows)
    d_merged, layer_out = lax.optimization_barrier((d_merged, layer_out))
    grad_rows = share(plain_dot(d_merged, whole[:QUARTERS, : 3 * PAIR].reshape(-1, D))) + grad_one
    grad_rows = grad_rows.astype(BF)
    grad_qkv = cols_dot(d_merged, x).astype(BF)
    sums = jnp.sum(d_merged.astype(F32), axis=0).reshape(QUARTERS, 3, PAIR)
    vector_grad = jnp.concatenate(
        [
            spread_part(sums[:, 0], core, 1),
            spread_part(sums[:, 2], core, 1),
            grad_bias_o,
            spread_part(grad_bias_up.reshape(QUARTERS, 4, PAIR).swapaxes(0, 1), core, 4),
            grad_bias_down,
            grad_gain_one,
            grad_shift_one,
            grad_gain_two,
            grad_shift_two,
        ]
    ).astype(BF)
    shares = vector_grad.reshape(count, dp_count, -1).swapaxes(0, 1)
    if by_hand():
        shares = shares.reshape(dp_count, -1, D)
        shares = jnp.pad(shares, ((0, 0), (0, EXTRA - shares.shape[1]), (0, 0)))
    else:
        shares = jnp.pad(shares, ((0, 0), (0, 0), (0, EXTRA * D - shares.shape[2])))
        shares = shares.reshape(dp_count, count * EXTRA, D)
    run = PAIR * QUARTERS // dp_count
    late = jnp.concatenate(
        [
            jnp.concatenate(
                [grad_qkv.reshape(QUARTERS, 3 * PAIR, D), grad_wo.reshape(QUARTERS, PAIR, D)], axis=1
            )
            .reshape(QUARTERS, 4, dp_count // QUARTERS, run, D)
            .swapaxes(1, 2)
            .reshape(dp_count, 4 * run, D),
            shares,
        ],
        axis=1,
    )
    if by_hand():
        late, sum_ff = reduce_late(late, sum_ff)
        slab = late[4 * PAIR :]
        chips = [late[: 3 * PAIR], slab, late[3 * PAIR : 4 * PAIR], sum_ff[: 2 * PAIR], slab]
        chips += [sum_ff[2 * PAIR : 5 * PAIR], slab, sum_ff[5 * PAIR :], slab]
        piece = lax.psum_scatter(
            jnp.concatenate(chips, axis=0), "z", scatter_dimension=0, tiled=True
        )
        piece, grad_rows = lax.optimization_barrier((piece, grad_rows))
        summed, grad_tokens = gather_pieces(piece, from_chips(grad_rows, z))
    else:
        grad_tokens = from_chips(grad_rows, z)
        sum_late = lax.psum_scatter(late.reshape(-1, D), "dp", scatter_dimension=0, tiled=True)
        parts = [sum_late[n * run : (n + 1) * run] for n in range(4)]
        parts += [sum_ff[n * run : (n + 1) * run] for n in range(8)]
        spare = sum_late[4 * run :].reshape(count, EXTRA, D)
        chips = [
            jnp.concatenate([*parts[3 * chip : 3 * chip + 3], spare[chip]], axis=0)
            for chip in range(count)
        ]
        piece = lax.psum_scatter(
            jnp.concatenate(chips, axis=0), "z", scatter_dimension=0, tiled=True
        )
        summed = lax.all_gather(piece, "dp", axis=0, tiled=True).reshape(dp_count, -1, D)
    blocks = summed[:, : 3 * run].reshape(dp_count, 3, run, D).swapaxes(0, 1).reshape(3, BLOCK, D)
    share_size = vectors.shape[0] * 2 // dp_count
    vector_sum = summed[:, 3 * run :].reshape(dp_count, -1)
    start = z * share_size if by_hand() else 0
    vector_sum = lax.dynamic_slice_in_dim(vector_sum, start, share_size, 1)
    vector_sum = vector_sum.reshape(2, -1).astype(F32)
    vector_sum = jnp.pad(vector_sum, ((0, 0), (0, 2 * D - vector_sum.shape[1])))
    shard_v = vector_sum[core] + swap(vector_sum[1 - core])
    shard_v = shard_v[: vectors.shape[0]]
    a, b, c = blocks
    middle = swap(jnp.where(core == 0, c, a))
    top = jnp.concatenate([jnp.where(core == 0, a, b), middle], axis=0)
    top = jnp.where(is_out_projection(z, core), top.T, top)
    shard_w = jnp.concatenate([top, jnp.where(core == 0, b, c)], axis=0).astype(F32)

    weight_change, new_first_weights, new_second_weights = adamw_update(
        weights, shard_w, first_weights, second_weights, 0.01
    )
    vector_change, new_first_vectors, new_second_vectors = adamw_update(
        vectors, shard_v, first_vectors, second_vectors, 0.0
    )
    return (
        layer_out,
        grad_tokens,
        shard_w,
        shard_v,
        weight_change,
        vector_change,
        new_first_weights,
        new_second_weights,
        new_first_vectors,
        new_second_vectors,
    )


def solution(mesh):
    chips = Mesh(
        mesh.devices.reshape(mesh.shape["dp"], mesh.shape["ctx"] // 2, 2), ("dp", "z", "core")
    )
    ctx = ("z", "core")
    activations, matrix, vector = P("dp", ctx, None), P(ctx, None), P(ctx)
    return jax.shard_map(
        shards,
        mesh=chips,
        in_specs=(activations, activations, P("dp"), matrix, vector, matrix, matrix, vector, vector),
        out_specs=(
            activations,
            activations,
            matrix,
            vector,
            matrix,
            vector,
            matrix,
            matrix,
            vector,
            vector,
        ),
        check_vma=False,
    )
```

time: 812 us -> 575 us (0.71)
  matrix products: 159 us -> 17.1 us
  Pallas kernels: 0 us -> 98.7 us
  other arithmetic: 139 us -> 60.9 us
  waiting for transfers between devices: 363 us -> 303 us
  blocking collectives: 44.9 us -> 0 us
    reduce_scatter x1 -> x2, waiting for transfers between devices: 206 us -> 52.7 us  [the longest x1 52.7 us: shards(): lax.psum_scatter(jnp.concatenate(chips, axis=0), 'z', scatter_dimension=0...]
    pallas_call x0 -> x5, Pallas kernels: none -> 98.7 us  [the longest x1 31 us: attention_backward(): pl.pallas_call(backward_kernel, grid=(HALF // PAIR, rows // step), in_spe...]
    dot_general x6 -> x0, matrix products: 86.2 us -> none  [the longest x1 22.3 us: attention_backward(): jnp.einsum('qhd,khd->hqk', grad_out, values, preferred_element_type=F32)]
    ppermute x5 -> x8, waiting for transfers between devices: 4.71 us -> 59.1 us  [across(): return lax.ppermute(value, 'dp', [(i, i ^ bit) for i in range(4)])]
    all_gather x1 -> x0, blocking collectives: 44.9 us -> none  [shards(): lax.all_gather(vectors.astype(BF), ('z', 'core'), axis=0, tiled=True)]
    concatenate x2 -> x5, other arithmetic: 35.6 us -> 4.83 us  [the longest x2 3.11 us: both(): return jnp.concatenate([rows, swap(rows)], axis=0)]
    convert_element_type x6 -> x9, other arithmetic: 37.5 us -> 10.9 us  [the longest x4 5.22 us: plus(): return (first.astype(F32) + second.astype(F32)).astype(BF)]
    dot_general x5 -> x1, matrix products: 28.2 us -> 3.86 us  [rows_dot(): lax.dot_general(operand, matrix, (((1,), (1,)), ((), ())), preferred_elem...]
  transfers between devices with their start and end apart: 30 -> 34, of which waited for: 15 -> 22; matrix products, arithmetic and copies ran while one was open for 8% -> 9% of each run, Pallas kernels for 0% -> 9%
where the time goes in v2:
time: 575 us; the launch traced here: 570 us
  waiting for transfers between devices  303 us (53%)
  Pallas kernels  98.7 us (17%)
  other arithmetic  60.9 us (11%)
  local copies, waits for them, and re-layouts  45.2 us (8%)
  starting transfers between devices  30.2 us (5%)
  matrix products  17.1 us (3%)
  between operations  15.1 us (3%)
    all_gather x1, waiting for transfers between devices, gather_weights(): whole = lax.all_gather(piece, ('z', 'dp'), axis=0, tiled=True)  134 us
    ppermute x8, waiting for transfers between devices, across(): return lax.ppermute(value, 'dp', [(i, i ^ bit) for i in range(4)])  59.1 us
    reduce_scatter x1, waiting for transfers between devices, shards(): lax.psum_scatter(jnp.concatenate(chips, axis=0), 'z', scatter_dimension=0...  52.7 us
    pallas_call x1, Pallas kernels, attention_backward(): pl.pallas_call(backward_kernel, grid=(HALF // PAIR, rows // step), in_spe...  31 us
    ppermute x6, waiting for transfers between devices, to_chips(): lax.ppermute(part, 'z', [(i, (i + shift) % count) for i in range(count)])  27.1 us
    pallas_call x1, Pallas kernels, feed_backward(): pl.pallas_call(feed_backward_kernel, grid=(QUARTERS,), in_specs=[whole_bl...  26.7 us
    ppermute x11, waiting for transfers between devices, swap(): return lax.ppermute(value, 'core', [(0, 1), (1, 0)])  19.9 us
    pallas_call x1, Pallas kernels, feed_forward(): pl.pallas_call(feed_forward_kernel, grid=(QUARTERS,), in_specs=[SCALAR, w...  18.1 us
  transfers between devices with their start and end apart: 34, of which 22 were waited for; matrix products, arithmetic and copies ran while one was open for 9% of the time, Pallas kernels for 9%

profile of v2, /device:TPU:0, one launch (start us, length us, event | category | flops | bytes accessed | tf_op | source)
XLA Modules:
  0.0 570.1 jit_solution(7324292200739429623)
XLA Ops:
  8.0 3.3 convert_element_type.184
  12.7 3.9 copy.22
  25.8 4.5 collective-permute-start.1
  32.8 5.5 collective-permute-done.1
  38.2 21.6 %collective-permute-done.2 = bf16[128,1024]{1,0:T(8,128)(2,1)} collective-permute-done((bf16[128,1024]{1,0:T(8,128)(2,1)}, bf16[128,1024]{1,0:T(8,128)(2,1)}, u32[]{:S(2)}, u32[]{:S(2)}) %collective-permute-start.2) | collective-permute-done | bytes 262176 | tf_op jit(solution)/shard_map/ppermute | solution.py:68
  65.9 134.2 %all-gather.2.cloned.1.call-done = bf16[6400,1024]{1,0:T(8,128)(2,1)} async-done(((bf16[400,1024]{1,0:T(8,128)(2,1)}), bf16[6400,1024]{1,0:T(8,128)(2,1)}) %all-gather.2.cloned.1.call-update) | async-done | bytes 13107216 | tf_op jit(solution)/shard_map/all_gather | solution.py:112
  208.7 6.5 %shard_map.168.q_ref.k_ref.v_ref = bf16[1024,1536]{1,0:T(8,128)(2,1)S(1)} custom-call(s32[1]{0:T(128)} %bitcast.core_ref, bf16[1024,1024]{1,0:T(8,128)(2,1)S(1)} %copy-done.2, bf16[16,400,1024]{2,1,0:T(8,128)(2,1)} %bitcast.151, f32[96,128]{1,0:T(8,128)S(1)} %reshape.334.vector_ref), custom_call_target="tpu_custom_call" | custom-call | flops 1 | bytes 1 | tf_op jit(solution)/shard_map/pallas_call | solution.py:218
  215.2 16.2 %shard_map.169 = (bf16[1024,512]{1,0:T(8,128)(2,1)S(1)}, bf16[1024,512]{1,0:T(8,128)(2,1)S(1)}) custom-call(bf16[1024,1536]{1,0:T(8,128)(2,1)S(1)} %shard_map.168.q_ref.k_ref.v_ref, bf16[1024,1536]{1,0:T(8,128)(2,1)S(1)} %shard_map.168.q_ref.k_ref.v_ref, bf16[1024,1536]{1,0:T(8,128)(2,1)S(1)} %shard_map.168.q_ref.k_ref.v_ref, ...), custom_call_target="tpu_custom_call" | custom-call | flops 1 | bytes 1 | tf_op jit(solution)/shard_map/pallas_call | solution.py:263
  238.4 2.6 collective-permute-done.8
  242.0 2.7 fusion.39
  245.7 2.5 collective-permute-done.9
  249.7 18.1 %shard_map.170 = (bf16[1024,2048]{1,0:T(8,128)(2,1)}, bf16[1024,2048]{1,0:T(8,128)(2,1)}, f32[512,1024]{1,0:T(8,128)}, bf16[512,1024]{1,0:T(8,128)(2,1)}) custom-call(s32[1]{0:T(128)} %bitcast.core_ref, bf16[1024,1024]{1,0:T(8,128)(2,1)} %pad_maximum_fusion.1.u_ref, bf16[16,400,1024]{2,1,0:T(8,128)(2,1)} %bitcast.153, bf16[16,400,1024]{2,1,0:T(8,128)(2,1)} %bitcast.154, ...), custom_call_target="tpu_custom_call" | custom-call | flops 1 | bytes 1 | tf_op jit(solution)/shard_map/pallas_call | solution.py:393
  276.6 2.5 collective-permute-done.11
  280.8 26.7 %shard_map.171 = (bf16[4,1024,1024]{2,1,0:T(8,128)(2,1)}, f32[1,2048]{1,0:T(1,128)}, f32[512,1024]{1,0:T(8,128)}, bf16[512,1024]{1,0:T(8,128)(2,1)}) custom-call(bf16[1024,1024]{1,0:T(8,128)(2,1)} %pad_maximum_fusion.2.df_ref, bf16[1024,1024]{1,0:T(8,128)(2,1)} %pad_maximum_fusion.1.u_ref, bf16[1024,2048]{1,0:T(8,128)(2,1)} %get-tuple-element.60.hidden_ref, ...), custom_call_target="tpu_custom_call" | custom-call | flops 1 | bytes 1 | tf_op jit(solution)/shard_map/pallas_call | solution.py:442
  307.8 2.7 collective-permute-done.12
  310.5 3.9 multiply_reduce_fusion.1
  319.7 3.9 convolution_convert_fusion.2.do_ref
  327.2 3.0 convolution_convert_fusion.1
  331.9 31.0 %shard_map.172 = bf16[1024,1536]{1,0:T(8,128)(2,1)} custom-call(bf16[1024,1536]{1,0:T(8,128)(2,1)} %copy-done, bf16[1024,512]{1,0:T(8,128)(2,1)} %copy-done.7, bf16[1024,1536]{1,0:T(8,128)(2,1)} %copy-done, bf16[1024,1536]{1,0:T(8,128)(2,1)} %copy-done, bf16[1024,128]{1,0:T(8,128)(2,1)} %copy-done.4, bf16[1024,512]{1,0:T(8,128)(2,1)} %copy-done.5, ...), custom_call_target="tpu_custom_call" | custom-call | flops 1 | bytes 1 | tf_op jit(solution)/shard_map/pallas_call | solution.py:325
  365.1 2.8 convert_reduce_fusion
  368.2 5.6 convolution_convert_fusion
  377.5 36.8 %collective-permute-done.17 = bf16[2,528,512]{2,1,0:T(8,128)(2,1)} collective-permute-done((bf16[2,528,512]{2,1,0:T(8,128)(2,1)S(1)}, bf16[2,528,512]{2,1,0:T(8,128)(2,1)}, u32[]{:S(2)}, u32[]{:S(2)}) %collective-permute-start.17) | collective-permute-done | bytes 1081376 | tf_op jit(solution)/shard_map/ppermute | solution.py:140
  419.4 10.2 %collective-permute-done.19 = bf16[528,512]{1,0:T(8,128)(2,1)S(1)} collective-permute-done((bf16[528,512]{1,0:T(8,128)(2,1)S(1)}, bf16[528,512]{1,0:T(8,128)(2,1)S(1)}, u32[]{:S(2)}, u32[]{:S(2)}) %collective-permute-start.19) | collective-permute-done | bytes 540704 | tf_op jit(solution)/shard_map/ppermute | solution.py:140
  441.0 3.4 fusion.47
  444.7 2.6 collective-permute-done.21
  448.0 52.7 %reduce-scatter.5.cloned.1.call-done = bf16[400,1024]{1,0:T(8,128)(2,1)} async-done(((bf16[1600,1024]{1,0:T(8,128)(2,1)}), bf16[400,1024]{1,0:T(8,128)(2,1)}) %reduce-scatter.5.cloned.1.call-update) | async-done | bytes 819216 | tf_op jit(solution)/shard_map/reduce_scatter | solution.py:600
  511.5 3.9 collective-permute-done.26
  516.4 5.4 collective-permute-done.22
  525.2 6.0 %collective-permute-done.27 = bf16[128,1024]{1,0:T(8,128)(2,1)S(1)} collective-permute-done((bf16[128,1024]{1,0:T(8,128)(2,1)S(1)}, bf16[128,1024]{1,0:T(8,128)(2,1)S(1)}, u32[]{:S(2)}, u32[]{:S(2)}) %collective-permute-start.27) | collective-permute-done | bytes 262176 | tf_op jit(solution)/shard_map/ppermute | solution.py:80
  541.5 3.0 fusion.9
  544.5 2.9 copy.25
  549.8 13.5 %add_multiply_fusion = (f32[1536,1024]{1,0:T(8,128)}, f32[1536,1024]{1,0:T(8,128)}, f32[1536,1024]{1,0:T(8,128)}, f32[1536,1024]{1,0:T(8,128)}) fusion(f32[1536,1024]{1,0:T(8,128)} %param.12, f32[1536,1024]{1,0:T(8,128)} %param.14, f32[1536,1024]{1,0:T(8,128)} %param.15, bf16[512,1024]{1,0:T(8,128)(2,1)S(1)} %bitcast.170, ...), kind=kLoop, calls=%fused_computation.2 | loop fusion | flops 28311552 | bytes 47185920 | tf_op jit(solution)/shard_map/mul | solution.py:473
  (279 shorter events, 110.5 us)
Async XLA Ops:
  7.2 192.9 %all-gather.2.cloned.1.call-start = ((), (), s32[]{:S(2)}) async-start(), calls=%async_computation.2 | async-start | bytes 13926400 | tf_op jit(solution)/shard_map/all_gather | solution.py:112
  18.6 3.1 collective-permute-start
  24.8 389.5 %reduce-scatter.3.cloned.1.call-start = ((), (), s32[]{:S(2)}) async-start(), calls=%async_computation.3 | async-start | bytes 10485760 | tf_op jit(solution)/shard_map/reduce_scatter | solution.py:128
  25.8 12.4 %collective-permute-start.1 = (bf16[128,1024]{1,0:T(8,128)(2,1)}, bf16[128,1024]{1,0:T(8,128)(2,1)S(1)}, u32[]{:S(2)}, u32[]{:S(2)}) collective-permute-start(bf16[128,1024]{1,0:T(8,128)(2,1)} %get-tuple-element.133), channel_id=1, source_target_pairs={{0,2},{2,4},{4,6},{6,0},{1,3},{3,5},{5,7},{7,1},{8,10},{10,12},{12... | collective-permute-start | bytes 786440 | tf_op jit(solution)/shard_map/ppermute | solution.py:68
  30.4 29.5 %collective-permute-start.2 = (bf16[128,1024]{1,0:T(8,128)(2,1)}, bf16[128,1024]{1,0:T(8,128)(2,1)}, u32[]{:S(2)}, u32[]{:S(2)}) collective-permute-start(bf16[128,1024]{1,0:T(8,128)(2,1)} %get-tuple-element.134), channel_id=1, source_target_pairs={{0,4},{2,6},{4,0},{6,2},{1,5},{3,7},{5,1},{7,3},{8,12},{10,14},{12... | collective-permute-start | bytes 786440 | tf_op jit(solution)/shard_map/ppermute | solution.py:68
  31.4 28.5 %collective-permute-start.3 = (bf16[128,1024]{1,0:T(8,128)(2,1)}, bf16[128,1024]{1,0:T(8,128)(2,1)}, u32[]{:S(2)}, u32[]{:S(2)}) collective-permute-start(bf16[128,1024]{1,0:T(8,128)(2,1)} %get-tuple-element.132), channel_id=1, source_target_pairs={{0,6},{2,0},{4,2},{6,4},{1,7},{3,1},{5,3},{7,5},{8,14},{10,8},{12,... | collective-permute-start | bytes 786440 | tf_op jit(solution)/shard_map/ppermute | solution.py:68
  60.9 3.6 collective-permute-start.4
  202.2 31.4 %collective-permute-start.7 = (bf16[128,1024]{1,0:T(8,128)(2,1)}, bf16[128,1024]{1,0:T(8,128)(2,1)S(1)}, u32[]{:S(2)}, u32[]{:S(2)}) collective-permute-start(bf16[128,1024]{1,0:T(8,128)(2,1)} %get-tuple-element.129), channel_id=1, source_target_pairs={{0,6},{2,0},{4,2},{6,4},{1,7},{3,1},{5,3},{7,5},{8,14},{10,8},{12,... | collective-permute-start | bytes 786440 | tf_op jit(solution)/shard_map/ppermute | solution.py:68
  203.6 30.0 %collective-permute-start.6 = (bf16[128,1024]{1,0:T(8,128)(2,1)}, bf16[128,1024]{1,0:T(8,128)(2,1)S(1)}, u32[]{:S(2)}, u32[]{:S(2)}) collective-permute-start(bf16[128,1024]{1,0:T(8,128)(2,1)} %get-tuple-element.130), channel_id=1, source_target_pairs={{0,4},{2,6},{4,0},{6,2},{1,5},{3,7},{5,1},{7,3},{8,12},{10,14},{12... | collective-permute-start | bytes 786440 | tf_op jit(solution)/shard_map/ppermute | solution.py:68
  203.7 29.9 %collective-permute-start.5 = (bf16[128,1024]{1,0:T(8,128)(2,1)}, bf16[128,1024]{1,0:T(8,128)(2,1)}, u32[]{:S(2)}, u32[]{:S(2)}) collective-permute-start(bf16[128,1024]{1,0:T(8,128)(2,1)} %get-tuple-element.131), channel_id=1, source_target_pairs={{0,2},{2,4},{4,6},{6,0},{1,3},{3,5},{5,7},{7,1},{8,10},{10,12},{12... | collective-permute-start | bytes 786440 | tf_op jit(solution)/shard_map/ppermute | solution.py:68
  238.3 2.7 collective-permute-start.8
  245.4 2.7 collective-permute-start.9
  267.8 2.9 collective-permute-start.10
  276.4 2.7 collective-permute-start.11
  307.5 193.1 %reduce-scatter.5.cloned.1.call-start = ((), (), s32[]{:S(2)}) async-start(), calls=%async_computation.4 | async-start | bytes 4096000 | tf_op jit(solution)/shard_map/reduce_scatter | solution.py:600
  307.6 2.9 collective-permute-start.12
  316.8 2.9 collective-permute-start.13
  323.6 39.3 %collective-permute-start.14 = (bf16[128,1024]{1,0:T(8,128)(2,1)S(1)}, bf16[128,1024]{1,0:T(8,128)(2,1)S(1)}, u32[]{:S(2)}, u32[]{:S(2)}) collective-permute-start(bf16[128,1024]{1,0:T(8,128)(2,1)S(1)} %get-tuple-element.127), channel_id=1, source_target_pairs={{0,6},{2,0},{4,2},{6,4},{1,7},{3,1},{5,3},{7,5},{8,14},{10,8},{12,... | collective-permute-start | bytes 786440 | tf_op jit(solution)/shard_map/ppermute | solution.py:80
  325.7 38.0 %collective-permute-start.15 = (bf16[128,1024]{1,0:T(8,128)(2,1)S(1)}, bf16[128,1024]{1,0:T(8,128)(2,1)S(1)}, u32[]{:S(2)}, u32[]{:S(2)}) collective-permute-start(bf16[128,1024]{1,0:T(8,128)(2,1)S(1)} %get-tuple-element.126), channel_id=1, source_target_pairs={{0,4},{2,6},{4,0},{6,2},{1,5},{3,7},{5,1},{7,3},{8,12},{10,14},{12... | collective-permute-start | bytes 786440 | tf_op jit(solution)/shard_map/ppermute | solution.py:80
  326.5 37.9 %collective-permute-start.16 = (bf16[128,1024]{1,0:T(8,128)(2,1)S(1)}, bf16[128,1024]{1,0:T(8,128)(2,1)S(1)}, u32[]{:S(2)}, u32[]{:S(2)}) collective-permute-start(bf16[128,1024]{1,0:T(8,128)(2,1)S(1)} %get-tuple-element.125), channel_id=1, source_target_pairs={{0,2},{2,4},{4,6},{6,0},{1,3},{3,5},{5,7},{7,1},{8,10},{10,12},{12... | collective-permute-start | bytes 786440 | tf_op jit(solution)/shard_map/ppermute | solution.py:80
  374.7 39.7 %collective-permute-start.17 = (bf16[2,528,512]{2,1,0:T(8,128)(2,1)S(1)}, bf16[2,528,512]{2,1,0:T(8,128)(2,1)}, u32[]{:S(2)}, u32[]{:S(2)}) collective-permute-start(bf16[2,528,512]{2,1,0:T(8,128)(2,1)S(1)} %dynamic-slice_bitcast_fusion.3), channel_id=1, source_target_pairs={{0,8},{8,0},{16,24},{24,16},{1,9},{9,1},{17,25},{25,17},{2,10},{10... | collective-permute-start | bytes 3244040 | tf_op jit(solution)/shard_map/ppermute | solution.py:140
  376.7 37.6 %collective-permute-start.18 = (bf16[2,528,512]{2,1,0:T(8,128)(2,1)}, bf16[2,528,512]{2,1,0:T(8,128)(2,1)}, u32[]{:S(2)}, u32[]{:S(2)}) collective-permute-start(bf16[2,528,512]{2,1,0:T(8,128)(2,1)} %dynamic-slice_bitcast_fusion.2), channel_id=1, source_target_pairs={{0,16},{8,24},{16,0},{24,8},{1,17},{9,25},{17,1},{25,9},{2,18},{10... | collective-permute-start | bytes 3244040 | tf_op jit(solution)/shard_map/ppermute | solution.py:140
  415.9 13.7 %collective-permute-start.19 = (bf16[528,512]{1,0:T(8,128)(2,1)S(1)}, bf16[528,512]{1,0:T(8,128)(2,1)S(1)}, u32[]{:S(2)}, u32[]{:S(2)}) collective-permute-start(bf16[528,512]{1,0:T(8,128)(2,1)S(1)} %fusion.13), channel_id=1, source_target_pairs={{0,16},{8,24},{16,0},{24,8},{1,17},{9,25},{17,1},{25,9},{2,18},{10... | collective-permute-start | bytes 1622024 | tf_op jit(solution)/shard_map/ppermute | solution.py:140
  418.6 13.5 %collective-permute-start.20 = (bf16[528,512]{1,0:T(8,128)(2,1)S(1)}, bf16[528,512]{1,0:T(8,128)(2,1)S(1)}, u32[]{:S(2)}, u32[]{:S(2)}) collective-permute-start(bf16[528,512]{1,0:T(8,128)(2,1)S(1)} %fusion.12), channel_id=1, source_target_pairs={{0,8},{8,0},{16,24},{24,16},{1,9},{9,1},{17,25},{25,17},{2,10},{10... | collective-permute-start | bytes 1622024 | tf_op jit(solution)/shard_map/ppermute | solution.py:140
  501.9 19.9 %collective-permute-start.22 = (bf16[2,400,512]{2,1,0:T(8,128)(2,1)S(1)}, bf16[2,400,512]{2,1,0:T(8,128)(2,1)S(1)}, u32[]{:S(2)}, u32[]{:S(2)}) collective-permute-start(bf16[2,400,512]{2,1,0:T(8,128)(2,1)S(1)} %pad_maximum_fusion.10), channel_id=1, source_target_pairs={{0,8},{8,0},{16,24},{24,16},{1,9},{9,1},{17,25},{25,17},{2,10},{10... | collective-permute-start | bytes 2457608 | tf_op jit(solution)/shard_map/ppermute | solution.py:140
  503.4 19.5 %collective-permute-start.23 = (bf16[2,400,512]{2,1,0:T(8,128)(2,1)S(1)}, bf16[2,400,512]{2,1,0:T(8,128)(2,1)S(1)}, u32[]{:S(2)}, u32[]{:S(2)}) collective-permute-start(bf16[2,400,512]{2,1,0:T(8,128)(2,1)S(1)} %pad_maximum_fusion.10), channel_id=1, source_target_pairs={{0,16},{8,24},{16,0},{24,8},{1,17},{9,25},{17,1},{25,9},{2,18},{10... | collective-permute-start | bytes 2457608 | tf_op jit(solution)/shard_map/ppermute | solution.py:140
  505.8 9.6 %collective-permute-start.26 = (bf16[128,1024]{1,0:T(8,128)(2,1)}, bf16[128,1024]{1,0:T(8,128)(2,1)}, u32[]{:S(2)}, u32[]{:S(2)}) collective-permute-start(bf16[128,1024]{1,0:T(8,128)(2,1)} %get-tuple-element.124), channel_id=1, source_target_pairs={{0,6},{2,0},{4,2},{6,4},{1,7},{3,1},{5,3},{7,5},{8,14},{10,8},{12,... | collective-permute-start | bytes 786440 | tf_op jit(solution)/shard_map/ppermute | solution.py:80
  509.2 22.0 %collective-permute-start.27 = (bf16[128,1024]{1,0:T(8,128)(2,1)S(1)}, bf16[128,1024]{1,0:T(8,128)(2,1)S(1)}, u32[]{:S(2)}, u32[]{:S(2)}) collective-permute-start(bf16[128,1024]{1,0:T(8,128)(2,1)S(1)} %copy-done.34), channel_id=1, source_target_pairs={{0,4},{2,6},{4,0},{6,2},{1,5},{3,7},{5,1},{7,3},{8,12},{10,14},{12... | collective-permute-start | bytes 786440 | tf_op jit(solution)/shard_map/ppermute | solution.py:80
  509.3 21.9 %collective-permute-start.28 = (bf16[128,1024]{1,0:T(8,128)(2,1)S(1)}, bf16[128,1024]{1,0:T(8,128)(2,1)S(1)}, u32[]{:S(2)}, u32[]{:S(2)}) collective-permute-start(bf16[128,1024]{1,0:T(8,128)(2,1)S(1)} %copy-done.33), channel_id=1, source_target_pairs={{0,2},{2,4},{4,6},{6,0},{1,3},{3,5},{5,7},{7,1},{8,10},{10,12},{12... | collective-permute-start | bytes 786440 | tf_op jit(solution)/shard_map/ppermute | solution.py:80
  523.0 9.9 %collective-permute-start.24 = (bf16[400,512]{1,0:T(8,128)(2,1)S(1)}, bf16[400,512]{1,0:T(8,128)(2,1)S(1)}, u32[]{:S(2)}, u32[]{:S(2)}) collective-permute-start(bf16[400,512]{1,0:T(8,128)(2,1)S(1)} %slice_bitcast_fusion.4), channel_id=1, source_target_pairs={{0,16},{8,24},{16,0},{24,8},{1,17},{9,25},{17,1},{25,9},{2,18},{10... | collective-permute-start | bytes 1228808 | tf_op jit(solution)/shard_map/ppermute | solution.py:140
  524.6 9.6 %collective-permute-start.25 = (bf16[400,512]{1,0:T(8,128)(2,1)S(1)}, bf16[400,512]{1,0:T(8,128)(2,1)S(1)}, u32[]{:S(2)}, u32[]{:S(2)}) collective-permute-start(bf16[400,512]{1,0:T(8,128)(2,1)S(1)} %slice_bitcast_fusion.3), channel_id=1, source_target_pairs={{0,8},{8,0},{16,24},{24,16},{1,9},{9,1},{17,25},{25,17},{2,10},{10... | collective-permute-start | bytes 1228808 | tf_op jit(solution)/shard_map/ppermute | solution.py:140
  538.2 3.3 collective-permute-start.29
  (43 other events, 493.5 us)
Sparse Core Ops, SparseCore 0:
  24.9 175.1 all-gather.1
  307.7 99.2 reduce-scatter.2
  438.3 62.2 reduce-scatter.4

commit v3 on v2

--- a/solution.py
+++ b/solution.py
@@ -22,7 +22,9 @@
 EXTRA = 16
 QUARTERS = 4
 PIECE = 3 * PAIR + EXTRA
-MIB = 2**20
+VMEM = 60 * 2**20
+SCALAR = pl.BlockSpec(memory_space=pltpu.SMEM)
+NO_COST = pl.CostEstimate(flops=1, bytes_accessed=1, transcendentals=0)
 
 
 def rows_dot(operand, matrix):
@@ -59,15 +61,16 @@
     return (inverse * inner_term, jnp.sum(grad_out * normed, axis=0), jnp.sum(grad_out, axis=0))
 
 
+def to_chip(blocks, z, shift):
+    count = lax.axis_size("z")
+    part = lax.dynamic_index_in_dim(blocks, (z + shift) % count, 0, keepdims=False)
+    if shift:
+        part = lax.ppermute(part, "z", [(i, (i + shift) % count) for i in range(count)])
+    return part
+
+
 def to_chips(blocks, z):
-    count = lax.axis_size("z")
-    parts = []
-    for shift in range(count):
-        part = lax.dynamic_index_in_dim(blocks, (z + shift) % count, 0, keepdims=False)
-        if shift:
-            part = lax.ppermute(part, "z", [(i, (i + shift) % count) for i in range(count)])
-        parts.append(part)
-    return jnp.concatenate(parts, axis=0)
+    return jnp.concatenate([to_chip(blocks, z, n) for n in range(lax.axis_size("z"))], axis=0)
 
 
 def from_chips(rows, z):
@@ -86,39 +89,162 @@
     return jnp.logical_and(z == 1, core == 0)
 
 
-def gather_weights(weights, vectors, z, core):
-    count = lax.axis_size("dp")
-    rows = BLOCK // count
-    low = weights.astype(BF)
-    top = jnp.where(is_out_projection(z, core), low[:D].T, low[:D])
-    vector = jnp.pad(vectors.astype(BF), (0, 2 * D - vectors.shape[0])).reshape(2, D)
-    vector = jnp.pad(vector, ((0, EXTRA - 2), (0, 0)))
-    other = swap(jnp.concatenate([top[BLOCK:], vector], axis=0))
-    pair = jnp.stack([vector, other[BLOCK:]])
-    pair = jnp.where(core == 0, pair, pair[::-1]).reshape(2, -1)[:, : vectors.shape[0]]
-    pair = jnp.pad(pair.reshape(-1, D), ((0, EXTRA - 3), (0, 0)))
-    start = lax.axis_index("dp") * rows
-    if count > QUARTERS:
-        spare = EXTRA * QUARTERS // count
-        pair = lax.dynamic_slice_in_dim(pair, (start % PAIR) // rows * spare, spare, 0)
-    first, last, middle = (
-        lax.dynamic_slice_in_dim(item, start, rows, 0) for item in (top, low[D:], other)
-    )
-    piece = jnp.where(
-        core == 0,
-        jnp.concatenate([first, last, middle, pair], axis=0),
-        jnp.concatenate([middle, first, last, pair], axis=0),
-    )
-    whole = lax.all_gather(piece, ("z", "dp"), axis=0, tiled=True)
-    if count == QUARTERS:
-        whole = whole.reshape(-1, PIECE, D)
-    else:
-        whole = whole.reshape(-1, count // QUARTERS, piece.shape[0], D)
-        blocks = whole[:, :, : 3 * rows].reshape(-1, count // QUARTERS, 3, rows, D).swapaxes(1, 2)
-        spare = whole[:, :, 3 * rows :].reshape(-1, EXTRA, D)
-        whole = jnp.concatenate([blocks.reshape(-1, 3 * PAIR, D), spare], axis=1)
-    found = whole.reshape(-1, QUARTERS, PIECE, D)[:, 0, 3 * PAIR : 3 * PAIR + 3]
-    return whole, found.reshape(-1).astype(F32)
+def pack_kernel(flag_ref, rows_ref, columns_ref, outer_ref, middle_ref):
+    step = pl.program_id(0)
+    turned = jnp.logical_and(flag_ref[0] == 1, step < 2)
+
+    def write(value):
+        @pl.when(step != 1)
+        def _():
+            outer_ref[...] = value
+
+        @pl.when(step == 1)
+        def _():
+            middle_ref[...] = value
+
+    @pl.when(turned)
+    def _():
+        write(columns_ref[...].T.astype(BF))
+
+    @pl.when(jnp.logical_not(turned))
+    def _():
+        write(rows_ref[...].astype(BF))
+
+
+def pack_weights(weights, flag):
+    return pl.pallas_call(
+        pack_kernel,
+        grid_spec=pltpu.PrefetchScalarGridSpec(
+            num_scalar_prefetch=1,
+            grid=(3,),
+            in_specs=[
+                pl.BlockSpec((BLOCK, D), lambda n, flag: (n, 0)),
+                pl.BlockSpec((D, BLOCK), lambda n, flag: (0, jnp.minimum(n, 1) * flag[0])),
+            ],
+            out_specs=[
+                pl.BlockSpec((BLOCK, D), lambda n, flag: (n // 2, 0)),
+                pl.BlockSpec((BLOCK, D), lambda n, flag: (0, 0)),
+            ],
+        ),
+        out_shape=[
+            jax.ShapeDtypeStruct((2 * BLOCK, D), BF),
+            jax.ShapeDtypeStruct((BLOCK, D), BF),
+        ],
+        cost_estimate=NO_COST,
+        compiler_params=pltpu.CompilerParams(vmem_limit_bytes=VMEM),
+    )(flag.astype(jnp.int32).reshape(1), weights, weights)
+
+
+def own_kernel(
+    where_ref, first_ref, last_ref, other_ref, mine_vector, other_vector, whole_ref, piece_ref
+):
+    core = where_ref[2]
+
+    def write(parts, vectors):
+        value = jnp.concatenate([*parts, *vectors], axis=0)
+        whole_ref[0] = value
+
+        @pl.when(pl.program_id(0) == 0)
+        def _():
+            piece_ref[...] = value
+
+    first, last, other = first_ref[...], last_ref[...], other_ref[...]
+    vectors = [mine_vector[...], other_vector[...]]
+
+    @pl.when(core == 0)
+    def _():
+        write([first, last, other], vectors)
+
+    @pl.when(core == 1)
+    def _():
+        write([other, first, last], vectors[::-1])
+
+
+def own_pieces(outer, other, vector, other_vector, z, core):
+    where = jnp.stack([z, lax.axis_index("dp") % QUARTERS, core]).astype(jnp.int32)
+    run = (PAIR, D)
+    small = pl.BlockSpec(vector.shape, lambda n, where: (0, 0))
+    return pl.pallas_call(
+        own_kernel,
+        grid_spec=pltpu.PrefetchScalarGridSpec(
+            num_scalar_prefetch=1,
+            grid=(QUARTERS,),
+            in_specs=[
+                pl.BlockSpec(run, lambda n, where: (where[1] ^ n, 0)),
+                pl.BlockSpec(run, lambda n, where: (QUARTERS + (where[1] ^ n), 0)),
+                pl.BlockSpec(run, lambda n, where: (where[1] ^ n, 0)),
+                small,
+                small,
+            ],
+            out_specs=[
+                pl.BlockSpec(
+                    (1, PIECE, D), lambda n, where: (where[0] * QUARTERS + (where[1] ^ n), 0, 0)
+                ),
+                pl.BlockSpec((PIECE, D), lambda n, where: (0, 0)),
+            ],
+        ),
+        out_shape=[
+            jax.ShapeDtypeStruct((4 * QUARTERS, PIECE, D), BF),
+            jax.ShapeDtypeStruct((PIECE, D), BF),
+        ],
+        cost_estimate=NO_COST,
+        compiler_params=pltpu.CompilerParams(vmem_limit_bytes=VMEM),
+    )(where, outer, outer, other, vector, other_vector)
+
+
+def gather_pieces_of_all(whole, z):
+    count = lax.axis_size("dp") // QUARTERS
+    mine = lax.dynamic_slice_in_dim(whole, z * QUARTERS, QUARTERS, 0)
+    share = lax.dynamic_index_in_dim(mine, lax.axis_index("dp") // count, 0, keepdims=False)
+    blocks = share[: 3 * PAIR].reshape(3, PAIR, D)
+    blocks = lax.dynamic_slice_in_dim(
+        blocks, lax.axis_index("dp") % count * (PAIR // count), PAIR // count, 1
+    )
+    everything = lax.all_gather(blocks.reshape(-1, D), ("z", "dp"), axis=0, tiled=True)
+    everything = everything.reshape(-1, count, 3, PAIR // count, D).swapaxes(1, 2)
+    spare = lax.all_gather(share[3 * PAIR :], "z", axis=0, tiled=True).reshape(-1, 1, EXTRA, D)
+    spare = jnp.broadcast_to(spare, (spare.shape[0], QUARTERS, EXTRA, D)).reshape(-1, EXTRA, D)
+    return jnp.concatenate([everything.reshape(-1, 3 * PAIR, D), spare], axis=1)
+
+
+def vectors_of(whole, size):
+    found = whole.reshape(-1, QUARTERS, PIECE, D)[:, 0, 3 * PAIR :]
+    found = found.reshape(-1, 2, EXTRA * D // 2)[:, :, :size]
+    return found.reshape(-1).astype(F32)
+
+
+def place_kernel(where_ref, whole_in, mine, got_x, got_y, far_a, far_b, whole_ref):
+    del where_ref, whole_in
+    for index, source in enumerate((mine, got_x, got_y)):
+
+        @pl.when(pl.program_id(0) == index)
+        def _(source=source):
+            whole_ref[0] = source[...]
+
+    @pl.when(pl.program_id(0) == 3)
+    def _():
+        whole_ref[0, :, :HALF] = far_a[...]
+        whole_ref[0, :, HALF:] = far_b[...]
+
+
+def place(whole, shard, values):
+    where = jnp.stack([shard, lax.axis_index("dp")]).astype(jnp.int32)
+    return pl.pallas_call(
+        place_kernel,
+        grid_spec=pltpu.PrefetchScalarGridSpec(
+            num_scalar_prefetch=1,
+            grid=(4,),
+            in_specs=[pl.BlockSpec(memory_space=pl.ANY)]
+            + [pl.BlockSpec(value.shape, lambda n, where: (0, 0)) for value in values],
+            out_specs=pl.BlockSpec(
+                (1, PIECE, D), lambda n, where: (where[0] * QUARTERS + (where[1] ^ n), 0, 0)
+            ),
+        ),
+        out_shape=jax.ShapeDtypeStruct(whole.shape, BF),
+        input_output_aliases={1: 0},
+        cost_estimate=NO_COST,
+        compiler_params=pltpu.CompilerParams(vmem_limit_bytes=VMEM),
+    )(where, whole, *values)
 
 
 def sum_over_dp(grads):
@@ -144,38 +270,110 @@
     return lax.dynamic_index_in_dim(value, index, axis, keepdims=False)
 
 
-def reduce_late(late, sum_ff):
+def along_z(value, pairs):
+    return lax.ppermute(value, "z", pairs)
+
+
+def pick(z, values):
+    result = values[-1]
+    for index in range(len(values) - 2, -1, -1):
+        result = jnp.where(z == index, values[index], result)
+    return result
+
+
+def wait(*values):
+    return lax.optimization_barrier(values)
+
+
+def reduce_late(late, sum_ff, grad_tokens):
     d = lax.axis_index("dp")
     x, y = d % 2, d // 2
     late = late.reshape(2, 2, -1, D)
     a, b = late[..., :HALF], late[..., HALF:]
     got_a, got_b = across(1, at(a, 1 - x, 1)), across(2, at(b, 1 - y, 0))
-    got_a, got_b, a, b, sum_ff = lax.optimization_barrier((got_a, got_b, a, b, sum_ff))
+    got_a, got_b, a, b, sum_ff, grad_tokens = wait(got_a, got_b, a, b, sum_ff, grad_tokens)
     a, b = at(a, x, 1), at(b, y, 0)
     far_a = across(2, plus(at(a, 1 - y, 0), at(got_a, 1 - y, 0)))
     far_b = across(1, plus(at(b, 1 - x, 0), at(got_b, 1 - x, 0)))
     far_a, far_b, a, b = lax.optimization_barrier((far_a, far_b, a, b))
     a = plus(plus(at(a, y, 0), at(got_a, y, 0)), far_a)
     b = plus(plus(at(b, x, 0), at(got_b, x, 0)), far_b)
-    return jnp.concatenate([a, b], axis=-1), sum_ff
-
-
-def gather_pieces(piece, grad_tokens):
+    return jnp.concatenate([a, b], axis=-1), sum_ff, grad_tokens
+
+
+def gather_pieces(piece):
+    got = across(1, piece), across(2, piece)
+    got, piece = wait(got, piece)
+    far = across(2, got[0][:, :HALF]), across(1, got[1][:, HALF:])
+    far, got, piece = wait(far, got, piece)
+    return (piece, *got, *far)
+
+
+def update_kernel(
+    where_ref, mine, got_x, got_y, far_a, far_b, middle_ref, weight_ref, first_ref, second_ref,
+    grad_ref, change_ref, first_out, second_out,
+):
+    d, core, turned = where_ref[0], where_ref[1], where_ref[2] == 1
+    block, pair = pl.program_id(0), pl.program_id(1)
+    pieces = (mine, got_x, got_y)
+    rows = pl.ds(pl.multiple_of((core + block // 2) * PAIR, PAIR), PAIR)
+    plain = jnp.logical_and(block != 1, jnp.logical_or(block == 2, jnp.logical_not(turned)))
+    for n in range(QUARTERS):
+        slot = pl.ds(pl.multiple_of((d % 2 ^ (n % 2)) * PAIR, PAIR), PAIR)
+        ours = pair == n // 2
+
+        @pl.when(ours & (block == 1) & jnp.logical_not(turned))
+        def _(n=n, slot=slot):
+            grad_ref[slot, :] = middle_ref[n].astype(F32)
+
+        @pl.when(ours & plain)
+        def _(n=n, slot=slot):
+            if n < 3:
+                grad_ref[slot, :] = pieces[n][rows, :].astype(F32)
+            else:
+                grad_ref[slot, :HALF] = far_a[rows, :].astype(F32)
+                grad_ref[slot, HALF:] = far_b[rows, :].astype(F32)
+
+        @pl.when(ours & (block < 2) & turned)
+        def _(n=n, slot=slot):
+            start = pl.multiple_of((d ^ n) * PAIR, PAIR)
+            columns = pl.ds(pl.multiple_of(block * HALF + start, PAIR), PAIR)
+            for m in range(QUARTERS):
+                low = pl.ds(pl.multiple_of((d ^ m) * PAIR, PAIR), PAIR)
+                high = pl.ds(pl.multiple_of(HALF + (d ^ m) * PAIR, PAIR), PAIR)
+                grad_ref[slot, high] = middle_ref[m, :, columns].astype(F32).T
+                if m < 3:
+                    grad_ref[slot, low] = pieces[m][:PAIR, columns].astype(F32).T
+            low = pl.ds(pl.multiple_of((d ^ 3) * PAIR, PAIR), PAIR)
+            for half, far in enumerate((far_a, far_b)):
+
+                @pl.when(block == half)
+                def _(far=far):
+                    grad_ref[slot, low] = far[:PAIR, pl.ds(start, PAIR)].astype(F32).T
+
+    change_ref[...], first_out[...], second_out[...] = adamw_update(
+        weight_ref[...], grad_ref[...], first_ref[...], second_ref[...], 0.01
+    )
+
+
+def update_weights(values, middle, weights, first_weights, second_weights, turned, core):
     d = lax.axis_index("dp")
-    a, b = piece[:, :HALF], piece[:, HALF:]
-    pair = jnp.stack([a, b])
-    got_x, got_y = across(1, pair), across(2, pair)
-    got_x, got_y, pair = lax.optimization_barrier((got_x, got_y, pair))
-    far_a, far_b = across(2, got_x[0]), across(1, got_y[1])
-    far_a, far_b, pair, grad_tokens = lax.optimization_barrier((far_a, far_b, pair, grad_tokens))
-    result = jnp.zeros((4, *piece.shape), BF)
-    far = jnp.stack([far_a, far_b])
-    for index, value in enumerate((pair, got_x, got_y, far)):
-        for half in range(2):
-            result = lax.dynamic_update_slice(
-                result, value[half][None], (d ^ index, 0, half * HALF)
-            )
-    return result, grad_tokens
+    where = jnp.stack([d, core, turned.astype(jnp.int32)]).astype(jnp.int32)
+    rows = pl.BlockSpec((2 * PAIR, D), lambda b, n, where: (b * 2 + (where[0] // 2 ^ n), 0))
+    return pl.pallas_call(
+        update_kernel,
+        grid_spec=pltpu.PrefetchScalarGridSpec(
+            num_scalar_prefetch=1,
+            grid=(3, 2),
+            in_specs=[pl.BlockSpec(value.shape, lambda b, n, where: (0, 0)) for value in values]
+            + [pl.BlockSpec(middle.shape, lambda b, n, where: (0, 0, 0))]
+            + [rows] * 3,
+            out_specs=[rows] * 4,
+        ),
+        out_shape=[jax.ShapeDtypeStruct(weights.shape, F32)] * 4,
+        cost_estimate=NO_COST,
+        compiler_params=pltpu.CompilerParams(vmem_limit_bytes=VMEM),
+    )(where, *values, middle, weights, first_weights, second_weights)
 
 
 def lanes_of(shape, head):
@@ -198,10 +396,6 @@
 
 def whole_block(shape):
     return pl.BlockSpec(shape, lambda *_: (0,) * len(shape))
-
-
-SCALAR = pl.BlockSpec(memory_space=pltpu.SMEM)
-NO_COST = pl.CostEstimate(flops=1, bytes_accessed=1, transcendentals=0)
 
 
 def qkv_kernel(core_ref, x_ref, w_ref, vector_ref, out_ref):
@@ -227,7 +421,7 @@
         out_specs=pl.BlockSpec((rows, 3 * PAIR), lambda quarter: (0, quarter)),
         out_shape=jax.ShapeDtypeStruct((rows, 3 * HALF), BF),
         cost_estimate=NO_COST,
-        compiler_params=pltpu.CompilerParams(vmem_limit_bytes=40 * MIB),
+        compiler_params=pltpu.CompilerParams(vmem_limit_bytes=VMEM),
     )(core, x, whole, vec)
 
 
@@ -254,21 +448,28 @@
     extra_ref[...] = jnp.where(in_first, extras[1], extras[0]).astype(BF)
 
 
-def attention_forward(merged, key_extra, step):
+def forward_more_kernel(q_ref, k_ref, v_ref, key_ref, o_in, extra_in, o_ref, extra_ref):
+    del o_in, extra_in
+    forward_kernel(q_ref, k_ref, v_ref, key_ref, o_ref, extra_ref)
+
+
+def attention_forward(merged, key_extra, step, start, pairs, done=()):
     rows = merged.shape[0]
-    some = pl.BlockSpec((step, PAIR), lambda pair, part: (part, 3 * pair))
-    ours = pl.BlockSpec((step, PAIR), lambda pair, part: (part, pair))
-    keys = pl.BlockSpec((rows, PAIR), lambda pair, part: (0, 3 * pair + 1))
-    values = pl.BlockSpec((rows, PAIR), lambda pair, part: (0, 3 * pair + 2))
+    some = pl.BlockSpec((step, PAIR), lambda pair, part: (part, 3 * (pair + start)))
+    ours = pl.BlockSpec((step, PAIR), lambda pair, part: (part, pair + start))
+    keys = pl.BlockSpec((rows, PAIR), lambda pair, part: (0, 3 * (pair + start) + 1))
+    values = pl.BlockSpec((rows, PAIR), lambda pair, part: (0, 3 * (pair + start) + 2))
     return pl.pallas_call(
-        forward_kernel,
-        grid=(HALF // PAIR, rows // step),
-        in_specs=[some, keys, values, whole_block(key_extra.shape)],
+        forward_more_kernel if done else forward_kernel,
+        grid=(pairs, rows // step),
+        in_specs=[some, keys, values, whole_block(key_extra.shape)]
+        + [pl.BlockSpec(memory_space=pl.ANY)] * len(done),
         out_specs=[ours, ours],
         out_shape=[jax.ShapeDtypeStruct((rows, HALF), BF)] * 2,
+        input_output_aliases={4: 0, 5: 1} if done else {},
         cost_estimate=NO_COST,
-        compiler_params=pltpu.CompilerParams(vmem_limit_bytes=48 * MIB),
-    )(merged, merged, merged, key_extra)
+        compiler_params=pltpu.CompilerParams(vmem_limit_bytes=VMEM),
+    )(merged, merged, merged, key_extra, *done)
 
 
 def backward_kernel(
@@ -330,7 +531,7 @@
         out_shape=jax.ShapeDtypeStruct((rows, 3 * HALF), BF),
         scratch_shapes=[pltpu.VMEM((rows, PAIR), F32)] * 2,
         cost_estimate=NO_COST,
-        compiler_params=pltpu.CompilerParams(vmem_limit_bytes=56 * MIB),
+        compiler_params=pltpu.CompilerParams(vmem_limit_bytes=VMEM),
     )(merged, extra, merged, merged, key_extra, heads_out, grad_out)
 
 
@@ -355,7 +556,7 @@
 
 
 def feed_forward_kernel(
-    core_ref, u_ref, up0, up1, up2, down0, down1, vector_ref,
+    core_ref, u_mine, u_other, up0, up1, up2, down0, down1, vector_ref,
     hidden_ref, slope_ref, mine_ref, other_ref, total,
 ):
     quarter = pl.program_id(0)
@@ -363,37 +564,43 @@
         vector_ref[pl.ds(3 * D // PAIR + (2 * n + core_ref[0]) * QUARTERS + quarter, 1), :]
         for n in range(4)
     ]
-    z = rows_dot(u_ref[...], joined((up0, up1, up2))) + jnp.concatenate(rows, axis=1)
-    cdf = 0.5 * (1.0 + lax.erf(z * (1.0 / math.sqrt(2.0))))
-    slope = cdf + z * jnp.exp(-0.5 * z * z) * (1.0 / math.sqrt(2.0 * math.pi))
-    hidden = (z * cdf).astype(BF)
-    hidden_ref[...] = hidden
-    slope_ref[...] = slope.astype(BF)
-    part = plain_dot(hidden, joined((down0, down1)))
-
-    @pl.when(quarter == 0)
-    def _():
-        total[...] = part
-
-    @pl.when(quarter > 0)
-    def _():
-        total[...] += part
+    bias = jnp.concatenate(rows, axis=1)
+    up, down = joined((up0, up1, up2)), joined((down0, down1))
+    half = mine_ref.shape[0]
+    for place, u_ref in ((slice(None, half), u_mine), (slice(half, None), u_other)):
+        z = rows_dot(u_ref[...], up) + bias
+        cdf = 0.5 * (1.0 + lax.erf(z * (1.0 / math.sqrt(2.0))))
+        slope = cdf + z * jnp.exp(-0.5 * z * z) * (1.0 / math.sqrt(2.0 * math.pi))
+        hidden = (z * cdf).astype(BF)
+        hidden_ref[place, :] = hidden
+        slope_ref[place, :] = slope.astype(BF)
+        part = plain_dot(hidden, down)
+
+        @pl.when(quarter == 0)
+        def _(place=place, part=part):
+            total[place, :] = part
+
+        @pl.when(quarter > 0)
+        def _(place=place, part=part):
+            total[place, :] += part
 
     @pl.when(quarter == QUARTERS - 1)
     def _():
-        half = mine_ref.shape[0]
         mine_ref[...] = total[:half]
         other_ref[...] = total[half:].astype(BF)
 
 
-def feed_forward(core, u, whole, vec):
-    rows = u.shape[0]
+def feed_forward(core, u_mine, u_other, whole, vec):
+    rows = 2 * u_mine.shape[0]
     columns = pl.BlockSpec((rows, BLOCK), lambda quarter: (0, quarter))
     half = (rows // 2, D)
     return pl.pallas_call(
         feed_forward_kernel,
         grid=(QUARTERS,),
-        in_specs=[SCALAR, whole_block(u.shape), *UP_BLOCKS, *DOWN_BLOCKS, whole_block(vec.shape)],
+        in_specs=[
+            SCALAR, whole_block(half), whole_block(half), *UP_BLOCKS, *DOWN_BLOCKS,
+            whole_block(vec.shape),
+        ],
         out_specs=[columns, columns, whole_block(half), whole_block(half)],
         out_shape=[
             jax.ShapeDtypeStruct((rows, FF // 2), BF),
@@ -403,47 +610,55 @@
         ],
         scratch_shapes=[pltpu.VMEM((rows, D), F32)],
         cost_estimate=NO_COST,
-        compiler_params=pltpu.CompilerParams(vmem_limit_bytes=56 * MIB),
-    )(core, u, whole, whole, whole, whole, whole, vec)
+        compiler_params=pltpu.CompilerParams(vmem_limit_bytes=VMEM),
+    )(core, u_mine, u_other, whole, whole, whole, whole, whole, vec)
 
 
 def feed_backward_kernel(
-    df_ref, u_ref, hidden_ref, slope_ref, up0, up1, up2, down0, down1,
+    df_mine, df_other, u_mine, u_other, hidden_ref, slope_ref, up0, up1, up2, down0, down1,
     grads_ref, bias_ref, mine_ref, other_ref, total,
 ):
     quarter = pl.program_id(0)
-    df = df_ref[...]
-    dz32 = rows_dot(df, joined((down0, down1))) * slope_ref[...].astype(F32)
-    dz = dz32.astype(BF)
-    bias_ref[...] = jnp.sum(dz.astype(F32), axis=0, keepdims=True)
-    grads_ref[0, :BLOCK] = cols_dot(dz, u_ref[...]).astype(BF)
-    grads_ref[0, BLOCK:] = cols_dot(hidden_ref[...], df).astype(BF)
-    part = plain_dot(dz, joined((up0, up1, up2)))
-
-    @pl.when(quarter == 0)
-    def _():
-        total[...] = part
-
-    @pl.when(quarter > 0)
-    def _():
-        total[...] += part
+    up, down = joined((up0, up1, up2)), joined((down0, down1))
+    half = mine_ref.shape[0]
+    grad_up = grad_down = bias = 0.0
+    for place, df_ref, u_ref in (
+        (slice(None, half), df_mine, u_mine), (slice(half, None), df_other, u_other)
+    ):
+        df = df_ref[...]
+        dz = (rows_dot(df, down) * slope_ref[place, :].astype(F32)).astype(BF)
+        bias = bias + jnp.sum(dz.astype(F32), axis=0, keepdims=True)
+        grad_up = grad_up + cols_dot(dz, u_ref[...])
+        grad_down = grad_down + cols_dot(hidden_ref[place, :], df)
+        part = plain_dot(dz, up)
+
+        @pl.when(quarter == 0)
+        def _(place=place, part=part):
+            total[place, :] = part
+
+        @pl.when(quarter > 0)
+        def _(place=place, part=part):
+            total[place, :] += part
+
+    bias_ref[...] = bias
+    grads_ref[0, :BLOCK] = grad_up.astype(BF)
+    grads_ref[0, BLOCK:] = grad_down.astype(BF)
 
     @pl.when(quarter == QUARTERS - 1)
     def _():
-        half = mine_ref.shape[0]
         mine_ref[...] = total[:half]
         other_ref[...] = total[half:].astype(BF)
 
 
-def feed_backward(df, u, hidden, slope, whole):
-    rows = u.shape[0]
+def feed_backward(df_mine, df_other, u_mine, u_other, hidden, slope, whole):
+    rows = 2 * u_mine.shape[0]
     columns = pl.BlockSpec((rows, BLOCK), lambda quarter: (0, quarter))
     half = (rows // 2, D)
     return pl.pallas_call(
         feed_backward_kernel,
         grid=(QUARTERS,),
         in_specs=[
-            whole_block(df.shape), whole_block(u.shape), columns, columns, *UP_BLOCKS, *DOWN_BLOCKS
+            *[whole_block(half)] * 4, columns, columns, *UP_BLOCKS, *DOWN_BLOCKS
         ],
         out_specs=[
             pl.BlockSpec((1, 2 * BLOCK, D), lambda quarter: (quarter, 0, 0)),
@@ -459,16 +674,16 @@
         ],
         scratch_shapes=[pltpu.VMEM((rows, D), F32)],
         cost_estimate=NO_COST,
-        compiler_params=pltpu.CompilerParams(vmem_limit_bytes=60 * MIB),
-    )(df, u, hidden, slope, whole, whole, whole, whole, whole)
+        compiler_params=pltpu.CompilerParams(vmem_limit_bytes=VMEM),
+    )(df_mine, df_other, u_mine, u_other, hidden, slope, whole, whole, whole, whole, whole)
 
 
 def adamw_update(parameter, gradient, first_old, second_old, decay_rate):
     step_float = float(STEP)
     first_new = 0.9 * first_old + 0.1 * gradient
     second_new = 0.999 * second_old + 0.001 * gradient * gradient
-    first_fix = first_new / (1.0 - 0.9**step_float)
-    second_fix = second_new / (1.0 - 0.999**step_float)
+    first_fix = first_new * (1.0 / (1.0 - 0.9**step_float))
+    second_fix = second_new * (1.0 / (1.0 - 0.999**step_float))
     update = first_fix / (jnp.sqrt(second_fix) + 1e-08)
     return (-LEARN_RATE * (update + decay_rate * parameter), first_new, second_new)
 
@@ -486,6 +701,11 @@
     parts = vector.reshape(pieces, 1, -1)
     mine = (jnp.arange(2) == core)[None, :, None]
     return jnp.where(mine, parts, 0.0).reshape(-1)
+
+
+def token_grads(d_merged, whole, grad_one):
+    rows = whole[:QUARTERS, : 3 * PAIR].reshape(-1, D)
+    return (share(plain_dot(d_merged, rows)) + grad_one).astype(BF)
 
 
 def shards(
@@ -513,11 +733,68 @@
     live = (here < length).astype(F32)[:, None]
     core_id = core.astype(jnp.int32).reshape(1)
 
-    whole, vec = gather_weights(weights, vectors, z, core)
-    x_mine = to_chips(tokens, z)
-    x = both(x_mine)
-    whole, x, x_mine, cotangent = lax.optimization_barrier((whole, x, x_mine, cotangent))
-    grad_out = to_chips(cotangent, z)
+    outer, middle = pack_weights(weights, is_out_projection(z, core))
+    vector = jnp.pad(vectors.astype(BF), (0, EXTRA * D // 2 - vectors.shape[0])).reshape(-1, D)
+    other, other_vector = swap(middle), swap(vector)
+    whole, piece = own_pieces(outer, other, vector, other_vector, z, core)
+    if by_hand():
+        x_parts = [to_chip(tokens, z, n) for n in (0, 2)]
+        piece, whole, x_parts, tokens = wait(piece, whole, x_parts, tokens)
+        up1 = along_z(piece, [(0, 1), (1, 2), (2, 3)])
+        down1 = along_z(piece, [(1, 0), (2, 1), (3, 2)])
+        up1, down1, whole = wait(up1, down1, whole)
+        mine = jnp.where(z == 0, down1, up1)
+        got = across(1, mine), across(2, mine)
+        up2 = along_z(up1, [(1, 2)])
+        down2 = along_z(down1, [(1, 0), (2, 1)])
+        mine, got, up1, up2, down1, down2 = wait(mine, got, up1, up2, down1, down2)
+        far = across(2, got[0][:, :HALF]), across(1, got[1][:, HALF:])
+        up3 = along_z(up2, [(2, 3)])
+        mine, got, far, up1, up2, up3, down1, down2 = wait(
+            mine, got, far, up1, up2, up3, down1, down2
+        )
+        mine2 = pick(z, [down2, down1, up2, up3])
+        got2 = across(1, mine2), across(2, mine2)
+        up4 = along_z(up1, [(2, 3)])
+        down3 = along_z(down2, [(1, 0)])
+        whole = place(whole, pick(z, [1, 0, 1, 2]), (mine, *got, *far))
+        mine, got, up4, down1, down2, down3, whole, tokens = wait(
+            mine2, got2, up4, down1, down2, down3, whole, tokens
+        )
+        far = across(2, got[0][:, :HALF]), across(1, got[1][:, HALF:])
+        x_parts += [to_chip(tokens, z, n) for n in (1, 3)]
+        mine, got, far, up4, down1, down2, down3, whole, x_parts, cotangent = wait(
+            mine, got, far, up4, down1, down2, down3, whole, x_parts, cotangent
+        )
+        x_mine = jnp.concatenate([x_parts[n] for n in (0, 2, 1, 3)], axis=0)
+        x = both(x_mine)
+        mine3 = pick(z, [down3, down2, down1, up4])
+        got3 = across(1, mine3), across(2, mine3)
+        grad_parts = [to_chip(cotangent, z, n) for n in (0, 1)]
+        whole = place(whole, pick(z, [2, 2, 0, 0]), (mine, *got, *far))
+        vec = vectors_of(whole[:QUARTERS], vectors.shape[0]).reshape(-1, PAIR)
+        merged = project(core_id, x, whole, vec)
+        done = attention_forward(merged, key_extra, rows * 2, 0, 2)
+        mine, got, whole, merged, done, grad_parts, cotangent = wait(
+            mine3, got3, whole, merged, done, grad_parts, cotangent
+        )
+        far = across(2, got[0][:, :HALF]), across(1, got[1][:, HALF:])
+        grad_parts += [to_chip(cotangent, z, n) for n in (2, 3)]
+        heads_out, extra = attention_forward(merged, key_extra, rows * 2, 2, 2, done)
+        mine, got, far, whole, heads_out, extra, grad_parts = wait(
+            mine, got, far, whole, heads_out, extra, grad_parts
+        )
+        whole = place(whole, pick(z, [3, 3, 3, 1]), (mine, *got, *far))
+        vec = vectors_of(whole, vectors.shape[0])
+    else:
+        whole = gather_pieces_of_all(whole, z)
+        vec = vectors_of(whole, vectors.shape[0])
+        x_mine = to_chips(tokens, z)
+        x = both(x_mine)
+        grad_parts = [to_chip(cotangent, z, n) for n in range(count)]
+        merged = project(core_id, x, whole, vec.reshape(-1, PAIR))
+        heads_out, extra = attention_forward(merged, key_extra, 2 * rows, 0, HALF // PAIR)
+    grad_out = jnp.concatenate(grad_parts, axis=0)
     bounds = [0, D, 2 * D, 3 * D, 3 * D + FF] + [(n + 4) * D + FF for n in range(6)]
     _, _, bias_o, _, bias_down, gain_one, shift_one, gain_two, shift_two = (
         vec[bounds[n] : bounds[n + 1]] for n in range(9)
@@ -525,15 +802,12 @@
     vec = vec.reshape(-1, PAIR)
     w_out = whole[QUARTERS : 2 * QUARTERS, :PAIR].reshape(HALF, D)
 
-    merged = project(core_id, x, whole, vec)
-    heads_out, extra = attention_forward(merged, key_extra, 2 * rows)
-    heads_out, extra, grad_out = lax.optimization_barrier((heads_out, extra, grad_out))
     normed_in, normed_one, inverse_one = layer_norm(
         x_mine.astype(F32) + share(plain_dot(heads_out, w_out)) + bias_o, gain_one, shift_one
     )
     u_mine = normed_in.astype(BF)
-    u = both(u_mine)
-    hidden, slope, feed, feed_other = feed_forward(core_id, u, whole, vec)
+    u_other = swap(u_mine)
+    hidden, slope, feed, feed_other = feed_forward(core_id, u_mine, u_other, whole, vec)
     feed = feed + swap(feed_other).astype(F32) + bias_down
     result, normed_two, inverse_two = layer_norm(u_mine.astype(F32) + feed, gain_two, shift_two)
     layer_out = result.astype(BF)
@@ -542,7 +816,9 @@
     grad_two, grad_gain_two, grad_shift_two = norm_back(grad_out, normed_two, inverse_two, gain_two)
     df_mine = grad_two.astype(BF)
     grad_bias_down = jnp.sum(df_mine.astype(F32), axis=0)
-    grads_ff, grad_bias_up, du, du_other = feed_backward(both(df_mine), u, hidden, slope, whole)
+    grads_ff, grad_bias_up, du, du_other = feed_backward(
+        df_mine, swap(df_mine), u_mine, u_other, hidden, slope, whole
+    )
     sum_ff = sum_over_dp(grads_ff)
     du = du + swap(du_other).astype(F32) + grad_two
     grad_one, grad_gain_one, grad_shift_one = norm_back(du, normed_one, inverse_one, gain_one)
@@ -555,8 +831,6 @@
     layer_out = from_chips(layer_out, z)
     d_merged = attention_backward(merged, extra, key_extra, heads_out, do, rows)
     d_merged, layer_out = lax.optimization_barrier((d_merged, layer_out))
-    grad_rows = share(plain_dot(d_merged, whole[:QUARTERS, : 3 * PAIR].reshape(-1, D))) + grad_one
-    grad_rows = grad_rows.astype(BF)
     grad_qkv = cols_dot(d_merged, x).astype(BF)
     sums = jnp.sum(d_merged.astype(F32), axis=0).reshape(QUARTERS, 3, PAIR)
     vector_grad = jnp.concatenate(
@@ -574,8 +848,7 @@
     ).astype(BF)
     shares = vector_grad.reshape(count, dp_count, -1).swapaxes(0, 1)
     if by_hand():
-        shares = shares.reshape(dp_count, -1, D)
-        shares = jnp.pad(shares, ((0, 0), (0, EXTRA - shares.shape[1]), (0, 0)))
+        shares = jnp.pad(shares, ((0, 0), (0, EXTRA - count), (0, D - shares.shape[2])))
     else:
         shares = jnp.pad(shares, ((0, 0), (0, 0), (0, EXTRA * D - shares.shape[2])))
         shares = shares.reshape(dp_count, count * EXTRA, D)
@@ -593,17 +866,45 @@
         axis=1,
     )
     if by_hand():
-        late, sum_ff = reduce_late(late, sum_ff)
+        late, d_merged = wait(late, d_merged)
+        grad_tokens = from_chips(token_grads(d_merged, whole, grad_one), z)
+        late, sum_ff, grad_tokens = reduce_late(late, sum_ff, grad_tokens)
         slab = late[4 * PAIR :]
         chips = [late[: 3 * PAIR], slab, late[3 * PAIR : 4 * PAIR], sum_ff[: 2 * PAIR], slab]
         chips += [sum_ff[2 * PAIR : 5 * PAIR], slab, sum_ff[5 * PAIR :], slab]
         piece = lax.psum_scatter(
             jnp.concatenate(chips, axis=0), "z", scatter_dimension=0, tiled=True
         )
-        piece, grad_rows = lax.optimization_barrier((piece, grad_rows))
-        summed, grad_tokens = gather_pieces(piece, from_chips(grad_rows, z))
+        values = gather_pieces(piece)
+        start = jnp.where(core == 0, 2 * PAIR, 0)
+        sent = jnp.stack(
+            [lax.dynamic_slice_in_dim(value, start, PAIR, 0) for value in values[:3]]
+            + [
+                jnp.concatenate(
+                    [lax.dynamic_slice_in_dim(value, start, PAIR, 0) for value in values[3:]], axis=1
+                )
+            ]
+        )
+        middle = swap(sent)
+        share_size = vectors.shape[0] // 2
+        found = [lax.dynamic_slice_in_dim(value, 3 * PAIR + z, 1, 0) for value in values[:4]]
+        last = lax.dynamic_slice_in_dim(values[4], 3 * PAIR + z, 1, 0)
+        found[3] = jnp.concatenate([found[3], last], axis=1)
+        d = lax.axis_index("dp")
+        found = jnp.stack([item[0, :share_size] for item in found])
+        found = jnp.where(d % 2 == 1, jnp.stack([found[n ^ 1] for n in range(4)]), found)
+        found = jnp.where(d >= 2, jnp.stack([found[n ^ 2] for n in range(4)]), found)
+        halves = found.reshape(2, -1).astype(F32)
+        kept, given = (
+            jnp.where(core == 0, halves[0], halves[1]), jnp.where(core == 0, halves[1], halves[0])
+        )
+        shard_v = kept + swap(given)
+        shard_w, weight_change, new_first_weights, new_second_weights = update_weights(
+            values, middle, weights, first_weights, second_weights,
+            is_out_projection(z, core), core,
+        )
     else:
-        grad_tokens = from_chips(grad_rows, z)
+        grad_tokens = from_chips(token_grads(d_merged, whole, grad_one), z)
         sum_late = lax.psum_scatter(late.reshape(-1, D), "dp", scatter_dimension=0, tiled=True)
         parts = [sum_late[n * run : (n + 1) * run] for n in range(4)]
         parts += [sum_ff[n * run : (n + 1) * run] for n in range(8)]
@@ -616,24 +917,24 @@
             jnp.concatenate(chips, axis=0), "z", scatter_dimension=0, tiled=True
         )
         summed = lax.all_gather(piece, "dp", axis=0, tiled=True).reshape(dp_count, -1, D)
-    blocks = summed[:, : 3 * run].reshape(dp_count, 3, run, D).swapaxes(0, 1).reshape(3, BLOCK, D)
-    share_size = vectors.shape[0] * 2 // dp_count
-    vector_sum = summed[:, 3 * run :].reshape(dp_count, -1)
-    start = z * share_size if by_hand() else 0
-    vector_sum = lax.dynamic_slice_in_dim(vector_sum, start, share_size, 1)
-    vector_sum = vector_sum.reshape(2, -1).astype(F32)
-    vector_sum = jnp.pad(vector_sum, ((0, 0), (0, 2 * D - vector_sum.shape[1])))
-    shard_v = vector_sum[core] + swap(vector_sum[1 - core])
-    shard_v = shard_v[: vectors.shape[0]]
-    a, b, c = blocks
-    middle = swap(jnp.where(core == 0, c, a))
-    top = jnp.concatenate([jnp.where(core == 0, a, b), middle], axis=0)
-    top = jnp.where(is_out_projection(z, core), top.T, top)
-    shard_w = jnp.concatenate([top, jnp.where(core == 0, b, c)], axis=0).astype(F32)
-
-    weight_change, new_first_weights, new_second_weights = adamw_update(
-        weights, shard_w, first_weights, second_weights, 0.01
-    )
+        blocks = summed[:, : 3 * run].reshape(dp_count, 3, run, D).swapaxes(0, 1).reshape(3, BLOCK, D)
+        share_size = vectors.shape[0] * 2 // dp_count
+        vector_sum = summed[:, 3 * run :].reshape(dp_count, -1)
+        start = 0
+        vector_sum = lax.dynamic_slice_in_dim(vector_sum, start, share_size, 1)
+        vector_sum = vector_sum.reshape(2, -1).astype(F32)
+        vector_sum = jnp.pad(vector_sum, ((0, 0), (0, 2 * D - vector_sum.shape[1])))
+        shard_v = vector_sum[core] + swap(vector_sum[1 - core])
+        shard_v = shard_v[: vectors.shape[0]]
+        a, b, c = blocks
+        middle = swap(jnp.where(core == 0, c, a))
+        top = jnp.concatenate([jnp.where(core == 0, a, b), middle], axis=0)
+        top = jnp.where(is_out_projection(z, core), top.T, top)
+        shard_w = jnp.concatenate([top, jnp.where(core == 0, b, c)], axis=0).astype(F32)
+
+        weight_change, new_first_weights, new_second_weights = adamw_update(
+            weights, shard_w, first_weights, second_weights, 0.01
+        )
     vector_change, new_first_vectors, new_second_vectors = adamw_update(
         vectors, shard_v, first_vectors, second_vectors, 0.0
     )

time: 575 us -> 564 us (0.981)
  waiting for transfers between devices: 303 us -> 206 us
  Pallas kernels: 98.7 us -> 150 us
  starting transfers between devices: 30.2 us -> 61.5 us
  other arithmetic: 60.9 us -> 39.2 us
  local copies, waits for them, and re-layouts: 45.2 us -> 63.4 us
    all_gather x1 -> x0, waiting for transfers between devices: 134 us -> none  [gather_weights(): whole = lax.all_gather(piece, ('z', 'dp'), axis=0, tiled=True)]
    pallas_call x2 -> x9, Pallas kernels: 43 us -> 92.5 us  [the longest x1 29.1 us: feed_backward(): pl.pallas_call(feed_backward_kernel, grid=(QUARTERS,), in_specs=[*[whole_...]
    ppermute x6 -> x13, waiting for transfers between devices: 27.1 us -> 44.4 us  [the longest x7 33.7 us: along_z(): return lax.ppermute(value, 'z', pairs)]
    ppermute x6 -> x13, starting transfers between devices: 10.6 us -> 26.1 us  [the longest x6 14 us: to_chip(): lax.ppermute(part, 'z', [(i, (i + shift) % count) for i in range(count)])]
    mul x2 -> x1, other arithmetic: 14.2 us -> 0.63 us  [adamw_update(): -LEARN_RATE * (update + decay_rate * parameter)]
    ppermute x8 -> x20, starting transfers between devices: 9.08 us -> 20.8 us  [across(): return lax.ppermute(value, 'dp', [(i, i ^ bit) for i in range(4)])]
    ppermute x6, waiting for transfers between devices: 9.88 us -> 20.5 us  [from_chips(): lax.ppermute(part, 'z', [(i, (i - shift) % count) for i in range(count)])]
    unnamed x105 -> x128, local copies, waits for them, and re-layouts: 14 us -> 23.3 us
  transfers between devices with their start and end apart: 34 -> 53, of which waited for: 22 -> 31; matrix products, arithmetic and copies ran while one was open for 9% -> 14% of each run, Pallas kernels for 9% -> 13%
where the time goes in v3:
time: 564 us; the launch traced here: 554 us
  waiting for transfers between devices  206 us (37%)
  Pallas kernels  150 us (27%)
  local copies, waits for them, and re-layouts  63.4 us (11%)
  starting transfers between devices  61.5 us (11%)
  other arithmetic  39.2 us (7%)
  matrix products  18.2 us (3%)
  between operations  15.6 us (3%)
    ppermute x20, waiting for transfers between devices, across(): return lax.ppermute(value, 'dp', [(i, i ^ bit) for i in range(4)])  67 us
    reduce_scatter x1, waiting for transfers between devices, shards(): lax.psum_scatter(jnp.concatenate(chips, axis=0), 'z', scatter_dimension=0...  61.6 us
    ppermute x7, waiting for transfers between devices, along_z(): return lax.ppermute(value, 'z', pairs)  33.7 us
    pallas_call x1, Pallas kernels, attention_backward(): pl.pallas_call(backward_kernel, grid=(HALF // PAIR, rows // step), in_spe...  30.6 us
    pallas_call x1, Pallas kernels, feed_backward(): pl.pallas_call(feed_backward_kernel, grid=(QUARTERS,), in_specs=[*[whole_...  29.1 us
    unnamed x128, local copies, waits for them, and re-layouts  23.3 us
    ppermute x20, starting transfers between devices, across(): return lax.ppermute(value, 'dp', [(i, i ^ bit) for i in range(4)])  20.8 us
    ppermute x6, waiting for transfers between devices, from_chips(): lax.ppermute(part, 'z', [(i, (i - shift) % count) for i in range(count)])  20.5 us
  transfers between devices with their start and end apart: 53, of which 31 were waited for; matrix products, arithmetic and copies ran while one was open for 14% of the time, Pallas kernels for 13%

profile of v3, /device:TPU:0, one launch (start us, length us, event | category | flops | bytes accessed | tf_op | source)
XLA Modules:
  0.0 554.4 jit_solution(8089132299489826587)
XLA Ops:
  7.3 5.9 %shard_map.168 = (bf16[1024,1024]{1,0:T(8,128)(2,1)}, bf16[512,1024]{1,0:T(8,128)(2,1)}) custom-call(s32[1]{0:T(128)} %bitcast.3.flag_ref, f32[1536,1024]{1,0:T(8,128)} %weight_ref.1, f32[1536,1024]{1,0:T(8,128)} %weight_ref.1), custom_call_target="tpu_custom_call" | custom-call | flops 1 | bytes 1 | tf_op jit(solution)/shard_map/pallas_call | solution.py:115
  19.6 5.3 shard_map.169
  24.8 5.0 collective-permute-done.2
  35.4 15.8 %collective-permute-done.3 = bf16[400,1024]{1,0:T(8,128)(2,1)} collective-permute-done((bf16[400,1024]{1,0:T(8,128)(2,1)}, bf16[400,1024]{1,0:T(8,128)(2,1)}, u32[]{:S(2)}, u32[]{:S(2)}) %collective-permute-start.3) | collective-permute-done | bytes 819232 | tf_op jit(solution)/shard_map/ppermute | solution.py:274
  51.2 4.9 collective-permute-done.4
  62.2 13.2 %collective-permute-done.5.got_x = bf16[400,1024]{1,0:T(8,128)(2,1)S(1)} collective-permute-done((bf16[400,1024]{1,0:T(8,128)(2,1)S(1)}, bf16[400,1024]{1,0:T(8,128)(2,1)S(1)}, u32[]{:S(2)}, u32[]{:S(2)}) %collective-permute-start.5) | collective-permute-done | bytes 819232 | tf_op jit(solution)/shard_map/ppermute | solution.py:266
  76.5 8.2 %collective-permute-done.8 = bf16[400,1024]{1,0:T(8,128)(2,1)S(1)} collective-permute-done((bf16[400,1024]{1,0:T(8,128)(2,1)S(1)}, bf16[400,1024]{1,0:T(8,128)(2,1)S(1)}, u32[]{:S(2)}, u32[]{:S(2)}) %collective-permute-start.8) | collective-permute-done | bytes 819232 | tf_op jit(solution)/shard_map/ppermute | solution.py:274
  88.9 7.3 %collective-permute-done.9.far_a = bf16[400,512]{1,0:T(8,128)(2,1)} collective-permute-done((bf16[400,512]{1,0:T(8,128)(2,1)}, bf16[400,512]{1,0:T(8,128)(2,1)}, u32[]{:S(2)}, u32[]{:S(2)}) %collective-permute-start.9) | collective-permute-done | bytes 409632 | tf_op jit(solution)/shard_map/ppermute | solution.py:266
  104.8 4.8 shard_map.170.whole_in
  109.6 5.5 collective-permute-done.12.got_x
  115.2 4.8 collective-permute-done.15
  125.0 5.7 %collective-permute-start.19 = (bf16[128,1024]{1,0:T(8,128)(2,1)}, bf16[128,1024]{1,0:T(8,128)(2,1)}, u32[]{:S(2)}, u32[]{:S(2)}) collective-permute-start(bf16[128,1024]{1,0:T(8,128)(2,1)} %get-tuple-element.275), channel_id=1, source_target_pairs={{0,6},{2,0},{4,2},{6,4},{1,7},{3,1},{5,3},{7,5},{8,14},{10,8},{12,... | collective-permute-start | bytes 786440 | tf_op jit(solution)/shard_map/ppermute | solution.py:68
  146.7 4.9 shard_map.171.w_ref.whole_in
  160.6 8.0 %shard_map.172.q_ref.k_ref.v_ref = bf16[1024,1536]{1,0:T(8,128)(2,1)} custom-call(s32[1]{0:T(128)} %bitcast.2.core_ref, bf16[1024,1024]{1,0:T(8,128)(2,1)} %constant_dynamic-update-slice_fusion.4.x_ref, bf16[16,400,1024]{2,1,0:T(8,128)(2,1)} %shard_map.171.w_ref.whole_in, f32[24,128]{1,0:T(8,128)} %reshape.339.vector_ref), custom_call_target="tpu_custom_call" | custom-call | flops 1 | bytes 1 | tf_op jit(solution)/shard_map/pallas_call | solution.py:412
  168.6 9.8 %shard_map.173 = (bf16[1024,512]{1,0:T(8,128)(2,1)}, bf16[1024,512]{1,0:T(8,128)(2,1)}) custom-call(bf16[1024,1536]{1,0:T(8,128)(2,1)} %shard_map.172.q_ref.k_ref.v_ref, bf16[1024,1536]{1,0:T(8,128)(2,1)} %shard_map.172.q_ref.k_ref.v_ref, bf16[1024,1536]{1,0:T(8,128)(2,1)} %shard_map.172.q_ref.k_ref.v_ref, bf16[1024,128]{1,0:T(8,128)(2,1)} %select_convert_fusion.key_ref), custom_call_target="tpu_custom_call" | custom-call | flops 1 | bytes 1 | tf_op jit(solution)/shard_map/pallas_call | solution.py:462
  187.9 9.8 %shard_map.174 = (bf16[1024,512]{1,0:T(8,128)(2,1)}, bf16[1024,512]{1,0:T(8,128)(2,1)}) custom-call(bf16[1024,1536]{1,0:T(8,128)(2,1)} %shard_map.172.q_ref.k_ref.v_ref, bf16[1024,1536]{1,0:T(8,128)(2,1)} %shard_map.172.q_ref.k_ref.v_ref, bf16[1024,1536]{1,0:T(8,128)(2,1)} %shard_map.172.q_ref.k_ref.v_ref, ...), custom_call_target="tpu_custom_call", output_to_operand_aliasing={{0}: (4, {}), {1}: (5, {})} | custom-call | flops 1 | bytes 1 | tf_op jit(solution)/shard_map/pallas_call | solution.py:462
  200.6 4.8 shard_map.175.up0.up1.up2.down0.down1
  220.2 19.0 %shard_map.176 = (bf16[1024,2048]{1,0:T(8,128)(2,1)}, bf16[1024,2048]{1,0:T(8,128)(2,1)}, f32[512,1024]{1,0:T(8,128)}, bf16[512,1024]{1,0:T(8,128)(2,1)}) custom-call(s32[1]{0:T(128)} %bitcast.2.core_ref, bf16[512,1024]{1,0:T(8,128)(2,1)} %copy-done.4, bf16[512,1024]{1,0:T(8,128)(2,1)} %collective-permute-done.29.u_other, ...), custom_call_target="tpu_custom_call" | custom-call | flops 1 | bytes 1 | tf_op jit(solution)/shard_map/pallas_call | solution.py:597
  254.9 29.1 %shard_map.177 = (bf16[4,1024,1024]{2,1,0:T(8,128)(2,1)}, f32[1,2048]{1,0:T(1,128)}, f32[512,1024]{1,0:T(8,128)}, bf16[512,1024]{1,0:T(8,128)(2,1)}) custom-call(bf16[512,1024]{1,0:T(8,128)(2,1)} %copy-done.7, bf16[512,1024]{1,0:T(8,128)(2,1)} %copy-done.31, bf16[512,1024]{1,0:T(8,128)(2,1)} %copy-done.4, bf16[512,1024]{1,0:T(8,128)(2,1)} %collective-permute-done.29.u_other, ...), custom_call_target="tpu_custom_call" | custom-call | flops 1 | bytes 1 | tf_op jit(solution)/shard_map/pallas_call | solution.py:657
  287.0 4.5 multiply_reduce_fusion.1
  294.2 4.0 slice.246
  298.3 4.0 convolution_convert_fusion.2.do_ref
  303.1 6.6 %collective-permute-start.34 = (bf16[128,1024]{1,0:T(8,128)(2,1)S(1)}, bf16[128,1024]{1,0:T(8,128)(2,1)S(1)}, u32[]{:S(2)}, u32[]{:S(2)}) collective-permute-start(bf16[128,1024]{1,0:T(8,128)(2,1)S(1)} %get-tuple-element.270), channel_id=1, source_target_pairs={{0,6},{2,0},{4,2},{6,4},{1,7},{3,1},{5,3},{7,5},{8,14},{10,8},{12,... | collective-permute-start | bytes 786440 | tf_op jit(solution)/shard_map/ppermute | solution.py:83
  310.5 3.9 convolution_convert_fusion.1
  316.1 30.6 %shard_map.178 = bf16[1024,1536]{1,0:T(8,128)(2,1)} custom-call(bf16[1024,1536]{1,0:T(8,128)(2,1)} %shard_map.172.q_ref.k_ref.v_ref, bf16[1024,512]{1,0:T(8,128)(2,1)} %get-tuple-element.192.extra_ref, bf16[1024,1536]{1,0:T(8,128)(2,1)} %shard_map.172.q_ref.k_ref.v_ref, bf16[1024,1536]{1,0:T(8,128)(2,1)} %shard_map.172.q_ref.k_ref.v_ref, ...), custom_call_target="tpu_custom_call" | custom-call | flops 1 | bytes 1 | tf_op jit(solution)/shard_map/pallas_call | solution.py:526
  352.6 5.6 %convolution_convert_fusion = bf16[1536,1024]{1,0:T(8,128)(2,1)S(1)} fusion(bf16[1024,1536]{1,0:T(8,128)(2,1)S(1)} %copy-done.1, bf16[1024,1024]{1,0:T(8,128)(2,1)} %constant_dynamic-update-slice_fusion.4.x_ref), kind=kOutput, calls=%fused_computation.4 | convolution fusion | flops 3222798336 | bytes 8388608 | tf_op jit(solution)/shard_map/dot_general | solution.py:35
  387.5 16.7 %collective-permute-done.41 = bf16[128,1024]{1,0:T(8,128)(2,1)S(1)} collective-permute-done((bf16[128,1024]{1,0:T(8,128)(2,1)S(1)}, bf16[128,1024]{1,0:T(8,128)(2,1)S(1)}, u32[]{:S(2)}, u32[]{:S(2)}) %collective-permute-start.41) | collective-permute-done | bytes 262176 | tf_op jit(solution)/shard_map/ppermute | solution.py:83
  410.9 10.1 %collective-permute-done.43 = bf16[528,512]{1,0:T(8,128)(2,1)S(1)} collective-permute-done((bf16[528,512]{1,0:T(8,128)(2,1)S(1)}, bf16[528,512]{1,0:T(8,128)(2,1)S(1)}, u32[]{:S(2)}, u32[]{:S(2)}) %collective-permute-start.43) | collective-permute-done | bytes 540704 | tf_op jit(solution)/shard_map/ppermute | solution.py:266
  428.4 61.6 %reduce-scatter.5.cloned.1.call-done.mine = bf16[400,1024]{1,0:T(8,128)(2,1)} async-done(((bf16[1600,1024]{1,0:T(8,128)(2,1)}), bf16[400,1024]{1,0:T(8,128)(2,1)}) %reduce-scatter.5.cloned.1.call-update) | async-done | bytes 819216 | tf_op jit(solution)/shard_map/reduce_scatter | solution.py:875
  492.9 17.1 %collective-permute-done.45.got_x = bf16[400,1024]{1,0:T(8,128)(2,1)S(1)} collective-permute-done((bf16[400,1024]{1,0:T(8,128)(2,1)}, bf16[400,1024]{1,0:T(8,128)(2,1)S(1)}, u32[]{:S(2)}, u32[]{:S(2)}) %collective-permute-start.45) | collective-permute-done | bytes 819232 | tf_op jit(solution)/shard_map/ppermute | solution.py:266
  513.4 7.8 %collective-permute-done.47.far_a = bf16[400,512]{1,0:T(8,128)(2,1)S(1)} collective-permute-done((bf16[400,512]{1,0:T(8,128)(2,1)S(1)}, bf16[400,512]{1,0:T(8,128)(2,1)S(1)}, u32[]{:S(2)}, u32[]{:S(2)}) %collective-permute-start.47) | collective-permute-done | bytes 409632 | tf_op jit(solution)/shard_map/ppermute | solution.py:266
  528.9 18.3 %shard_map.179 = (f32[1536,1024]{1,0:T(8,128)}, f32[1536,1024]{1,0:T(8,128)}, f32[1536,1024]{1,0:T(8,128)}, f32[1536,1024]{1,0:T(8,128)}) custom-call(s32[3]{0:T(128)} %pad_add_fusion.4.where_ref, bf16[400,1024]{1,0:T(8,128)(2,1)} %reduce-scatter.5.cloned.1.call-done.mine, bf16[400,1024]{1,0:T(8,128)(2,1)} %copy-done.14, bf16[400,1024]{1,0:T(8,128)(2,1)} %copy-done.15, ...), custom_call_target="tpu_custom_call" | custom-call | flops 1 | bytes 1 | tf_op jit(solution)/shard_map/pallas_call | solution.py:363
  (345 shorter events, 176.5 us)
Async XLA Ops:
  7.2 398.4 %reduce-scatter.3.cloned.1.call-start = ((), (), s32[]{:S(2)}) async-start(), calls=%async_computation.2 | async-start | bytes 10485760 | tf_op jit(solution)/shard_map/reduce_scatter | solution.py:254
  13.6 16.2 %collective-permute-start.2 = (bf16[128,1024]{1,0:T(8,128)(2,1)S(1)}, bf16[128,1024]{1,0:T(8,128)(2,1)S(1)}, u32[]{:S(2)}, u32[]{:S(2)}) collective-permute-start(bf16[128,1024]{1,0:T(8,128)(2,1)S(1)} %get-tuple-element.277), channel_id=1, source_target_pairs={{0,4},{2,6},{4,0},{6,2},{1,5},{3,7},{5,1},{7,3},{8,12},{10,14},{12... | collective-permute-start | bytes 786440 | tf_op jit(solution)/shard_map/ppermute | solution.py:68
  30.6 20.7 %collective-permute-start.3 = (bf16[400,1024]{1,0:T(8,128)(2,1)}, bf16[400,1024]{1,0:T(8,128)(2,1)}, u32[]{:S(2)}, u32[]{:S(2)}) collective-permute-start(bf16[400,1024]{1,0:T(8,128)(2,1)} %get-tuple-element.129), channel_id=1, source_target_pairs={{0,2},{2,4},{4,6},{1,3},{3,5},{5,7},{8,10},{10,12},{12,14},{9,11},... | collective-permute-start | bytes 2457608 | tf_op jit(solution)/shard_map/ppermute | solution.py:274
  34.1 22.0 %collective-permute-start.4 = (bf16[400,1024]{1,0:T(8,128)(2,1)}, bf16[400,1024]{1,0:T(8,128)(2,1)S(1)}, u32[]{:S(2)}, u32[]{:S(2)}) collective-permute-start(bf16[400,1024]{1,0:T(8,128)(2,1)} %get-tuple-element.129), channel_id=1, source_target_pairs={{2,0},{4,2},{6,4},{3,1},{5,3},{7,5},{10,8},{12,10},{14,12},{11,9},... | collective-permute-start | bytes 2457608 | tf_op jit(solution)/shard_map/ppermute | solution.py:274
  56.2 19.1 %collective-permute-start.5 = (bf16[400,1024]{1,0:T(8,128)(2,1)S(1)}, bf16[400,1024]{1,0:T(8,128)(2,1)S(1)}, u32[]{:S(2)}, u32[]{:S(2)}) collective-permute-start(bf16[400,1024]{1,0:T(8,128)(2,1)S(1)} %broadcast_select_fusion.mine), channel_id=1, source_target_pairs={{0,8},{8,0},{16,24},{24,16},{1,9},{9,1},{17,25},{25,17},{2,10},{10... | collective-permute-start | bytes 2457608 | tf_op jit(solution)/shard_map/ppermute | solution.py:266
  57.8 18.7 %collective-permute-start.6 = (bf16[400,1024]{1,0:T(8,128)(2,1)S(1)}, bf16[400,1024]{1,0:T(8,128)(2,1)S(1)}, u32[]{:S(2)}, u32[]{:S(2)}) collective-permute-start(bf16[400,1024]{1,0:T(8,128)(2,1)S(1)} %broadcast_select_fusion.mine), channel_id=1, source_target_pairs={{0,16},{8,24},{16,0},{24,8},{1,17},{9,25},{17,1},{25,9},{2,18},{10... | collective-permute-start | bytes 2457608 | tf_op jit(solution)/shard_map/ppermute | solution.py:266
  59.3 17.2 %collective-permute-start.7 = (bf16[400,1024]{1,0:T(8,128)(2,1)}, bf16[400,1024]{1,0:T(8,128)(2,1)}, u32[]{:S(2)}, u32[]{:S(2)}) collective-permute-start(bf16[400,1024]{1,0:T(8,128)(2,1)} %collective-permute-done.3), channel_id=1, source_target_pairs={{2,4},{3,5},{10,12},{11,13},{18,20},{19,21},{26,28},{27,29}} | collective-permute-start | bytes 2457608 | tf_op jit(solution)/shard_map/ppermute | solution.py:274
  60.9 23.8 %collective-permute-start.8 = (bf16[400,1024]{1,0:T(8,128)(2,1)S(1)}, bf16[400,1024]{1,0:T(8,128)(2,1)S(1)}, u32[]{:S(2)}, u32[]{:S(2)}) collective-permute-start(bf16[400,1024]{1,0:T(8,128)(2,1)S(1)} %collective-permute-done.4), channel_id=1, source_target_pairs={{2,0},{4,2},{3,1},{5,3},{10,8},{12,10},{11,9},{13,11},{18,16},{20,... | collective-permute-start | bytes 2457608 | tf_op jit(solution)/shard_map/ppermute | solution.py:274
  98.5 16.6 %collective-permute-start.12 = (bf16[400,1024]{1,0:T(8,128)(2,1)S(1)}, bf16[400,1024]{1,0:T(8,128)(2,1)}, u32[]{:S(2)}, u32[]{:S(2)}) collective-permute-start(bf16[400,1024]{1,0:T(8,128)(2,1)S(1)} %select_select_fusion.1.mine), channel_id=1, source_target_pairs={{0,8},{8,0},{16,24},{24,16},{1,9},{9,1},{17,25},{25,17},{2,10},{10... | collective-permute-start | bytes 2457608 | tf_op jit(solution)/shard_map/ppermute | solution.py:266
  99.1 16.1 %collective-permute-start.13 = (bf16[400,1024]{1,0:T(8,128)(2,1)S(1)}, bf16[400,1024]{1,0:T(8,128)(2,1)S(1)}, u32[]{:S(2)}, u32[]{:S(2)}) collective-permute-start(bf16[400,1024]{1,0:T(8,128)(2,1)S(1)} %select_select_fusion.1.mine), channel_id=1, source_target_pairs={{0,16},{8,24},{16,0},{24,8},{1,17},{9,25},{17,1},{25,9},{2,18},{10... | collective-permute-start | bytes 2457608 | tf_op jit(solution)/shard_map/ppermute | solution.py:266
  100.6 14.6 %collective-permute-start.14 = (bf16[400,1024]{1,0:T(8,128)(2,1)}, bf16[400,1024]{1,0:T(8,128)(2,1)}, u32[]{:S(2)}, u32[]{:S(2)}) collective-permute-start(bf16[400,1024]{1,0:T(8,128)(2,1)} %collective-permute-done.3), channel_id=1, source_target_pairs={{4,6},{5,7},{12,14},{13,15},{20,22},{21,23},{28,30},{29,31}} | collective-permute-start | bytes 2457608 | tf_op jit(solution)/shard_map/ppermute | solution.py:274
  102.2 17.8 %collective-permute-start.15 = (bf16[400,1024]{1,0:T(8,128)(2,1)S(1)}, bf16[400,1024]{1,0:T(8,128)(2,1)}, u32[]{:S(2)}, u32[]{:S(2)}) collective-permute-start(bf16[400,1024]{1,0:T(8,128)(2,1)S(1)} %collective-permute-done.8), channel_id=1, source_target_pairs={{2,0},{3,1},{10,8},{11,9},{18,16},{19,17},{26,24},{27,25}} | collective-permute-start | bytes 2457608 | tf_op jit(solution)/shard_map/ppermute | solution.py:274
  121.0 15.9 %collective-permute-start.16 = (bf16[400,512]{1,0:T(8,128)(2,1)S(1)}, bf16[400,512]{1,0:T(8,128)(2,1)}, u32[]{:S(2)}, u32[]{:S(2)}) collective-permute-start(bf16[400,512]{1,0:T(8,128)(2,1)S(1)} %slice.177), channel_id=1, source_target_pairs={{0,16},{8,24},{16,0},{24,8},{1,17},{9,25},{17,1},{25,9},{2,18},{10... | collective-permute-start | bytes 1228808 | tf_op jit(solution)/shard_map/ppermute | solution.py:266
  121.6 15.3 %collective-permute-start.17 = (bf16[400,512]{1,0:T(8,128)(2,1)S(1)}, bf16[400,512]{1,0:T(8,128)(2,1)}, u32[]{:S(2)}, u32[]{:S(2)}) collective-permute-start(bf16[400,512]{1,0:T(8,128)(2,1)S(1)} %slice.178), channel_id=1, source_target_pairs={{0,8},{8,0},{16,24},{24,16},{1,9},{9,1},{17,25},{25,17},{2,10},{10... | collective-permute-start | bytes 1228808 | tf_op jit(solution)/shard_map/ppermute | solution.py:266
  144.1 13.3 %collective-permute-start.22 = (bf16[512,1024]{1,0:T(8,128)(2,1)}, bf16[512,1024]{1,0:T(8,128)(2,1)}, u32[]{:S(2)}, u32[]{:S(2)}) collective-permute-start(bf16[512,1024]{1,0:T(8,128)(2,1)} %get-tuple-element.279), channel_id=1, source_target_pairs={{0,1},{1,0},{2,3},{3,2},{4,5},{5,4},{6,7},{7,6},{8,9},{9,8},{10,11... | collective-permute-start | bytes 3145736 | tf_op jit(solution)/shard_map/ppermute | solution.py:43
  145.6 32.8 %collective-permute-start.20 = (bf16[400,1024]{1,0:T(8,128)(2,1)S(1)}, bf16[400,1024]{1,0:T(8,128)(2,1)S(1)}, u32[]{:S(2)}, u32[]{:S(2)}) collective-permute-start(bf16[400,1024]{1,0:T(8,128)(2,1)S(1)} %select_select_fusion.mine), channel_id=1, source_target_pairs={{0,8},{8,0},{16,24},{24,16},{1,9},{9,1},{17,25},{25,17},{2,10},{10... | collective-permute-start | bytes 2457608 | tf_op jit(solution)/shard_map/ppermute | solution.py:266
  146.2 32.2 %collective-permute-start.21 = (bf16[400,1024]{1,0:T(8,128)(2,1)S(1)}, bf16[400,1024]{1,0:T(8,128)(2,1)}, u32[]{:S(2)}, u32[]{:S(2)}) collective-permute-start(bf16[400,1024]{1,0:T(8,128)(2,1)S(1)} %select_select_fusion.mine), channel_id=1, source_target_pairs={{0,16},{8,24},{16,0},{24,8},{1,17},{9,25},{17,1},{25,9},{2,18},{10... | collective-permute-start | bytes 2457608 | tf_op jit(solution)/shard_map/ppermute | solution.py:266
  155.6 22.7 %collective-permute-start.23 = (bf16[128,1024]{1,0:T(8,128)(2,1)S(1)}, bf16[128,1024]{1,0:T(8,128)(2,1)S(1)}, u32[]{:S(2)}, u32[]{:S(2)}) collective-permute-start(bf16[128,1024]{1,0:T(8,128)(2,1)S(1)} %get-tuple-element.273), channel_id=1, source_target_pairs={{0,2},{2,4},{4,6},{6,0},{1,3},{3,5},{5,7},{7,1},{8,10},{10,12},{12... | collective-permute-start | bytes 786440 | tf_op jit(solution)/shard_map/ppermute | solution.py:68
  178.4 21.3 %collective-permute-start.24 = (bf16[400,512]{1,0:T(8,128)(2,1)S(1)}, bf16[400,512]{1,0:T(8,128)(2,1)S(1)}, u32[]{:S(2)}, u32[]{:S(2)}) collective-permute-start(bf16[400,512]{1,0:T(8,128)(2,1)S(1)} %slice.182), channel_id=1, source_target_pairs={{0,16},{8,24},{16,0},{24,8},{1,17},{9,25},{17,1},{25,9},{2,18},{10... | collective-permute-start | bytes 1228808 | tf_op jit(solution)/shard_map/ppermute | solution.py:266
  181.1 18.7 %collective-permute-start.25 = (bf16[400,512]{1,0:T(8,128)(2,1)S(1)}, bf16[400,512]{1,0:T(8,128)(2,1)}, u32[]{:S(2)}, u32[]{:S(2)}) collective-permute-start(bf16[400,512]{1,0:T(8,128)(2,1)S(1)} %slice.183), channel_id=1, source_target_pairs={{0,8},{8,0},{16,24},{24,16},{1,9},{9,1},{17,25},{25,17},{2,10},{10... | collective-permute-start | bytes 1228808 | tf_op jit(solution)/shard_map/ppermute | solution.py:266
  184.5 13.9 %collective-permute-start.26 = (bf16[128,1024]{1,0:T(8,128)(2,1)}, bf16[128,1024]{1,0:T(8,128)(2,1)S(1)}, u32[]{:S(2)}, u32[]{:S(2)}) collective-permute-start(bf16[128,1024]{1,0:T(8,128)(2,1)} %get-tuple-element.272), channel_id=1, source_target_pairs={{0,4},{2,6},{4,0},{6,2},{1,5},{3,7},{5,1},{7,3},{8,12},{10,14},{12... | collective-permute-start | bytes 786440 | tf_op jit(solution)/shard_map/ppermute | solution.py:68
  284.0 205.9 %reduce-scatter.5.cloned.1.call-start = ((), (), s32[]{:S(2)}) async-start(), calls=%async_computation.3 | async-start | bytes 4096000 | tf_op jit(solution)/shard_map/reduce_scatter | solution.py:875
  303.1 43.6 %collective-permute-start.34 = (bf16[128,1024]{1,0:T(8,128)(2,1)S(1)}, bf16[128,1024]{1,0:T(8,128)(2,1)S(1)}, u32[]{:S(2)}, u32[]{:S(2)}) collective-permute-start(bf16[128,1024]{1,0:T(8,128)(2,1)S(1)} %get-tuple-element.270), channel_id=1, source_target_pairs={{0,6},{2,0},{4,2},{6,4},{1,7},{3,1},{5,3},{7,5},{8,14},{10,8},{12,... | collective-permute-start | bytes 786440 | tf_op jit(solution)/shard_map/ppermute | solution.py:83
  309.8 37.7 %collective-permute-start.35 = (bf16[128,1024]{1,0:T(8,128)(2,1)}, bf16[128,1024]{1,0:T(8,128)(2,1)}, u32[]{:S(2)}, u32[]{:S(2)}) collective-permute-start(bf16[128,1024]{1,0:T(8,128)(2,1)} %get-tuple-element.269), channel_id=1, source_target_pairs={{0,4},{2,6},{4,0},{6,2},{1,5},{3,7},{5,1},{7,3},{8,12},{10,14},{12... | collective-permute-start | bytes 786440 | tf_op jit(solution)/shard_map/ppermute | solution.py:83
  309.8 39.5 %collective-permute-start.36 = (bf16[128,1024]{1,0:T(8,128)(2,1)}, bf16[128,1024]{1,0:T(8,128)(2,1)S(1)}, u32[]{:S(2)}, u32[]{:S(2)}) collective-permute-start(bf16[128,1024]{1,0:T(8,128)(2,1)} %get-tuple-element.268), channel_id=1, source_target_pairs={{0,2},{2,4},{4,6},{6,0},{1,3},{3,5},{5,7},{7,1},{8,10},{10,12},{12... | collective-permute-start | bytes 786440 | tf_op jit(solution)/shard_map/ppermute | solution.py:83
  371.3 34.2 %collective-permute-start.37 = (bf16[2,528,512]{2,1,0:T(8,128)(2,1)}, bf16[2,528,512]{2,1,0:T(8,128)(2,1)}, u32[]{:S(2)}, u32[]{:S(2)}) collective-permute-start(bf16[2,528,512]{2,1,0:T(8,128)(2,1)} %dynamic-slice_bitcast_fusion.3), channel_id=1, source_target_pairs={{0,8},{8,0},{16,24},{24,16},{1,9},{9,1},{17,25},{25,17},{2,10},{10... | collective-permute-start | bytes 3244040 | tf_op jit(solution)/shard_map/ppermute | solution.py:266
  372.9 32.6 %collective-permute-start.38 = (bf16[2,528,512]{2,1,0:T(8,128)(2,1)}, bf16[2,528,512]{2,1,0:T(8,128)(2,1)}, u32[]{:S(2)}, u32[]{:S(2)}) collective-permute-start(bf16[2,528,512]{2,1,0:T(8,128)(2,1)} %dynamic-slice_bitcast_fusion.2), channel_id=1, source_target_pairs={{0,16},{8,24},{16,0},{24,8},{1,17},{9,25},{17,1},{25,9},{2,18},{10... | collective-permute-start | bytes 3244040 | tf_op jit(solution)/shard_map/ppermute | solution.py:266
  380.8 23.3 %collective-permute-start.41 = (bf16[128,1024]{1,0:T(8,128)(2,1)S(1)}, bf16[128,1024]{1,0:T(8,128)(2,1)S(1)}, u32[]{:S(2)}, u32[]{:S(2)}) collective-permute-start(bf16[128,1024]{1,0:T(8,128)(2,1)S(1)} %copy-done.43), channel_id=1, source_target_pairs={{0,4},{2,6},{4,0},{6,2},{1,5},{3,7},{5,1},{7,3},{8,12},{10,14},{12... | collective-permute-start | bytes 786440 | tf_op jit(solution)/shard_map/ppermute | solution.py:83
  382.3 22.6 %collective-permute-start.42 = (bf16[128,1024]{1,0:T(8,128)(2,1)S(1)}, bf16[128,1024]{1,0:T(8,128)(2,1)S(1)}, u32[]{:S(2)}, u32[]{:S(2)}) collective-permute-start(bf16[128,1024]{1,0:T(8,128)(2,1)S(1)} %copy-done.42), channel_id=1, source_target_pairs={{0,2},{2,4},{4,6},{6,0},{1,3},{3,5},{5,7},{7,1},{8,10},{10,12},{12... | collective-permute-start | bytes 786440 | tf_op jit(solution)/shard_map/ppermute | solution.py:83
  407.1 13.9 %collective-permute-start.43 = (bf16[528,512]{1,0:T(8,128)(2,1)S(1)}, bf16[528,512]{1,0:T(8,128)(2,1)S(1)}, u32[]{:S(2)}, u32[]{:S(2)}) collective-permute-start(bf16[528,512]{1,0:T(8,128)(2,1)S(1)} %fusion.12), channel_id=1, source_target_pairs={{0,16},{8,24},{16,0},{24,8},{1,17},{9,25},{17,1},{25,9},{2,18},{10... | collective-permute-start | bytes 1622024 | tf_op jit(solution)/shard_map/ppermute | solution.py:266
  490.0 20.0 %collective-permute-start.45 = (bf16[400,1024]{1,0:T(8,128)(2,1)}, bf16[400,1024]{1,0:T(8,128)(2,1)S(1)}, u32[]{:S(2)}, u32[]{:S(2)}) collective-permute-start(bf16[400,1024]{1,0:T(8,128)(2,1)} %reduce-scatter.5.cloned.1.call-done.mine), channel_id=1, source_target_pairs={{0,8},{8,0},{16,24},{24,16},{1,9},{9,1},{17,25},{25,17},{2,10},{10... | collective-permute-start | bytes 2457608 | tf_op jit(solution)/shard_map/ppermute | solution.py:266
  491.4 19.8 %collective-permute-start.46 = (bf16[400,1024]{1,0:T(8,128)(2,1)}, bf16[400,1024]{1,0:T(8,128)(2,1)S(1)}, u32[]{:S(2)}, u32[]{:S(2)}) collective-permute-start(bf16[400,1024]{1,0:T(8,128)(2,1)} %reduce-scatter.5.cloned.1.call-done.mine), channel_id=1, source_target_pairs={{0,16},{8,24},{16,0},{24,8},{1,17},{9,25},{17,1},{25,9},{2,18},{10... | collective-permute-start | bytes 2457608 | tf_op jit(solution)/shard_map/ppermute | solution.py:266
  (75 other events, 495.9 us)
Sparse Core Ops, SparseCore 0:
  284.2 88.7 reduce-scatter.2
  428.5 61.4 reduce-scatter.4

commit v4 on v3

--- a/solution.py
+++ b/solution.py
@@ -73,16 +73,24 @@
     return jnp.concatenate([to_chip(blocks, z, n) for n in range(lax.axis_size("z"))], axis=0)
 
 
+def from_chip(rows, shift):
+    count = lax.axis_size("z")
+    part = rows.reshape(count, -1, rows.shape[-1])[shift]
+    if shift:
+        part = lax.ppermute(part, "z", [(i, (i - shift) % count) for i in range(count)])
+    return part
+
+
+def put_together(parts, z):
+    count = lax.axis_size("z")
+    result = jnp.zeros((count, *parts[0].shape), BF)
+    for shift in range(count):
+        result = lax.dynamic_update_index_in_dim(result, parts[shift], (z + shift) % count, 0)
+    return result
+
+
 def from_chips(rows, z):
-    count = lax.axis_size("z")
-    blocks = rows.reshape(count, -1, rows.shape[-1])
-    result = blocks
-    for shift in range(count):
-        part = blocks[shift]
-        if shift:
-            part = lax.ppermute(part, "z", [(i, (i - shift) % count) for i in range(count)])
-        result = lax.dynamic_update_index_in_dim(result, part, (z + shift) % count, 0)
-    return result
+    return put_together([from_chip(rows, n) for n in range(lax.axis_size("z"))], z)
 
 
 def is_out_projection(z, core):
@@ -207,10 +215,9 @@
     return jnp.concatenate([everything.reshape(-1, 3 * PAIR, D), spare], axis=1)
 
 
-def vectors_of(whole, size):
-    found = whole.reshape(-1, QUARTERS, PIECE, D)[:, 0, 3 * PAIR :]
-    found = found.reshape(-1, 2, EXTRA * D // 2)[:, :, :size]
-    return found.reshape(-1).astype(F32)
+def vectors_of(whole, size, chips):
+    found = jnp.stack([whole[QUARTERS * chip, 3 * PAIR :] for chip in range(chips)])
+    return found.reshape(-1, 2, EXTRA * D // 2)[:, :, :size].reshape(-1).astype(F32)
 
 
 def place_kernel(where_ref, whole_in, mine, got_x, got_y, far_a, far_b, whole_ref):
@@ -285,28 +292,68 @@
     return lax.optimization_barrier(values)
 
 
-def reduce_late(late, sum_ff, grad_tokens):
+def assemble_kernel(a_ref, b_ref, sums_ref, out_ref):
+    chip = pl.program_id(0)
+    rows = 3 * PAIR
+    out_ref[rows:, :HALF] = a_ref[4 * PAIR :]
+    out_ref[rows:, HALF:] = b_ref[4 * PAIR :]
+
+    @pl.when(chip == 0)
+    def _():
+        out_ref[:rows, :HALF] = a_ref[:rows]
+        out_ref[:rows, HALF:] = b_ref[:rows]
+
+    @pl.when(chip == 1)
+    def _():
+        out_ref[:PAIR, :HALF] = a_ref[rows : rows + PAIR]
+        out_ref[:PAIR, HALF:] = b_ref[rows : rows + PAIR]
+        out_ref[PAIR:rows] = sums_ref[: 2 * PAIR]
+
+    @pl.when(chip == 2)
+    def _():
+        out_ref[:rows] = sums_ref[2 * PAIR : 5 * PAIR]
+
+    @pl.when(chip == 3)
+    def _():
+        out_ref[:rows] = sums_ref[5 * PAIR :]
+
+
+def assemble(a, b, sums):
+    return pl.pallas_call(
+        assemble_kernel,
+        grid=(4,),
+        in_specs=[whole_block(item.shape) for item in (a, b, sums)],
+        out_specs=pl.BlockSpec((PIECE, D), lambda chip: (chip, 0)),
+        out_shape=jax.ShapeDtypeStruct((4 * PIECE, D), BF),
+        cost_estimate=NO_COST,
+        compiler_params=pltpu.CompilerParams(vmem_limit_bytes=VMEM),
+    )(a, b, sums)
+
+
+def reduce_late(late, sum_ff, grad_rows):
     d = lax.axis_index("dp")
     x, y = d % 2, d // 2
     late = late.reshape(2, 2, -1, D)
     a, b = late[..., :HALF], late[..., HALF:]
     got_a, got_b = across(1, at(a, 1 - x, 1)), across(2, at(b, 1 - y, 0))
-    got_a, got_b, a, b, sum_ff, grad_tokens = wait(got_a, got_b, a, b, sum_ff, grad_tokens)
+    got_a, got_b, a, b, sum_ff, grad_rows = wait(got_a, got_b, a, b, sum_ff, grad_rows)
     a, b = at(a, x, 1), at(b, y, 0)
     far_a = across(2, plus(at(a, 1 - y, 0), at(got_a, 1 - y, 0)))
     far_b = across(1, plus(at(b, 1 - x, 0), at(got_b, 1 - x, 0)))
-    far_a, far_b, a, b = lax.optimization_barrier((far_a, far_b, a, b))
+    parts = {n: from_chip(grad_rows, n) for n in (0, 1, 3)}
+    far_a, far_b, a, b, parts, grad_rows = wait(far_a, far_b, a, b, parts, grad_rows)
     a = plus(plus(at(a, y, 0), at(got_a, y, 0)), far_a)
     b = plus(plus(at(b, x, 0), at(got_b, x, 0)), far_b)
-    return jnp.concatenate([a, b], axis=-1), sum_ff, grad_tokens
-
-
-def gather_pieces(piece):
+    return assemble(a, b, sum_ff), parts, grad_rows
+
+
+def gather_pieces(piece, grad_rows, parts, z):
     got = across(1, piece), across(2, piece)
-    got, piece = wait(got, piece)
+    parts = {**parts, 2: from_chip(grad_rows, 2)}
+    got, piece, parts = wait(got, piece, parts)
     far = across(2, got[0][:, :HALF]), across(1, got[1][:, HALF:])
-    far, got, piece = wait(far, got, piece)
-    return (piece, *got, *far)
+    far, got, piece, parts = wait(far, got, piece, parts)
+    return (piece, *got, *far), put_together(parts, z)
 
 
 def update_kernel(
@@ -398,23 +445,26 @@
     return pl.BlockSpec(shape, lambda *_: (0,) * len(shape))
 
 
-def qkv_kernel(core_ref, x_ref, w_ref, vector_ref, out_ref):
+def qkv_kernel(core_ref, x_mine, x_other, w_ref, vector_ref, out_ref):
     quarter = pl.program_id(0)
     row = core_ref[0] * QUARTERS + quarter
     bias_q = vector_ref[pl.ds(row, 1), :]
     bias_v = vector_ref[pl.ds(D // PAIR + row, 1), :]
     bias = jnp.concatenate([bias_q, jnp.zeros_like(bias_q), bias_v], axis=1)
-    out_ref[...] = (rows_dot(x_ref[...], w_ref[0]) + bias).astype(BF)
-
-
-def project(core, x, whole, vec):
-    rows = x.shape[0]
+    half = x_mine.shape[0]
+    out_ref[:half] = (rows_dot(x_mine[...], w_ref[0]) + bias).astype(BF)
+    out_ref[half:] = (rows_dot(x_other[...], w_ref[0]) + bias).astype(BF)
+
+
+def project(core, x_mine, x_other, whole, vec):
+    rows = 2 * x_mine.shape[0]
     return pl.pallas_call(
         qkv_kernel,
         grid=(QUARTERS,),
         in_specs=[
             SCALAR,
-            whole_block(x.shape),
+            whole_block(x_mine.shape),
+            whole_block(x_mine.shape),
             pl.BlockSpec((1, 3 * PAIR, D), lambda quarter: (quarter, 0, 0)),
             whole_block(vec.shape),
         ],
@@ -422,7 +472,7 @@
         out_shape=jax.ShapeDtypeStruct((rows, 3 * HALF), BF),
         cost_estimate=NO_COST,
         compiler_params=pltpu.CompilerParams(vmem_limit_bytes=VMEM),
-    )(core, x, whole, vec)
+    )(core, x_mine, x_other, whole, vec)
 
 
 def forward_kernel(q_ref, k_ref, v_ref, key_ref, o_ref, extra_ref):
@@ -767,32 +817,31 @@
             mine, got, far, up4, down1, down2, down3, whole, x_parts, cotangent
         )
         x_mine = jnp.concatenate([x_parts[n] for n in (0, 2, 1, 3)], axis=0)
-        x = both(x_mine)
+        x_other = swap(x_mine)
         mine3 = pick(z, [down3, down2, down1, up4])
         got3 = across(1, mine3), across(2, mine3)
         grad_parts = [to_chip(cotangent, z, n) for n in (0, 1)]
         whole = place(whole, pick(z, [2, 2, 0, 0]), (mine, *got, *far))
-        vec = vectors_of(whole[:QUARTERS], vectors.shape[0]).reshape(-1, PAIR)
-        merged = project(core_id, x, whole, vec)
-        done = attention_forward(merged, key_extra, rows * 2, 0, 2)
-        mine, got, whole, merged, done, grad_parts, cotangent = wait(
-            mine3, got3, whole, merged, done, grad_parts, cotangent
+        vec = vectors_of(whole, vectors.shape[0], 1).reshape(-1, PAIR)
+        merged = project(core_id, x_mine, x_other, whole, vec)
+        mine, got, whole, merged, grad_parts, cotangent = wait(
+            mine3, got3, whole, merged, grad_parts, cotangent
         )
         far = across(2, got[0][:, :HALF]), across(1, got[1][:, HALF:])
         grad_parts += [to_chip(cotangent, z, n) for n in (2, 3)]
-        heads_out, extra = attention_forward(merged, key_extra, rows * 2, 2, 2, done)
+        heads_out, extra = attention_forward(merged, key_extra, rows * 2, 0, HALF // PAIR)
         mine, got, far, whole, heads_out, extra, grad_parts = wait(
             mine, got, far, whole, heads_out, extra, grad_parts
         )
         whole = place(whole, pick(z, [3, 3, 3, 1]), (mine, *got, *far))
-        vec = vectors_of(whole, vectors.shape[0])
+        vec = vectors_of(whole, vectors.shape[0], count)
     else:
         whole = gather_pieces_of_all(whole, z)
-        vec = vectors_of(whole, vectors.shape[0])
+        vec = vectors_of(whole, vectors.shape[0], count)
         x_mine = to_chips(tokens, z)
-        x = both(x_mine)
+        x_other = swap(x_mine)
         grad_parts = [to_chip(cotangent, z, n) for n in range(count)]
-        merged = project(core_id, x, whole, vec.reshape(-1, PAIR))
+        merged = project(core_id, x_mine, x_other, whole, vec.reshape(-1, PAIR))
         heads_out, extra = attention_forward(merged, key_extra, 2 * rows, 0, HALF // PAIR)
     grad_out = jnp.concatenate(grad_parts, axis=0)
     bounds = [0, D, 2 * D, 3 * D, 3 * D + FF] + [(n + 4) * D + FF for n in range(6)]
@@ -831,7 +880,8 @@
     layer_out = from_chips(layer_out, z)
     d_merged = attention_backward(merged, extra, key_extra, heads_out, do, rows)
     d_merged, layer_out = lax.optimization_barrier((d_merged, layer_out))
-    grad_qkv = cols_dot(d_merged, x).astype(BF)
+    d_merged, x_mine, x_other = wait(d_merged, x_mine, x_other)
+    grad_qkv = cols_dot(d_merged, jnp.concatenate([x_mine, x_other], axis=0)).astype(BF)
     sums = jnp.sum(d_merged.astype(F32), axis=0).reshape(QUARTERS, 3, PAIR)
     vector_grad = jnp.concatenate(
         [
@@ -866,16 +916,12 @@
         axis=1,
     )
     if by_hand():
-        late, d_merged = wait(late, d_merged)
-        grad_tokens = from_chips(token_grads(d_merged, whole, grad_one), z)
-        late, sum_ff, grad_tokens = reduce_late(late, sum_ff, grad_tokens)
-        slab = late[4 * PAIR :]
-        chips = [late[: 3 * PAIR], slab, late[3 * PAIR : 4 * PAIR], sum_ff[: 2 * PAIR], slab]
-        chips += [sum_ff[2 * PAIR : 5 * PAIR], slab, sum_ff[5 * PAIR :], slab]
-        piece = lax.psum_scatter(
-            jnp.concatenate(chips, axis=0), "z", scatter_dimension=0, tiled=True
-        )
-        values = gather_pieces(piece)
+        late, d_merged, whole = wait(late, d_merged, whole)
+        grad_rows = token_grads(d_merged, whole, grad_one)
+        chips, parts, grad_rows = reduce_late(late, sum_ff, grad_rows)
+        piece = lax.psum_scatter(chips, "z", scatter_dimension=0, tiled=True)
+        piece, grad_rows, parts = wait(piece, grad_rows, parts)
+        values, grad_tokens = gather_pieces(piece, grad_rows, parts, z)
         start = jnp.where(core == 0, 2 * PAIR, 0)
         sent = jnp.stack(
             [lax.dynamic_slice_in_dim(value, start, PAIR, 0) for value in values[:3]]

time: 564 us -> 542 us (0.961)
  local copies, waits for them, and re-layouts: 63.4 us -> 43.7 us
    unnamed x128 -> x137, local copies, waits for them, and re-layouts: 23.3 us -> 11 us
    pallas_call x2 -> x1, Pallas kernels: 19.6 us -> 17.5 us  [attention_forward(): pl.pallas_call(forward_more_kernel if done else forward_kernel, grid=(pai...]
  transfers between devices with their start and end apart: 53 -> 53, of which waited for: 31 -> 30; matrix products, arithmetic and copies ran while one was open for 14% -> 13% of each run, Pallas kernels for 13% -> 13%
where the time goes in v4:
time: 542 us; the launch traced here: 535 us
  waiting for transfers between devices  203 us (37%)
  Pallas kernels  152 us (28%)
  starting transfers between devices  60.9 us (11%)
  local copies, waits for them, and re-layouts  43.7 us (8%)
  other arithmetic  42.4 us (8%)
  matrix products  17.1 us (3%)
  between operations  15.4 us (3%)
    ppermute x20, waiting for transfers between devices, across(): return lax.ppermute(value, 'dp', [(i, i ^ bit) for i in range(4)])  63.8 us
    reduce_scatter x1, waiting for transfers between devices, shards(): piece = lax.psum_scatter(chips, 'z', scatter_dimension=0, tiled=True)  60.9 us
    ppermute x7, waiting for transfers between devices, along_z(): return lax.ppermute(value, 'z', pairs)  33.6 us
    pallas_call x1, Pallas kernels, attention_backward(): pl.pallas_call(backward_kernel, grid=(HALF // PAIR, rows // step), in_spe...  30.5 us
    pallas_call x1, Pallas kernels, feed_backward(): pl.pallas_call(feed_backward_kernel, grid=(QUARTERS,), in_specs=[*[whole_...  29.1 us
    ppermute x6, waiting for transfers between devices, from_chip(): lax.ppermute(part, 'z', [(i, (i - shift) % count) for i in range(count)])  22.6 us
    ppermute x20, starting transfers between devices, across(): return lax.ppermute(value, 'dp', [(i, i ^ bit) for i in range(4)])  21.5 us
    pallas_call x1, Pallas kernels, feed_forward(): pl.pallas_call(feed_forward_kernel, grid=(QUARTERS,), in_specs=[SCALAR, w...  19 us
  transfers between devices with their start and end apart: 53, of which 30 were waited for; matrix products, arithmetic and copies ran while one was open for 13% of the time, Pallas kernels for 13%

profile of v4, /device:TPU:0, one launch (start us, length us, event | category | flops | bytes accessed | tf_op | source)
XLA Modules:
  0.0 535.0 jit_solution(1394588657714608976)
XLA Ops:
  7.3 5.9 %shard_map.168 = (bf16[1024,1024]{1,0:T(8,128)(2,1)}, bf16[512,1024]{1,0:T(8,128)(2,1)}) custom-call(s32[1]{0:T(128)} %bitcast.3.flag_ref, f32[1536,1024]{1,0:T(8,128)} %weight_ref.1, f32[1536,1024]{1,0:T(8,128)} %weight_ref.1), custom_call_target="tpu_custom_call" | custom-call | flops 1 | bytes 1 | tf_op jit(solution)/shard_map/pallas_call | solution.py:123
  13.6 3.7 collective-permute-start.2
  19.5 5.3 shard_map.169
  24.9 5.0 collective-permute-done.2
  34.7 15.8 %collective-permute-done.3 = bf16[400,1024]{1,0:T(8,128)(2,1)} collective-permute-done((bf16[400,1024]{1,0:T(8,128)(2,1)}, bf16[400,1024]{1,0:T(8,128)(2,1)}, u32[]{:S(2)}, u32[]{:S(2)}) %collective-permute-start.3) | collective-permute-done | bytes 819232 | tf_op jit(solution)/shard_map/ppermute | solution.py:281
  50.5 4.9 collective-permute-done.4
  61.4 13.2 %collective-permute-done.5.got_x = bf16[400,1024]{1,0:T(8,128)(2,1)S(1)} collective-permute-done((bf16[400,1024]{1,0:T(8,128)(2,1)S(1)}, bf16[400,1024]{1,0:T(8,128)(2,1)S(1)}, u32[]{:S(2)}, u32[]{:S(2)}) %collective-permute-start.5) | collective-permute-done | bytes 819232 | tf_op jit(solution)/shard_map/ppermute | solution.py:273
  75.8 8.1 %collective-permute-done.8 = bf16[400,1024]{1,0:T(8,128)(2,1)S(1)} collective-permute-done((bf16[400,1024]{1,0:T(8,128)(2,1)S(1)}, bf16[400,1024]{1,0:T(8,128)(2,1)S(1)}, u32[]{:S(2)}, u32[]{:S(2)}) %collective-permute-start.8) | collective-permute-done | bytes 819232 | tf_op jit(solution)/shard_map/ppermute | solution.py:281
  88.1 7.3 %collective-permute-done.9.far_a = bf16[400,512]{1,0:T(8,128)(2,1)} collective-permute-done((bf16[400,512]{1,0:T(8,128)(2,1)}, bf16[400,512]{1,0:T(8,128)(2,1)}, u32[]{:S(2)}, u32[]{:S(2)}) %collective-permute-start.9) | collective-permute-done | bytes 409632 | tf_op jit(solution)/shard_map/ppermute | solution.py:273
  103.9 4.8 shard_map.170.whole_in
  108.7 5.6 %collective-permute-done.12.got_x = bf16[400,1024]{1,0:T(8,128)(2,1)} collective-permute-done((bf16[400,1024]{1,0:T(8,128)(2,1)S(1)}, bf16[400,1024]{1,0:T(8,128)(2,1)}, u32[]{:S(2)}, u32[]{:S(2)}) %collective-permute-start.12) | collective-permute-done | bytes 819232 | tf_op jit(solution)/shard_map/ppermute | solution.py:273
  114.5 4.8 collective-permute-done.15
  123.6 5.8 %collective-permute-start.19 = (bf16[128,1024]{1,0:T(8,128)(2,1)S(1)}, bf16[128,1024]{1,0:T(8,128)(2,1)S(1)}, u32[]{:S(2)}, u32[]{:S(2)}) collective-permute-start(bf16[128,1024]{1,0:T(8,128)(2,1)S(1)} %get-tuple-element.313), channel_id=1, source_target_pairs={{0,6},{2,0},{4,2},{6,4},{1,7},{3,1},{5,3},{7,5},{8,14},{10,8},{12,... | collective-permute-start | bytes 786440 | tf_op jit(solution)/shard_map/ppermute | solution.py:68
  129.5 4.3 collective-permute-done.18
  141.6 4.8 shard_map.171.w_ref.whole_in
  151.3 8.0 %shard_map.172.q_ref.k_ref.v_ref = bf16[1024,1536]{1,0:T(8,128)(2,1)} custom-call(s32[1]{0:T(128)} %bitcast.2.core_ref, bf16[512,1024]{1,0:T(8,128)(2,1)} %copy-done.5, bf16[512,1024]{1,0:T(8,128)(2,1)} %collective-permute-done.22.x_other, bf16[16,400,1024]{2,1,0:T(8,128)(2,1)} %shard_map.171.w_ref.whole_in, f32[24,128]{1,0:T(8,128)} %reshape.336.vector_ref), custom_call_target="tpu_custom_call" | custom-call | flops 1 | bytes 1 | tf_op jit(solution)/shard_map/pallas_call | solution.py:461
  169.7 17.5 %shard_map.173 = (bf16[1024,512]{1,0:T(8,128)(2,1)}, bf16[1024,512]{1,0:T(8,128)(2,1)}) custom-call(bf16[1024,1536]{1,0:T(8,128)(2,1)} %shard_map.172.q_ref.k_ref.v_ref, bf16[1024,1536]{1,0:T(8,128)(2,1)} %shard_map.172.q_ref.k_ref.v_ref, bf16[1024,1536]{1,0:T(8,128)(2,1)} %shard_map.172.q_ref.k_ref.v_ref, bf16[1024,128]{1,0:T(8,128)(2,1)} %select_convert_fusion.key_ref), custom_call_target="tpu_custom_call" | custom-call | flops 1 | bytes 1 | tf_op jit(solution)/shard_map/pallas_call | solution.py:512
  187.3 4.8 shard_map.174.up0.up1.up2.down0.down1
  207.7 19.0 %shard_map.175 = (bf16[1024,2048]{1,0:T(8,128)(2,1)}, bf16[1024,2048]{1,0:T(8,128)(2,1)}, f32[512,1024]{1,0:T(8,128)}, bf16[512,1024]{1,0:T(8,128)(2,1)}) custom-call(s32[1]{0:T(128)} %bitcast.2.core_ref, bf16[512,1024]{1,0:T(8,128)(2,1)} %copy-done.4, bf16[512,1024]{1,0:T(8,128)(2,1)} %collective-permute-done.29.u_other, ...), custom_call_target="tpu_custom_call" | custom-call | flops 1 | bytes 1 | tf_op jit(solution)/shard_map/pallas_call | solution.py:647
  242.2 29.1 %shard_map.176 = (bf16[4,1024,1024]{2,1,0:T(8,128)(2,1)}, f32[1,2048]{1,0:T(1,128)}, f32[512,1024]{1,0:T(8,128)}, bf16[512,1024]{1,0:T(8,128)(2,1)}) custom-call(bf16[512,1024]{1,0:T(8,128)(2,1)} %copy-done.7, bf16[512,1024]{1,0:T(8,128)(2,1)} %copy-done.29, bf16[512,1024]{1,0:T(8,128)(2,1)} %copy-done.4, bf16[512,1024]{1,0:T(8,128)(2,1)} %collective-permute-done.29.u_other, ...), custom_call_target="tpu_custom_call" | custom-call | flops 1 | bytes 1 | tf_op jit(solution)/shard_map/pallas_call | solution.py:707
  274.4 4.7 multiply_reduce_fusion.1
  292.3 3.6 convolution_convert_fusion.1
  297.7 30.5 %shard_map.177 = bf16[1024,1536]{1,0:T(8,128)(2,1)} custom-call(bf16[1024,1536]{1,0:T(8,128)(2,1)} %shard_map.172.q_ref.k_ref.v_ref, bf16[1024,512]{1,0:T(8,128)(2,1)} %get-tuple-element.205.extra_ref, bf16[1024,1536]{1,0:T(8,128)(2,1)} %shard_map.172.q_ref.k_ref.v_ref, bf16[1024,1536]{1,0:T(8,128)(2,1)} %shard_map.172.q_ref.k_ref.v_ref, ...), custom_call_target="tpu_custom_call" | custom-call | flops 1 | bytes 1 | tf_op jit(solution)/shard_map/pallas_call | solution.py:576
  334.2 5.4 %convolution_convert_fusion = bf16[1536,1024]{1,0:T(8,128)(2,1)S(1)} fusion(bf16[1024,1536]{1,0:T(8,128)(2,1)S(1)} %copy-done.1, bf16[512,1024]{1,0:T(8,128)(2,1)} %collective-permute-done.22.x_other, bf16[512,1024]{1,0:T(8,128)(2,1)} %copy-done.5), kind=kOutput, calls=%fused_computation.4 | convolution fusion | flops 3226992640 | bytes 8388608 | tf_op jit(solution)/shard_map/dot_general | solution.py:35
  355.5 22.3 %collective-permute-done.37 = bf16[2,528,512]{2,1,0:T(8,128)(2,1)} collective-permute-done((bf16[2,528,512]{2,1,0:T(8,128)(2,1)}, bf16[2,528,512]{2,1,0:T(8,128)(2,1)}, u32[]{:S(2)}, u32[]{:S(2)}) %collective-permute-start.37) | collective-permute-done | bytes 1081376 | tf_op jit(solution)/shard_map/ppermute | solution.py:273
  386.4 6.4 %collective-permute-done.42 = bf16[128,1024]{1,0:T(8,128)(2,1)S(1)} collective-permute-done((bf16[128,1024]{1,0:T(8,128)(2,1)S(1)}, bf16[128,1024]{1,0:T(8,128)(2,1)S(1)}, u32[]{:S(2)}, u32[]{:S(2)}) %collective-permute-start.42) | collective-permute-done | bytes 262176 | tf_op jit(solution)/shard_map/ppermute | solution.py:80
  392.8 4.8 collective-permute-done.43
  401.9 4.1 shard_map.178
  406.0 60.9 %reduce-scatter.5.cloned.1.call-done.mine = bf16[400,1024]{1,0:T(8,128)(2,1)} async-done(((bf16[1600,1024]{1,0:T(8,128)(2,1)}), bf16[400,1024]{1,0:T(8,128)(2,1)}) %reduce-scatter.5.cloned.1.call-update) | async-done | bytes 819216 | tf_op jit(solution)/shard_map/reduce_scatter | solution.py:922
  472.5 11.4 %collective-permute-done.46 = bf16[128,1024]{1,0:T(8,128)(2,1)S(1)} collective-permute-done((bf16[128,1024]{1,0:T(8,128)(2,1)S(1)}, bf16[128,1024]{1,0:T(8,128)(2,1)S(1)}, u32[]{:S(2)}, u32[]{:S(2)}) %collective-permute-start.46) | collective-permute-done | bytes 262176 | tf_op jit(solution)/shard_map/ppermute | solution.py:80
  491.7 6.4 %collective-permute-done.47.far_a = bf16[400,512]{1,0:T(8,128)(2,1)S(1)} collective-permute-done((bf16[400,512]{1,0:T(8,128)(2,1)S(1)}, bf16[400,512]{1,0:T(8,128)(2,1)S(1)}, u32[]{:S(2)}, u32[]{:S(2)}) %collective-permute-start.47) | collective-permute-done | bytes 409632 | tf_op jit(solution)/shard_map/ppermute | solution.py:273
  509.8 18.3 %shard_map.179 = (f32[1536,1024]{1,0:T(8,128)}, f32[1536,1024]{1,0:T(8,128)}, f32[1536,1024]{1,0:T(8,128)}, f32[1536,1024]{1,0:T(8,128)}) custom-call(s32[3]{0:T(128)} %pad_add_fusion.4.where_ref, bf16[400,1024]{1,0:T(8,128)(2,1)} %reduce-scatter.5.cloned.1.call-done.mine, bf16[400,1024]{1,0:T(8,128)(2,1)} %copy-done.11, bf16[400,1024]{1,0:T(8,128)(2,1)} %copy-done.12, ...), custom_call_target="tpu_custom_call" | custom-call | flops 1 | bytes 1 | tf_op jit(solution)/shard_map/pallas_call | solution.py:410
  (350 shorter events, 163.1 us)
Async XLA Ops:
  7.2 370.6 %reduce-scatter.3.cloned.1.call-start = ((), (), s32[]{:S(2)}) async-start(), calls=%async_computation.2 | async-start | bytes 10485760 | tf_op jit(solution)/shard_map/reduce_scatter | solution.py:261
  13.6 16.2 %collective-permute-start.2 = (bf16[128,1024]{1,0:T(8,128)(2,1)S(1)}, bf16[128,1024]{1,0:T(8,128)(2,1)S(1)}, u32[]{:S(2)}, u32[]{:S(2)}) collective-permute-start(bf16[128,1024]{1,0:T(8,128)(2,1)S(1)} %get-tuple-element.315), channel_id=1, source_target_pairs={{0,4},{2,6},{4,0},{6,2},{1,5},{3,7},{5,1},{7,3},{8,12},{10,14},{12... | collective-permute-start | bytes 786440 | tf_op jit(solution)/shard_map/ppermute | solution.py:68
  29.9 20.7 %collective-permute-start.3 = (bf16[400,1024]{1,0:T(8,128)(2,1)}, bf16[400,1024]{1,0:T(8,128)(2,1)}, u32[]{:S(2)}, u32[]{:S(2)}) collective-permute-start(bf16[400,1024]{1,0:T(8,128)(2,1)} %get-tuple-element.146), channel_id=1, source_target_pairs={{0,2},{2,4},{4,6},{1,3},{3,5},{5,7},{8,10},{10,12},{12,14},{9,11},... | collective-permute-start | bytes 2457608 | tf_op jit(solution)/shard_map/ppermute | solution.py:281
  33.4 22.0 %collective-permute-start.4 = (bf16[400,1024]{1,0:T(8,128)(2,1)}, bf16[400,1024]{1,0:T(8,128)(2,1)S(1)}, u32[]{:S(2)}, u32[]{:S(2)}) collective-permute-start(bf16[400,1024]{1,0:T(8,128)(2,1)} %get-tuple-element.146), channel_id=1, source_target_pairs={{2,0},{4,2},{6,4},{3,1},{5,3},{7,5},{10,8},{12,10},{14,12},{11,9},... | collective-permute-start | bytes 2457608 | tf_op jit(solution)/shard_map/ppermute | solution.py:281
  55.5 19.1 %collective-permute-start.5 = (bf16[400,1024]{1,0:T(8,128)(2,1)S(1)}, bf16[400,1024]{1,0:T(8,128)(2,1)S(1)}, u32[]{:S(2)}, u32[]{:S(2)}) collective-permute-start(bf16[400,1024]{1,0:T(8,128)(2,1)S(1)} %broadcast_select_fusion.mine), channel_id=1, source_target_pairs={{0,8},{8,0},{16,24},{24,16},{1,9},{9,1},{17,25},{25,17},{2,10},{10... | collective-permute-start | bytes 2457608 | tf_op jit(solution)/shard_map/ppermute | solution.py:273
  57.1 18.7 %collective-permute-start.6 = (bf16[400,1024]{1,0:T(8,128)(2,1)S(1)}, bf16[400,1024]{1,0:T(8,128)(2,1)S(1)}, u32[]{:S(2)}, u32[]{:S(2)}) collective-permute-start(bf16[400,1024]{1,0:T(8,128)(2,1)S(1)} %broadcast_select_fusion.mine), channel_id=1, source_target_pairs={{0,16},{8,24},{16,0},{24,8},{1,17},{9,25},{17,1},{25,9},{2,18},{10... | collective-permute-start | bytes 2457608 | tf_op jit(solution)/shard_map/ppermute | solution.py:273
  58.6 17.2 %collective-permute-start.7 = (bf16[400,1024]{1,0:T(8,128)(2,1)}, bf16[400,1024]{1,0:T(8,128)(2,1)}, u32[]{:S(2)}, u32[]{:S(2)}) collective-permute-start(bf16[400,1024]{1,0:T(8,128)(2,1)} %collective-permute-done.3), channel_id=1, source_target_pairs={{2,4},{3,5},{10,12},{11,13},{18,20},{19,21},{26,28},{27,29}} | collective-permute-start | bytes 2457608 | tf_op jit(solution)/shard_map/ppermute | solution.py:281
  60.2 23.8 %collective-permute-start.8 = (bf16[400,1024]{1,0:T(8,128)(2,1)S(1)}, bf16[400,1024]{1,0:T(8,128)(2,1)S(1)}, u32[]{:S(2)}, u32[]{:S(2)}) collective-permute-start(bf16[400,1024]{1,0:T(8,128)(2,1)S(1)} %collective-permute-done.4), channel_id=1, source_target_pairs={{2,0},{4,2},{3,1},{5,3},{10,8},{12,10},{11,9},{13,11},{18,16},{20,... | collective-permute-start | bytes 2457608 | tf_op jit(solution)/shard_map/ppermute | solution.py:281
  97.8 16.6 %collective-permute-start.12 = (bf16[400,1024]{1,0:T(8,128)(2,1)S(1)}, bf16[400,1024]{1,0:T(8,128)(2,1)}, u32[]{:S(2)}, u32[]{:S(2)}) collective-permute-start(bf16[400,1024]{1,0:T(8,128)(2,1)S(1)} %select_select_fusion.1.mine), channel_id=1, source_target_pairs={{0,8},{8,0},{16,24},{24,16},{1,9},{9,1},{17,25},{25,17},{2,10},{10... | collective-permute-start | bytes 2457608 | tf_op jit(solution)/shard_map/ppermute | solution.py:273
  98.4 16.1 %collective-permute-start.13 = (bf16[400,1024]{1,0:T(8,128)(2,1)S(1)}, bf16[400,1024]{1,0:T(8,128)(2,1)S(1)}, u32[]{:S(2)}, u32[]{:S(2)}) collective-permute-start(bf16[400,1024]{1,0:T(8,128)(2,1)S(1)} %select_select_fusion.1.mine), channel_id=1, source_target_pairs={{0,16},{8,24},{16,0},{24,8},{1,17},{9,25},{17,1},{25,9},{2,18},{10... | collective-permute-start | bytes 2457608 | tf_op jit(solution)/shard_map/ppermute | solution.py:273
  99.9 14.6 %collective-permute-start.14 = (bf16[400,1024]{1,0:T(8,128)(2,1)}, bf16[400,1024]{1,0:T(8,128)(2,1)}, u32[]{:S(2)}, u32[]{:S(2)}) collective-permute-start(bf16[400,1024]{1,0:T(8,128)(2,1)} %collective-permute-done.3), channel_id=1, source_target_pairs={{4,6},{5,7},{12,14},{13,15},{20,22},{21,23},{28,30},{29,31}} | collective-permute-start | bytes 2457608 | tf_op jit(solution)/shard_map/ppermute | solution.py:281
  101.4 17.8 %collective-permute-start.15 = (bf16[400,1024]{1,0:T(8,128)(2,1)S(1)}, bf16[400,1024]{1,0:T(8,128)(2,1)}, u32[]{:S(2)}, u32[]{:S(2)}) collective-permute-start(bf16[400,1024]{1,0:T(8,128)(2,1)S(1)} %collective-permute-done.8), channel_id=1, source_target_pairs={{2,0},{3,1},{10,8},{11,9},{18,16},{19,17},{26,24},{27,25}} | collective-permute-start | bytes 2457608 | tf_op jit(solution)/shard_map/ppermute | solution.py:281
  120.3 14.9 %collective-permute-start.16 = (bf16[400,512]{1,0:T(8,128)(2,1)S(1)}, bf16[400,512]{1,0:T(8,128)(2,1)S(1)}, u32[]{:S(2)}, u32[]{:S(2)}) collective-permute-start(bf16[400,512]{1,0:T(8,128)(2,1)S(1)} %slice.163), channel_id=1, source_target_pairs={{0,16},{8,24},{16,0},{24,8},{1,17},{9,25},{17,1},{25,9},{2,18},{10... | collective-permute-start | bytes 1228808 | tf_op jit(solution)/shard_map/ppermute | solution.py:273
  120.9 14.3 %collective-permute-start.17 = (bf16[400,512]{1,0:T(8,128)(2,1)S(1)}, bf16[400,512]{1,0:T(8,128)(2,1)S(1)}, u32[]{:S(2)}, u32[]{:S(2)}) collective-permute-start(bf16[400,512]{1,0:T(8,128)(2,1)S(1)} %slice.164), channel_id=1, source_target_pairs={{0,8},{8,0},{16,24},{24,16},{1,9},{9,1},{17,25},{25,17},{2,10},{10... | collective-permute-start | bytes 1228808 | tf_op jit(solution)/shard_map/ppermute | solution.py:273
  136.0 15.3 %collective-permute-start.22 = (bf16[512,1024]{1,0:T(8,128)(2,1)S(1)}, bf16[512,1024]{1,0:T(8,128)(2,1)}, u32[]{:S(2)}, u32[]{:S(2)}) collective-permute-start(bf16[512,1024]{1,0:T(8,128)(2,1)S(1)} %constant_dynamic-update-slice_fusion.x_mine), channel_id=1, source_target_pairs={{0,1},{1,0},{2,3},{3,2},{4,5},{5,4},{6,7},{7,6},{8,9},{9,8},{10,11... | collective-permute-start | bytes 3145736 | tf_op jit(solution)/shard_map/ppermute | solution.py:43
  138.9 20.5 %collective-permute-start.20 = (bf16[400,1024]{1,0:T(8,128)(2,1)}, bf16[400,1024]{1,0:T(8,128)(2,1)S(1)}, u32[]{:S(2)}, u32[]{:S(2)}) collective-permute-start(bf16[400,1024]{1,0:T(8,128)(2,1)} %select_select_fusion.mine), channel_id=1, source_target_pairs={{0,8},{8,0},{16,24},{24,16},{1,9},{9,1},{17,25},{25,17},{2,10},{10... | collective-permute-start | bytes 2457608 | tf_op jit(solution)/shard_map/ppermute | solution.py:273
  139.4 20.2 %collective-permute-start.21 = (bf16[400,1024]{1,0:T(8,128)(2,1)}, bf16[400,1024]{1,0:T(8,128)(2,1)S(1)}, u32[]{:S(2)}, u32[]{:S(2)}) collective-permute-start(bf16[400,1024]{1,0:T(8,128)(2,1)} %select_select_fusion.mine), channel_id=1, source_target_pairs={{0,16},{8,24},{16,0},{24,8},{1,17},{9,25},{17,1},{25,9},{2,18},{10... | collective-permute-start | bytes 2457608 | tf_op jit(solution)/shard_map/ppermute | solution.py:273
  160.6 26.7 %collective-permute-start.24 = (bf16[400,512]{1,0:T(8,128)(2,1)}, bf16[400,512]{1,0:T(8,128)(2,1)}, u32[]{:S(2)}, u32[]{:S(2)}) collective-permute-start(bf16[400,512]{1,0:T(8,128)(2,1)} %slice.167), channel_id=1, source_target_pairs={{0,16},{8,24},{16,0},{24,8},{1,17},{9,25},{17,1},{25,9},{2,18},{10... | collective-permute-start | bytes 1228808 | tf_op jit(solution)/shard_map/ppermute | solution.py:273
  162.6 24.7 %collective-permute-start.25 = (bf16[400,512]{1,0:T(8,128)(2,1)}, bf16[400,512]{1,0:T(8,128)(2,1)}, u32[]{:S(2)}, u32[]{:S(2)}) collective-permute-start(bf16[400,512]{1,0:T(8,128)(2,1)} %slice.168), channel_id=1, source_target_pairs={{0,8},{8,0},{16,24},{24,16},{1,9},{9,1},{17,25},{25,17},{2,10},{10... | collective-permute-start | bytes 1228808 | tf_op jit(solution)/shard_map/ppermute | solution.py:273
  164.9 22.4 %collective-permute-start.26 = (bf16[128,1024]{1,0:T(8,128)(2,1)}, bf16[128,1024]{1,0:T(8,128)(2,1)S(1)}, u32[]{:S(2)}, u32[]{:S(2)}) collective-permute-start(bf16[128,1024]{1,0:T(8,128)(2,1)} %get-tuple-element.310), channel_id=1, source_target_pairs={{0,4},{2,6},{4,0},{6,2},{1,5},{3,7},{5,1},{7,3},{8,12},{10,14},{12... | collective-permute-start | bytes 786440 | tf_op jit(solution)/shard_map/ppermute | solution.py:68
  167.1 20.2 %collective-permute-start.27 = (bf16[128,1024]{1,0:T(8,128)(2,1)}, bf16[128,1024]{1,0:T(8,128)(2,1)S(1)}, u32[]{:S(2)}, u32[]{:S(2)}) collective-permute-start(bf16[128,1024]{1,0:T(8,128)(2,1)} %get-tuple-element.309), channel_id=1, source_target_pairs={{0,6},{2,0},{4,2},{6,4},{1,7},{3,1},{5,3},{7,5},{8,14},{10,8},{12,... | collective-permute-start | bytes 786440 | tf_op jit(solution)/shard_map/ppermute | solution.py:68
  271.4 195.5 %reduce-scatter.5.cloned.1.call-start = ((), (), s32[]{:S(2)}) async-start(), calls=%async_computation.3 | async-start | bytes 4096000 | tf_op jit(solution)/shard_map/reduce_scatter | solution.py:922
  288.7 39.5 %collective-permute-start.34 = (bf16[128,1024]{1,0:T(8,128)(2,1)S(1)}, bf16[128,1024]{1,0:T(8,128)(2,1)S(1)}, u32[]{:S(2)}, u32[]{:S(2)}) collective-permute-start(bf16[128,1024]{1,0:T(8,128)(2,1)S(1)} %get-tuple-element.308), channel_id=1, source_target_pairs={{0,6},{2,0},{4,2},{6,4},{1,7},{3,1},{5,3},{7,5},{8,14},{10,8},{12,... | collective-permute-start | bytes 786440 | tf_op jit(solution)/shard_map/ppermute | solution.py:80
  290.0 38.9 %collective-permute-start.35 = (bf16[128,1024]{1,0:T(8,128)(2,1)}, bf16[128,1024]{1,0:T(8,128)(2,1)}, u32[]{:S(2)}, u32[]{:S(2)}) collective-permute-start(bf16[128,1024]{1,0:T(8,128)(2,1)} %get-tuple-element.307), channel_id=1, source_target_pairs={{0,4},{2,6},{4,0},{6,2},{1,5},{3,7},{5,1},{7,3},{8,12},{10,14},{12... | collective-permute-start | bytes 786440 | tf_op jit(solution)/shard_map/ppermute | solution.py:80
  291.2 39.7 %collective-permute-start.36 = (bf16[128,1024]{1,0:T(8,128)(2,1)}, bf16[128,1024]{1,0:T(8,128)(2,1)S(1)}, u32[]{:S(2)}, u32[]{:S(2)}) collective-permute-start(bf16[128,1024]{1,0:T(8,128)(2,1)} %get-tuple-element.306), channel_id=1, source_target_pairs={{0,2},{2,4},{4,6},{6,0},{1,3},{3,5},{5,7},{7,1},{8,10},{10,12},{12... | collective-permute-start | bytes 786440 | tf_op jit(solution)/shard_map/ppermute | solution.py:80
  349.1 28.7 %collective-permute-start.37 = (bf16[2,528,512]{2,1,0:T(8,128)(2,1)}, bf16[2,528,512]{2,1,0:T(8,128)(2,1)}, u32[]{:S(2)}, u32[]{:S(2)}) collective-permute-start(bf16[2,528,512]{2,1,0:T(8,128)(2,1)} %dynamic-slice_bitcast_fusion.3), channel_id=1, source_target_pairs={{0,8},{8,0},{16,24},{24,16},{1,9},{9,1},{17,25},{25,17},{2,10},{10... | collective-permute-start | bytes 3244040 | tf_op jit(solution)/shard_map/ppermute | solution.py:273
  350.8 26.9 %collective-permute-start.38 = (bf16[2,528,512]{2,1,0:T(8,128)(2,1)}, bf16[2,528,512]{2,1,0:T(8,128)(2,1)}, u32[]{:S(2)}, u32[]{:S(2)}) collective-permute-start(bf16[2,528,512]{2,1,0:T(8,128)(2,1)} %dynamic-slice_bitcast_fusion.2), channel_id=1, source_target_pairs={{0,16},{8,24},{16,0},{24,8},{1,17},{9,25},{17,1},{25,9},{2,18},{10... | collective-permute-start | bytes 3244040 | tf_op jit(solution)/shard_map/ppermute | solution.py:273
  379.3 18.3 %collective-permute-start.40 = (bf16[528,512]{1,0:T(8,128)(2,1)S(1)}, bf16[528,512]{1,0:T(8,128)(2,1)S(1)}, u32[]{:S(2)}, u32[]{:S(2)}) collective-permute-start(bf16[528,512]{1,0:T(8,128)(2,1)S(1)} %fusion.15), channel_id=1, source_target_pairs={{0,16},{8,24},{16,0},{24,8},{1,17},{9,25},{17,1},{25,9},{2,18},{10... | collective-permute-start | bytes 1622024 | tf_op jit(solution)/shard_map/ppermute | solution.py:273
  382.0 15.6 %collective-permute-start.41 = (bf16[528,512]{1,0:T(8,128)(2,1)S(1)}, bf16[528,512]{1,0:T(8,128)(2,1)S(1)}, u32[]{:S(2)}, u32[]{:S(2)}) collective-permute-start(bf16[528,512]{1,0:T(8,128)(2,1)S(1)} %fusion.14), channel_id=1, source_target_pairs={{0,8},{8,0},{16,24},{24,16},{1,9},{9,1},{17,25},{25,17},{2,10},{10... | collective-permute-start | bytes 1622024 | tf_op jit(solution)/shard_map/ppermute | solution.py:273
  466.9 20.0 %collective-permute-start.44 = (bf16[400,1024]{1,0:T(8,128)(2,1)}, bf16[400,1024]{1,0:T(8,128)(2,1)S(1)}, u32[]{:S(2)}, u32[]{:S(2)}) collective-permute-start(bf16[400,1024]{1,0:T(8,128)(2,1)} %reduce-scatter.5.cloned.1.call-done.mine), channel_id=1, source_target_pairs={{0,8},{8,0},{16,24},{24,16},{1,9},{9,1},{17,25},{25,17},{2,10},{10... | collective-permute-start | bytes 2457608 | tf_op jit(solution)/shard_map/ppermute | solution.py:273
  468.4 19.7 %collective-permute-start.45 = (bf16[400,1024]{1,0:T(8,128)(2,1)}, bf16[400,1024]{1,0:T(8,128)(2,1)S(1)}, u32[]{:S(2)}, u32[]{:S(2)}) collective-permute-start(bf16[400,1024]{1,0:T(8,128)(2,1)} %reduce-scatter.5.cloned.1.call-done.mine), channel_id=1, source_target_pairs={{0,16},{8,24},{16,0},{24,8},{1,17},{9,25},{17,1},{25,9},{2,18},{10... | collective-permute-start | bytes 2457608 | tf_op jit(solution)/shard_map/ppermute | solution.py:273
  469.9 14.0 %collective-permute-start.46 = (bf16[128,1024]{1,0:T(8,128)(2,1)S(1)}, bf16[128,1024]{1,0:T(8,128)(2,1)S(1)}, u32[]{:S(2)}, u32[]{:S(2)}) collective-permute-start(bf16[128,1024]{1,0:T(8,128)(2,1)S(1)} %slice.198), channel_id=1, source_target_pairs={{0,4},{2,6},{4,0},{6,2},{1,5},{3,7},{5,1},{7,3},{8,12},{10,14},{12... | collective-permute-start | bytes 786440 | tf_op jit(solution)/shard_map/ppermute | solution.py:80
  (82 other events, 632.1 us)
Sparse Core Ops, SparseCore 0:
  271.5 87.3 reduce-scatter.2
  406.1 60.7 reduce-scatter.4

commit v5 on v4

--- a/solution.py
+++ b/solution.py
@@ -292,21 +292,27 @@
     return lax.optimization_barrier(values)
 
 
-def assemble_kernel(a_ref, b_ref, sums_ref, out_ref):
+def assemble_kernel(where_ref, a, got_a, far_a, b, got_b, far_b, sums_ref, out_ref):
     chip = pl.program_id(0)
     rows = 3 * PAIR
-    out_ref[rows:, :HALF] = a_ref[4 * PAIR :]
-    out_ref[rows:, HALF:] = b_ref[4 * PAIR :]
+
+    def write(target, source):
+        for index, (mine, got, far, columns) in enumerate(
+            ((a, got_a, far_a, slice(None, HALF)), (b, got_b, far_b, slice(HALF, None)))
+        ):
+            side = where_ref[index]
+            value = plus(plus(mine[side, source], got[side, source]), far[source])
+            out_ref[target, columns] = value
+
+    write(slice(rows, None), slice(4 * PAIR, None))
 
     @pl.when(chip == 0)
     def _():
-        out_ref[:rows, :HALF] = a_ref[:rows]
-        out_ref[:rows, HALF:] = b_ref[:rows]
+        write(slice(None, rows), slice(None, rows))
 
     @pl.when(chip == 1)
     def _():
-        out_ref[:PAIR, :HALF] = a_ref[rows : rows + PAIR]
-        out_ref[:PAIR, HALF:] = b_ref[rows : rows + PAIR]
+        write(slice(None, PAIR), slice(rows, rows + PAIR))
         out_ref[PAIR:rows] = sums_ref[: 2 * PAIR]
 
     @pl.when(chip == 2)
@@ -318,16 +324,16 @@
         out_ref[:rows] = sums_ref[5 * PAIR :]
 
 
-def assemble(a, b, sums):
+def assemble(x, y, late, sums):
     return pl.pallas_call(
         assemble_kernel,
         grid=(4,),
-        in_specs=[whole_block(item.shape) for item in (a, b, sums)],
+        in_specs=[SCALAR] + [whole_block(item.shape) for item in (*late, sums)],
         out_specs=pl.BlockSpec((PIECE, D), lambda chip: (chip, 0)),
         out_shape=jax.ShapeDtypeStruct((4 * PIECE, D), BF),
         cost_estimate=NO_COST,
         compiler_params=pltpu.CompilerParams(vmem_limit_bytes=VMEM),
-    )(a, b, sums)
+    )(jnp.stack([y, x]).astype(jnp.int32), *late, sums)
 
 
 def reduce_late(late, sum_ff, grad_rows):
@@ -340,20 +346,19 @@
     a, b = at(a, x, 1), at(b, y, 0)
     far_a = across(2, plus(at(a, 1 - y, 0), at(got_a, 1 - y, 0)))
     far_b = across(1, plus(at(b, 1 - x, 0), at(got_b, 1 - x, 0)))
-    parts = {n: from_chip(grad_rows, n) for n in (0, 1, 3)}
+    parts = {n: from_chip(grad_rows, n) for n in (0, 1)}
     far_a, far_b, a, b, parts, grad_rows = wait(far_a, far_b, a, b, parts, grad_rows)
-    a = plus(plus(at(a, y, 0), at(got_a, y, 0)), far_a)
-    b = plus(plus(at(b, x, 0), at(got_b, x, 0)), far_b)
-    return assemble(a, b, sum_ff), parts, grad_rows
+    return assemble(x, y, (a, got_a, far_a, b, got_b, far_b), sum_ff), parts, grad_rows
 
 
 def gather_pieces(piece, grad_rows, parts, z):
     got = across(1, piece), across(2, piece)
-    parts = {**parts, 2: from_chip(grad_rows, 2)}
+    parts = {**parts, **{n: from_chip(grad_rows, n) for n in (2, 3)}}
     got, piece, parts = wait(got, piece, parts)
     far = across(2, got[0][:, :HALF]), across(1, got[1][:, HALF:])
-    far, got, piece, parts = wait(far, got, piece, parts)
-    return (piece, *got, *far), put_together(parts, z)
+    grad_tokens = put_together(parts, z)
+    far, got, piece, grad_tokens = wait(far, got, piece, grad_tokens)
+    return (piece, *got, *far), grad_tokens
 
 
 def update_kernel(
@@ -662,6 +667,38 @@
         cost_estimate=NO_COST,
         compiler_params=pltpu.CompilerParams(vmem_limit_bytes=VMEM),
     )(core, u_mine, u_other, whole, whole, whole, whole, whole, vec)
+
+
+def out_forward_kernel(o_ref, w0, w1, w2, w3, mine_ref, other_ref):
+    part = plain_dot(o_ref[...], joined((w0, w1, w2, w3)))
+
+    @pl.when(pl.program_id(0) == 0)
+    def _():
+        mine_ref[...] = part
+
+    @pl.when(pl.program_id(0) == 1)
+    def _():
+        other_ref[...] = part.astype(BF)
+
+
+def out_forward(heads_out, whole):
+    rows = heads_out.shape[0]
+    half = (rows // 2, D)
+
+    def run(quarter):
+        return pl.BlockSpec((1, PAIR, D), lambda n: (QUARTERS + quarter, 0, 0))
+
+    return pl.pallas_call(
+        out_forward_kernel,
+        grid=(2,),
+        in_specs=[
+            pl.BlockSpec((rows // 2, HALF), lambda n: (n, 0)), *[run(q) for q in range(QUARTERS)]
+        ],
+        out_specs=[whole_block(half), whole_block(half)],
+        out_shape=[jax.ShapeDtypeStruct(half, F32), jax.ShapeDtypeStruct(half, BF)],
+        cost_estimate=NO_COST,
+        compiler_params=pltpu.CompilerParams(vmem_limit_bytes=VMEM),
+    )(heads_out, whole, whole, whole, whole)
 
 
 def feed_backward_kernel(
@@ -851,8 +888,9 @@
     vec = vec.reshape(-1, PAIR)
     w_out = whole[QUARTERS : 2 * QUARTERS, :PAIR].reshape(HALF, D)
 
+    branch, branch_other = out_forward(heads_out, whole)
     normed_in, normed_one, inverse_one = layer_norm(
-        x_mine.astype(F32) + share(plain_dot(heads_out, w_out)) + bias_o, gain_one, shift_one
+        x_mine.astype(F32) + branch + swap(branch_other).astype(F32) + bias_o, gain_one, shift_one
     )
     u_mine = normed_in.astype(BF)
     u_other = swap(u_mine)

time: 542 us -> 538 us (level)
  Pallas kernels: 152 us -> 158 us
    pallas_call x1 -> x2, Pallas kernels: 4.11 us -> 10.5 us  [the longest x1 5.77 us: assemble(): pl.pallas_call(assemble_kernel, grid=(4,), in_specs=[SCALAR] + [whole_blo...]
    unnamed x137 -> x131, local copies, waits for them, and re-layouts: 11 us -> 9.59 us
  transfers between devices with their start and end apart: 53 -> 53, of which waited for: 30 -> 30; matrix products, arithmetic and copies ran while one was open for 13% -> 12% of each run, Pallas kernels for 13% -> 13%
where the time goes in v5:
time: 538 us; the launch traced here: 531 us
  waiting for transfers between devices  207 us (38%)
  Pallas kernels  158 us (29%)
  starting transfers between devices  59.3 us (11%)
  local copies, waits for them, and re-layouts  39.6 us (7%)
  other arithmetic  37.8 us (7%)
  between operations  15.3 us (3%)
  matrix products  13.4 us (2%)
    ppermute x20, waiting for transfers between devices, across(): return lax.ppermute(value, 'dp', [(i, i ^ bit) for i in range(4)])  68.3 us
    reduce_scatter x1, waiting for transfers between devices, shards(): piece = lax.psum_scatter(chips, 'z', scatter_dimension=0, tiled=True)  62.3 us
    ppermute x7, waiting for transfers between devices, along_z(): return lax.ppermute(value, 'z', pairs)  32.6 us
    pallas_call x1, Pallas kernels, attention_backward(): pl.pallas_call(backward_kernel, grid=(HALF // PAIR, rows // step), in_spe...  30.5 us
    pallas_call x1, Pallas kernels, feed_backward(): pl.pallas_call(feed_backward_kernel, grid=(QUARTERS,), in_specs=[*[whole_...  29.1 us
    ppermute x20, starting transfers between devices, across(): return lax.ppermute(value, 'dp', [(i, i ^ bit) for i in range(4)])  20 us
    ppermute x6, waiting for transfers between devices, from_chip(): lax.ppermute(part, 'z', [(i, (i - shift) % count) for i in range(count)])  19.4 us
    pallas_call x1, Pallas kernels, feed_forward(): pl.pallas_call(feed_forward_kernel, grid=(QUARTERS,), in_specs=[SCALAR, w...  19 us
  transfers between devices with their start and end apart: 53, of which 30 were waited for; matrix products, arithmetic and copies ran while one was open for 12% of the time, Pallas kernels for 13%

profile of v5, /device:TPU:0, one launch (start us, length us, event | category | flops | bytes accessed | tf_op | source)
XLA Modules:
  0.0 530.9 jit_solution(13115852664068207763)
XLA Ops:
  7.3 5.9 %shard_map.168 = (bf16[1024,1024]{1,0:T(8,128)(2,1)}, bf16[512,1024]{1,0:T(8,128)(2,1)}) custom-call(s32[1]{0:T(128)} %bitcast.3.flag_ref, f32[1536,1024]{1,0:T(8,128)} %weight_ref.1, f32[1536,1024]{1,0:T(8,128)} %weight_ref.1), custom_call_target="tpu_custom_call" | custom-call | flops 1 | bytes 1 | tf_op jit(solution)/shard_map/pallas_call | solution.py:123
  13.6 3.7 collective-permute-start.2
  19.6 5.3 shard_map.169
  24.8 5.0 collective-permute-done.2
  29.9 3.6 collective-permute-start.3
  34.7 15.8 %collective-permute-done.3 = bf16[400,1024]{1,0:T(8,128)(2,1)} collective-permute-done((bf16[400,1024]{1,0:T(8,128)(2,1)}, bf16[400,1024]{1,0:T(8,128)(2,1)}, u32[]{:S(2)}, u32[]{:S(2)}) %collective-permute-start.3) | collective-permute-done | bytes 819232 | tf_op jit(solution)/shard_map/ppermute | solution.py:281
  50.5 4.9 collective-permute-done.4
  61.4 13.2 %collective-permute-done.5.got_x = bf16[400,1024]{1,0:T(8,128)(2,1)S(1)} collective-permute-done((bf16[400,1024]{1,0:T(8,128)(2,1)S(1)}, bf16[400,1024]{1,0:T(8,128)(2,1)S(1)}, u32[]{:S(2)}, u32[]{:S(2)}) %collective-permute-start.5) | collective-permute-done | bytes 819232 | tf_op jit(solution)/shard_map/ppermute | solution.py:273
  75.8 8.1 %collective-permute-done.8 = bf16[400,1024]{1,0:T(8,128)(2,1)S(1)} collective-permute-done((bf16[400,1024]{1,0:T(8,128)(2,1)S(1)}, bf16[400,1024]{1,0:T(8,128)(2,1)S(1)}, u32[]{:S(2)}, u32[]{:S(2)}) %collective-permute-start.8) | collective-permute-done | bytes 819232 | tf_op jit(solution)/shard_map/ppermute | solution.py:281
  88.1 7.3 %collective-permute-done.10.far_b = bf16[400,512]{1,0:T(8,128)(2,1)} collective-permute-done((bf16[400,512]{1,0:T(8,128)(2,1)}, bf16[400,512]{1,0:T(8,128)(2,1)}, u32[]{:S(2)}, u32[]{:S(2)}) %collective-permute-start.10) | collective-permute-done | bytes 409632 | tf_op jit(solution)/shard_map/ppermute | solution.py:273
  103.4 4.8 shard_map.170.whole_in
  108.2 6.2 %collective-permute-done.12.got_x = bf16[400,1024]{1,0:T(8,128)(2,1)} collective-permute-done((bf16[400,1024]{1,0:T(8,128)(2,1)S(1)}, bf16[400,1024]{1,0:T(8,128)(2,1)}, u32[]{:S(2)}, u32[]{:S(2)}) %collective-permute-start.12) | collective-permute-done | bytes 819232 | tf_op jit(solution)/shard_map/ppermute | solution.py:273
  115.5 3.8 collective-permute-done.15
  123.6 5.8 %collective-permute-start.19 = (bf16[128,1024]{1,0:T(8,128)(2,1)S(1)}, bf16[128,1024]{1,0:T(8,128)(2,1)S(1)}, u32[]{:S(2)}, u32[]{:S(2)}) collective-permute-start(bf16[128,1024]{1,0:T(8,128)(2,1)S(1)} %get-tuple-element.308), channel_id=1, source_target_pairs={{0,6},{2,0},{4,2},{6,4},{1,7},{3,1},{5,3},{7,5},{8,14},{10,8},{12,... | collective-permute-start | bytes 786440 | tf_op jit(solution)/shard_map/ppermute | solution.py:68
  129.5 4.4 collective-permute-done.18
  141.7 4.8 shard_map.171.w_ref.whole_in
  151.4 8.0 %shard_map.172.q_ref.k_ref.v_ref = bf16[1024,1536]{1,0:T(8,128)(2,1)} custom-call(s32[1]{0:T(128)} %bitcast.2.core_ref, bf16[512,1024]{1,0:T(8,128)(2,1)} %copy-done.5, bf16[512,1024]{1,0:T(8,128)(2,1)} %collective-permute-done.22.x_other, bf16[16,400,1024]{2,1,0:T(8,128)(2,1)} %shard_map.171.w_ref.whole_in, f32[24,128]{1,0:T(8,128)} %reshape.324.vector_ref), custom_call_target="tpu_custom_call" | custom-call | flops 1 | bytes 1 | tf_op jit(solution)/shard_map/pallas_call | solution.py:466
  169.7 17.5 %shard_map.173 = (bf16[1024,512]{1,0:T(8,128)(2,1)}, bf16[1024,512]{1,0:T(8,128)(2,1)}) custom-call(bf16[1024,1536]{1,0:T(8,128)(2,1)} %shard_map.172.q_ref.k_ref.v_ref, bf16[1024,1536]{1,0:T(8,128)(2,1)} %shard_map.172.q_ref.k_ref.v_ref, bf16[1024,1536]{1,0:T(8,128)(2,1)} %shard_map.172.q_ref.k_ref.v_ref, bf16[1024,128]{1,0:T(8,128)(2,1)} %select_convert_fusion.key_ref), custom_call_target="tpu_custom_call" | custom-call | flops 1 | bytes 1 | tf_op jit(solution)/shard_map/pallas_call | solution.py:517
  187.3 4.8 shard_map.174.w0.w1.w2.w3.up0.up1.up2.down0.down1
  192.1 4.7 shard_map.175
  206.8 19.0 %shard_map.176 = (bf16[1024,2048]{1,0:T(8,128)(2,1)}, bf16[1024,2048]{1,0:T(8,128)(2,1)}, f32[512,1024]{1,0:T(8,128)}, bf16[512,1024]{1,0:T(8,128)(2,1)}) custom-call(s32[1]{0:T(128)} %bitcast.2.core_ref, bf16[512,1024]{1,0:T(8,128)(2,1)} %copy-done.4, bf16[512,1024]{1,0:T(8,128)(2,1)} %collective-permute-done.29.u_other, ...), custom_call_target="tpu_custom_call" | custom-call | flops 1 | bytes 1 | tf_op jit(solution)/shard_map/pallas_call | solution.py:652
  241.3 29.1 %shard_map.177 = (bf16[4,1024,1024]{2,1,0:T(8,128)(2,1)}, f32[1,2048]{1,0:T(1,128)}, f32[512,1024]{1,0:T(8,128)}, bf16[512,1024]{1,0:T(8,128)(2,1)}) custom-call(bf16[512,1024]{1,0:T(8,128)(2,1)} %copy-done.7, bf16[512,1024]{1,0:T(8,128)(2,1)} %copy-done.29, bf16[512,1024]{1,0:T(8,128)(2,1)} %copy-done.4, bf16[512,1024]{1,0:T(8,128)(2,1)} %collective-permute-done.29.u_other, ...), custom_call_target="tpu_custom_call" | custom-call | flops 1 | bytes 1 | tf_op jit(solution)/shard_map/pallas_call | solution.py:744
  273.5 4.7 multiply_reduce_fusion.1
  293.9 30.5 %shard_map.178 = bf16[1024,1536]{1,0:T(8,128)(2,1)} custom-call(bf16[1024,1536]{1,0:T(8,128)(2,1)} %shard_map.172.q_ref.k_ref.v_ref, bf16[1024,512]{1,0:T(8,128)(2,1)} %get-tuple-element.202.extra_ref, bf16[1024,1536]{1,0:T(8,128)(2,1)} %shard_map.172.q_ref.k_ref.v_ref, bf16[1024,1536]{1,0:T(8,128)(2,1)} %shard_map.172.q_ref.k_ref.v_ref, ...), custom_call_target="tpu_custom_call" | custom-call | flops 1 | bytes 1 | tf_op jit(solution)/shard_map/pallas_call | solution.py:581
  330.9 5.4 %convolution_convert_fusion = bf16[1536,1024]{1,0:T(8,128)(2,1)S(1)} fusion(bf16[1024,1536]{1,0:T(8,128)(2,1)S(1)} %copy-done.1, bf16[512,1024]{1,0:T(8,128)(2,1)} %collective-permute-done.22.x_other, bf16[512,1024]{1,0:T(8,128)(2,1)} %copy-done.5), kind=kOutput, calls=%fused_computation.4 | convolution fusion | flops 3226992640 | bytes 8388608 | tf_op jit(solution)/shard_map/dot_general | solution.py:35
  351.4 25.4 %collective-permute-done.38.got_b = bf16[2,528,512]{2,1,0:T(8,128)(2,1)} collective-permute-done((bf16[2,528,512]{2,1,0:T(8,128)(2,1)}, bf16[2,528,512]{2,1,0:T(8,128)(2,1)}, u32[]{:S(2)}, u32[]{:S(2)}) %collective-permute-start.38) | collective-permute-done | bytes 1081376 | tf_op jit(solution)/shard_map/ppermute | solution.py:273
  382.3 3.6 collective-permute-start.42
  395.6 5.8 %shard_map.179 = bf16[1600,1024]{1,0:T(8,128)(2,1)} custom-call(s32[2]{0:T(128)} %pad_add_fusion.4.where_ref, bf16[2,528,512]{2,1,0:T(8,128)(2,1)} %dynamic-slice_bitcast_fusion.1.a, bf16[2,528,512]{2,1,0:T(8,128)(2,1)} %collective-permute-done.37.got_a, bf16[528,512]{1,0:T(8,128)(2,1)} %copy-done.40, bf16[2,528,512]{2,1,0:T(8,128)(2,1)} %dynamic-slice_bitcast_fusion.b, ...), custom_call_target="tpu_custom_call" | custom-call | flops 1 | bytes 1 | tf_op jit(solution)/shard_map/pallas_call | solution.py:328
  401.4 62.3 %reduce-scatter.5.cloned.1.call-done.mine = bf16[400,1024]{1,0:T(8,128)(2,1)} async-done(((bf16[1600,1024]{1,0:T(8,128)(2,1)}), bf16[400,1024]{1,0:T(8,128)(2,1)}) %reduce-scatter.5.cloned.1.call-update) | async-done | bytes 819216 | tf_op jit(solution)/shard_map/reduce_scatter | solution.py:960
  470.4 16.8 %collective-permute-done.45 = bf16[128,1024]{1,0:T(8,128)(2,1)S(1)} collective-permute-done((bf16[128,1024]{1,0:T(8,128)(2,1)}, bf16[128,1024]{1,0:T(8,128)(2,1)S(1)}, u32[]{:S(2)}, u32[]{:S(2)}) %collective-permute-start.45) | collective-permute-done | bytes 262176 | tf_op jit(solution)/shard_map/ppermute | solution.py:80
  490.5 8.3 %collective-permute-done.47.far_a = bf16[400,512]{1,0:T(8,128)(2,1)S(1)} collective-permute-done((bf16[400,512]{1,0:T(8,128)(2,1)S(1)}, bf16[400,512]{1,0:T(8,128)(2,1)S(1)}, u32[]{:S(2)}, u32[]{:S(2)}) %collective-permute-start.47) | collective-permute-done | bytes 409632 | tf_op jit(solution)/shard_map/ppermute | solution.py:273
  505.6 18.3 %shard_map.180 = (f32[1536,1024]{1,0:T(8,128)}, f32[1536,1024]{1,0:T(8,128)}, f32[1536,1024]{1,0:T(8,128)}, f32[1536,1024]{1,0:T(8,128)}) custom-call(s32[3]{0:T(128)} %pad_add_fusion.5.where_ref, bf16[400,1024]{1,0:T(8,128)(2,1)} %reduce-scatter.5.cloned.1.call-done.mine, bf16[400,1024]{1,0:T(8,128)(2,1)} %copy-done.12, bf16[400,1024]{1,0:T(8,128)(2,1)} %copy-done.13, ...), custom_call_target="tpu_custom_call" | custom-call | flops 1 | bytes 1 | tf_op jit(solution)/shard_map/pallas_call | solution.py:415
  (342 shorter events, 149.1 us)
Async XLA Ops:
  7.2 369.7 %reduce-scatter.3.cloned.1.call-start = ((), (), s32[]{:S(2)}) async-start(), calls=%async_computation.2 | async-start | bytes 10485760 | tf_op jit(solution)/shard_map/reduce_scatter | solution.py:261
  13.6 16.2 %collective-permute-start.2 = (bf16[128,1024]{1,0:T(8,128)(2,1)S(1)}, bf16[128,1024]{1,0:T(8,128)(2,1)S(1)}, u32[]{:S(2)}, u32[]{:S(2)}) collective-permute-start(bf16[128,1024]{1,0:T(8,128)(2,1)S(1)} %get-tuple-element.310), channel_id=1, source_target_pairs={{0,4},{2,6},{4,0},{6,2},{1,5},{3,7},{5,1},{7,3},{8,12},{10,14},{12... | collective-permute-start | bytes 786440 | tf_op jit(solution)/shard_map/ppermute | solution.py:68
  29.9 20.7 %collective-permute-start.3 = (bf16[400,1024]{1,0:T(8,128)(2,1)}, bf16[400,1024]{1,0:T(8,128)(2,1)}, u32[]{:S(2)}, u32[]{:S(2)}) collective-permute-start(bf16[400,1024]{1,0:T(8,128)(2,1)} %get-tuple-element.143), channel_id=1, source_target_pairs={{0,2},{2,4},{4,6},{1,3},{3,5},{5,7},{8,10},{10,12},{12,14},{9,11},... | collective-permute-start | bytes 2457608 | tf_op jit(solution)/shard_map/ppermute | solution.py:281
  33.4 22.0 %collective-permute-start.4 = (bf16[400,1024]{1,0:T(8,128)(2,1)}, bf16[400,1024]{1,0:T(8,128)(2,1)S(1)}, u32[]{:S(2)}, u32[]{:S(2)}) collective-permute-start(bf16[400,1024]{1,0:T(8,128)(2,1)} %get-tuple-element.143), channel_id=1, source_target_pairs={{2,0},{4,2},{6,4},{3,1},{5,3},{7,5},{10,8},{12,10},{14,12},{11,9},... | collective-permute-start | bytes 2457608 | tf_op jit(solution)/shard_map/ppermute | solution.py:281
  55.5 19.1 %collective-permute-start.5 = (bf16[400,1024]{1,0:T(8,128)(2,1)S(1)}, bf16[400,1024]{1,0:T(8,128)(2,1)S(1)}, u32[]{:S(2)}, u32[]{:S(2)}) collective-permute-start(bf16[400,1024]{1,0:T(8,128)(2,1)S(1)} %broadcast_select_fusion.mine), channel_id=1, source_target_pairs={{0,8},{8,0},{16,24},{24,16},{1,9},{9,1},{17,25},{25,17},{2,10},{10... | collective-permute-start | bytes 2457608 | tf_op jit(solution)/shard_map/ppermute | solution.py:273
  57.1 18.7 %collective-permute-start.6 = (bf16[400,1024]{1,0:T(8,128)(2,1)S(1)}, bf16[400,1024]{1,0:T(8,128)(2,1)S(1)}, u32[]{:S(2)}, u32[]{:S(2)}) collective-permute-start(bf16[400,1024]{1,0:T(8,128)(2,1)S(1)} %broadcast_select_fusion.mine), channel_id=1, source_target_pairs={{0,16},{8,24},{16,0},{24,8},{1,17},{9,25},{17,1},{25,9},{2,18},{10... | collective-permute-start | bytes 2457608 | tf_op jit(solution)/shard_map/ppermute | solution.py:273
  58.6 17.2 %collective-permute-start.7 = (bf16[400,1024]{1,0:T(8,128)(2,1)}, bf16[400,1024]{1,0:T(8,128)(2,1)}, u32[]{:S(2)}, u32[]{:S(2)}) collective-permute-start(bf16[400,1024]{1,0:T(8,128)(2,1)} %collective-permute-done.3), channel_id=1, source_target_pairs={{2,4},{3,5},{10,12},{11,13},{18,20},{19,21},{26,28},{27,29}} | collective-permute-start | bytes 2457608 | tf_op jit(solution)/shard_map/ppermute | solution.py:281
  60.2 23.8 %collective-permute-start.8 = (bf16[400,1024]{1,0:T(8,128)(2,1)S(1)}, bf16[400,1024]{1,0:T(8,128)(2,1)S(1)}, u32[]{:S(2)}, u32[]{:S(2)}) collective-permute-start(bf16[400,1024]{1,0:T(8,128)(2,1)S(1)} %collective-permute-done.4), channel_id=1, source_target_pairs={{2,0},{4,2},{3,1},{5,3},{10,8},{12,10},{11,9},{13,11},{18,16},{20,... | collective-permute-start | bytes 2457608 | tf_op jit(solution)/shard_map/ppermute | solution.py:281
  97.8 16.6 %collective-permute-start.12 = (bf16[400,1024]{1,0:T(8,128)(2,1)S(1)}, bf16[400,1024]{1,0:T(8,128)(2,1)}, u32[]{:S(2)}, u32[]{:S(2)}) collective-permute-start(bf16[400,1024]{1,0:T(8,128)(2,1)S(1)} %select_select_fusion.1.mine), channel_id=1, source_target_pairs={{0,8},{8,0},{16,24},{24,16},{1,9},{9,1},{17,25},{25,17},{2,10},{10... | collective-permute-start | bytes 2457608 | tf_op jit(solution)/shard_map/ppermute | solution.py:273
  99.3 16.1 %collective-permute-start.13 = (bf16[400,1024]{1,0:T(8,128)(2,1)S(1)}, bf16[400,1024]{1,0:T(8,128)(2,1)S(1)}, u32[]{:S(2)}, u32[]{:S(2)}) collective-permute-start(bf16[400,1024]{1,0:T(8,128)(2,1)S(1)} %select_select_fusion.1.mine), channel_id=1, source_target_pairs={{0,16},{8,24},{16,0},{24,8},{1,17},{9,25},{17,1},{25,9},{2,18},{10... | collective-permute-start | bytes 2457608 | tf_op jit(solution)/shard_map/ppermute | solution.py:273
  99.9 15.6 %collective-permute-start.14 = (bf16[400,1024]{1,0:T(8,128)(2,1)}, bf16[400,1024]{1,0:T(8,128)(2,1)}, u32[]{:S(2)}, u32[]{:S(2)}) collective-permute-start(bf16[400,1024]{1,0:T(8,128)(2,1)} %collective-permute-done.3), channel_id=1, source_target_pairs={{4,6},{5,7},{12,14},{13,15},{20,22},{21,23},{28,30},{29,31}} | collective-permute-start | bytes 2457608 | tf_op jit(solution)/shard_map/ppermute | solution.py:281
  101.4 17.8 %collective-permute-start.15 = (bf16[400,1024]{1,0:T(8,128)(2,1)S(1)}, bf16[400,1024]{1,0:T(8,128)(2,1)}, u32[]{:S(2)}, u32[]{:S(2)}) collective-permute-start(bf16[400,1024]{1,0:T(8,128)(2,1)S(1)} %collective-permute-done.8), channel_id=1, source_target_pairs={{2,0},{3,1},{10,8},{11,9},{18,16},{19,17},{26,24},{27,25}} | collective-permute-start | bytes 2457608 | tf_op jit(solution)/shard_map/ppermute | solution.py:281
  120.2 14.9 %collective-permute-start.16 = (bf16[400,512]{1,0:T(8,128)(2,1)S(1)}, bf16[400,512]{1,0:T(8,128)(2,1)S(1)}, u32[]{:S(2)}, u32[]{:S(2)}) collective-permute-start(bf16[400,512]{1,0:T(8,128)(2,1)S(1)} %slice.156), channel_id=1, source_target_pairs={{0,16},{8,24},{16,0},{24,8},{1,17},{9,25},{17,1},{25,9},{2,18},{10... | collective-permute-start | bytes 1228808 | tf_op jit(solution)/shard_map/ppermute | solution.py:273
  136.0 15.4 %collective-permute-start.22 = (bf16[512,1024]{1,0:T(8,128)(2,1)S(1)}, bf16[512,1024]{1,0:T(8,128)(2,1)}, u32[]{:S(2)}, u32[]{:S(2)}) collective-permute-start(bf16[512,1024]{1,0:T(8,128)(2,1)S(1)} %constant_dynamic-update-slice_fusion.x_mine), channel_id=1, source_target_pairs={{0,1},{1,0},{2,3},{3,2},{4,5},{5,4},{6,7},{7,6},{8,9},{9,8},{10,11... | collective-permute-start | bytes 3145736 | tf_op jit(solution)/shard_map/ppermute | solution.py:43
  138.8 20.6 %collective-permute-start.20 = (bf16[400,1024]{1,0:T(8,128)(2,1)}, bf16[400,1024]{1,0:T(8,128)(2,1)S(1)}, u32[]{:S(2)}, u32[]{:S(2)}) collective-permute-start(bf16[400,1024]{1,0:T(8,128)(2,1)} %select_select_fusion.mine), channel_id=1, source_target_pairs={{0,8},{8,0},{16,24},{24,16},{1,9},{9,1},{17,25},{25,17},{2,10},{10... | collective-permute-start | bytes 2457608 | tf_op jit(solution)/shard_map/ppermute | solution.py:273
  139.4 20.2 %collective-permute-start.21 = (bf16[400,1024]{1,0:T(8,128)(2,1)}, bf16[400,1024]{1,0:T(8,128)(2,1)S(1)}, u32[]{:S(2)}, u32[]{:S(2)}) collective-permute-start(bf16[400,1024]{1,0:T(8,128)(2,1)} %select_select_fusion.mine), channel_id=1, source_target_pairs={{0,16},{8,24},{16,0},{24,8},{1,17},{9,25},{17,1},{25,9},{2,18},{10... | collective-permute-start | bytes 2457608 | tf_op jit(solution)/shard_map/ppermute | solution.py:273
  160.5 26.8 %collective-permute-start.24 = (bf16[400,512]{1,0:T(8,128)(2,1)}, bf16[400,512]{1,0:T(8,128)(2,1)}, u32[]{:S(2)}, u32[]{:S(2)}) collective-permute-start(bf16[400,512]{1,0:T(8,128)(2,1)} %slice.160), channel_id=1, source_target_pairs={{0,16},{8,24},{16,0},{24,8},{1,17},{9,25},{17,1},{25,9},{2,18},{10... | collective-permute-start | bytes 1228808 | tf_op jit(solution)/shard_map/ppermute | solution.py:273
  162.6 24.7 %collective-permute-start.25 = (bf16[400,512]{1,0:T(8,128)(2,1)}, bf16[400,512]{1,0:T(8,128)(2,1)}, u32[]{:S(2)}, u32[]{:S(2)}) collective-permute-start(bf16[400,512]{1,0:T(8,128)(2,1)} %slice.161), channel_id=1, source_target_pairs={{0,8},{8,0},{16,24},{24,16},{1,9},{9,1},{17,25},{25,17},{2,10},{10... | collective-permute-start | bytes 1228808 | tf_op jit(solution)/shard_map/ppermute | solution.py:273
  165.0 22.3 %collective-permute-start.26 = (bf16[128,1024]{1,0:T(8,128)(2,1)}, bf16[128,1024]{1,0:T(8,128)(2,1)S(1)}, u32[]{:S(2)}, u32[]{:S(2)}) collective-permute-start(bf16[128,1024]{1,0:T(8,128)(2,1)} %get-tuple-element.305), channel_id=1, source_target_pairs={{0,4},{2,6},{4,0},{6,2},{1,5},{3,7},{5,1},{7,3},{8,12},{10,14},{12... | collective-permute-start | bytes 786440 | tf_op jit(solution)/shard_map/ppermute | solution.py:68
  167.1 20.2 %collective-permute-start.27 = (bf16[128,1024]{1,0:T(8,128)(2,1)}, bf16[128,1024]{1,0:T(8,128)(2,1)S(1)}, u32[]{:S(2)}, u32[]{:S(2)}) collective-permute-start(bf16[128,1024]{1,0:T(8,128)(2,1)} %get-tuple-element.304), channel_id=1, source_target_pairs={{0,6},{2,0},{4,2},{6,4},{1,7},{3,1},{5,3},{7,5},{8,14},{10,8},{12,... | collective-permute-start | bytes 786440 | tf_op jit(solution)/shard_map/ppermute | solution.py:68
  270.5 193.2 %reduce-scatter.5.cloned.1.call-start = ((), (), s32[]{:S(2)}) async-start(), calls=%async_computation.3 | async-start | bytes 4096000 | tf_op jit(solution)/shard_map/reduce_scatter | solution.py:960
  286.0 38.5 %collective-permute-start.34 = (bf16[128,1024]{1,0:T(8,128)(2,1)S(1)}, bf16[128,1024]{1,0:T(8,128)(2,1)S(1)}, u32[]{:S(2)}, u32[]{:S(2)}) collective-permute-start(bf16[128,1024]{1,0:T(8,128)(2,1)S(1)} %get-tuple-element.303), channel_id=1, source_target_pairs={{0,6},{2,0},{4,2},{6,4},{1,7},{3,1},{5,3},{7,5},{8,14},{10,8},{12,... | collective-permute-start | bytes 786440 | tf_op jit(solution)/shard_map/ppermute | solution.py:80
  287.2 37.9 %collective-permute-start.35 = (bf16[128,1024]{1,0:T(8,128)(2,1)}, bf16[128,1024]{1,0:T(8,128)(2,1)}, u32[]{:S(2)}, u32[]{:S(2)}) collective-permute-start(bf16[128,1024]{1,0:T(8,128)(2,1)} %get-tuple-element.302), channel_id=1, source_target_pairs={{0,4},{2,6},{4,0},{6,2},{1,5},{3,7},{5,1},{7,3},{8,12},{10,14},{12... | collective-permute-start | bytes 786440 | tf_op jit(solution)/shard_map/ppermute | solution.py:80
  288.5 38.5 %collective-permute-start.36 = (bf16[128,1024]{1,0:T(8,128)(2,1)}, bf16[128,1024]{1,0:T(8,128)(2,1)S(1)}, u32[]{:S(2)}, u32[]{:S(2)}) collective-permute-start(bf16[128,1024]{1,0:T(8,128)(2,1)} %get-tuple-element.301), channel_id=1, source_target_pairs={{0,2},{2,4},{4,6},{6,0},{1,3},{3,5},{5,7},{7,1},{8,10},{10,12},{12... | collective-permute-start | bytes 786440 | tf_op jit(solution)/shard_map/ppermute | solution.py:80
  345.8 31.0 %collective-permute-start.38 = (bf16[2,528,512]{2,1,0:T(8,128)(2,1)}, bf16[2,528,512]{2,1,0:T(8,128)(2,1)}, u32[]{:S(2)}, u32[]{:S(2)}) collective-permute-start(bf16[2,528,512]{2,1,0:T(8,128)(2,1)} %dynamic-slice_bitcast_fusion.2), channel_id=1, source_target_pairs={{0,16},{8,24},{16,0},{24,8},{1,17},{9,25},{17,1},{25,9},{2,18},{10... | collective-permute-start | bytes 3244040 | tf_op jit(solution)/shard_map/ppermute | solution.py:273
  347.9 28.9 %collective-permute-start.37 = (bf16[2,528,512]{2,1,0:T(8,128)(2,1)}, bf16[2,528,512]{2,1,0:T(8,128)(2,1)}, u32[]{:S(2)}, u32[]{:S(2)}) collective-permute-start(bf16[2,528,512]{2,1,0:T(8,128)(2,1)} %dynamic-slice_bitcast_fusion.3), channel_id=1, source_target_pairs={{0,8},{8,0},{16,24},{24,16},{1,9},{9,1},{17,25},{25,17},{2,10},{10... | collective-permute-start | bytes 3244040 | tf_op jit(solution)/shard_map/ppermute | solution.py:273
  378.2 13.7 %collective-permute-start.41 = (bf16[528,512]{1,0:T(8,128)(2,1)S(1)}, bf16[528,512]{1,0:T(8,128)(2,1)S(1)}, u32[]{:S(2)}, u32[]{:S(2)}) collective-permute-start(bf16[528,512]{1,0:T(8,128)(2,1)S(1)} %fusion.10), channel_id=1, source_target_pairs={{0,8},{8,0},{16,24},{24,16},{1,9},{9,1},{17,25},{25,17},{2,10},{10... | collective-permute-start | bytes 1622024 | tf_op jit(solution)/shard_map/ppermute | solution.py:273
  381.1 13.7 %collective-permute-start.40 = (bf16[528,512]{1,0:T(8,128)(2,1)S(1)}, bf16[528,512]{1,0:T(8,128)(2,1)S(1)}, u32[]{:S(2)}, u32[]{:S(2)}) collective-permute-start(bf16[528,512]{1,0:T(8,128)(2,1)S(1)} %fusion.11), channel_id=1, source_target_pairs={{0,16},{8,24},{16,0},{24,8},{1,17},{9,25},{17,1},{25,9},{2,18},{10... | collective-permute-start | bytes 1622024 | tf_op jit(solution)/shard_map/ppermute | solution.py:273
  463.6 23.6 %collective-permute-start.43 = (bf16[400,1024]{1,0:T(8,128)(2,1)}, bf16[400,1024]{1,0:T(8,128)(2,1)S(1)}, u32[]{:S(2)}, u32[]{:S(2)}) collective-permute-start(bf16[400,1024]{1,0:T(8,128)(2,1)} %reduce-scatter.5.cloned.1.call-done.mine), channel_id=1, source_target_pairs={{0,8},{8,0},{16,24},{24,16},{1,9},{9,1},{17,25},{25,17},{2,10},{10... | collective-permute-start | bytes 2457608 | tf_op jit(solution)/shard_map/ppermute | solution.py:273
  465.1 22.1 %collective-permute-start.44 = (bf16[400,1024]{1,0:T(8,128)(2,1)}, bf16[400,1024]{1,0:T(8,128)(2,1)S(1)}, u32[]{:S(2)}, u32[]{:S(2)}) collective-permute-start(bf16[400,1024]{1,0:T(8,128)(2,1)} %reduce-scatter.5.cloned.1.call-done.mine), channel_id=1, source_target_pairs={{0,16},{8,24},{16,0},{24,8},{1,17},{9,25},{17,1},{25,9},{2,18},{10... | collective-permute-start | bytes 2457608 | tf_op jit(solution)/shard_map/ppermute | solution.py:273
  467.4 19.8 %collective-permute-start.45 = (bf16[128,1024]{1,0:T(8,128)(2,1)}, bf16[128,1024]{1,0:T(8,128)(2,1)S(1)}, u32[]{:S(2)}, u32[]{:S(2)}) collective-permute-start(bf16[128,1024]{1,0:T(8,128)(2,1)} %get-tuple-element.298), channel_id=1, source_target_pairs={{0,4},{2,6},{4,0},{6,2},{1,5},{3,7},{5,1},{7,3},{8,12},{10,14},{12... | collective-permute-start | bytes 786440 | tf_op jit(solution)/shard_map/ppermute | solution.py:80
  469.9 17.3 %collective-permute-start.46 = (bf16[128,1024]{1,0:T(8,128)(2,1)}, bf16[128,1024]{1,0:T(8,128)(2,1)S(1)}, u32[]{:S(2)}, u32[]{:S(2)}) collective-permute-start(bf16[128,1024]{1,0:T(8,128)(2,1)} %get-tuple-element.297), channel_id=1, source_target_pairs={{0,2},{2,4},{4,6},{6,0},{1,3},{3,5},{5,7},{7,1},{8,10},{10,12},{12... | collective-permute-start | bytes 786440 | tf_op jit(solution)/shard_map/ppermute | solution.py:80
  (79 other events, 573.5 us)
Sparse Core Ops, SparseCore 0:
  270.6 90.0 reduce-scatter.2
  401.5 62.1 reduce-scatter.4

commit v6 on v5

--- a/solution.py
+++ b/solution.py
@@ -371,8 +371,8 @@
     rows = pl.ds(pl.multiple_of((core + block // 2) * PAIR, PAIR), PAIR)
     plain = jnp.logical_and(block != 1, jnp.logical_or(block == 2, jnp.logical_not(turned)))
     for n in range(QUARTERS):
-        slot = pl.ds(pl.multiple_of((d % 2 ^ (n % 2)) * PAIR, PAIR), PAIR)
-        ours = pair == n // 2
+        slot = pl.ds(pl.multiple_of((d ^ n) * PAIR, PAIR), PAIR)
+        ours = pair == 0
 
         @pl.when(ours & (block == 1) & jnp.logical_not(turned))
         def _(n=n, slot=slot):
@@ -411,12 +411,12 @@
 def update_weights(values, middle, weights, first_weights, second_weights, turned, core):
     d = lax.axis_index("dp")
     where = jnp.stack([d, core, turned.astype(jnp.int32)]).astype(jnp.int32)
-    rows = pl.BlockSpec((2 * PAIR, D), lambda b, n, where: (b * 2 + (where[0] // 2 ^ n), 0))
+    rows = pl.BlockSpec((BLOCK, D), lambda b, n, where: (b, 0))
     return pl.pallas_call(
         update_kernel,
         grid_spec=pltpu.PrefetchScalarGridSpec(
             num_scalar_prefetch=1,
-            grid=(3, 2),
+            grid=(3, 1),
             in_specs=[pl.BlockSpec(value.shape, lambda b, n, where: (0, 0)) for value in values]
             + [pl.BlockSpec(middle.shape, lambda b, n, where: (0, 0, 0))]
             + [rows] * 3,

time: 538 us -> 538 us (level)
  no operation moved by 1% of the time
where the time goes in v6:
time: 538 us; the launch traced here: 531 us
  waiting for transfers between devices  207 us (38%)
  Pallas kernels  159 us (30%)
  starting transfers between devices  59.3 us (11%)
  local copies, waits for them, and re-layouts  39.6 us (7%)
  other arithmetic  37.8 us (7%)
  between operations  15.3 us (3%)
  matrix products  13.4 us (2%)
    ppermute x20, waiting for transfers between devices, across(): return lax.ppermute(value, 'dp', [(i, i ^ bit) for i in range(4)])  68.3 us
    reduce_scatter x1, waiting for transfers between devices, shards(): piece = lax.psum_scatter(chips, 'z', scatter_dimension=0, tiled=True)  62.3 us
    ppermute x7, waiting for transfers between devices, along_z(): return lax.ppermute(value, 'z', pairs)  32.6 us
    pallas_call x1, Pallas kernels, attention_backward(): pl.pallas_call(backward_kernel, grid=(HALF // PAIR, rows // step), in_spe...  30.5 us
    pallas_call x1, Pallas kernels, feed_backward(): pl.pallas_call(feed_backward_kernel, grid=(QUARTERS,), in_specs=[*[whole_...  29.1 us
    ppermute x20, starting transfers between devices, across(): return lax.ppermute(value, 'dp', [(i, i ^ bit) for i in range(4)])  20 us
    ppermute x6, waiting for transfers between devices, from_chip(): lax.ppermute(part, 'z', [(i, (i - shift) % count) for i in range(count)])  19.4 us
    pallas_call x1, Pallas kernels, feed_forward(): pl.pallas_call(feed_forward_kernel, grid=(QUARTERS,), in_specs=[SCALAR, w...  19 us
  transfers between devices with their start and end apart: 53, of which 30 were waited for; matrix products, arithmetic and copies ran while one was open for 12% of the time, Pallas kernels for 13%

profile of v6, /device:TPU:0, one launch (start us, length us, event | category | flops | bytes accessed | tf_op | source)
XLA Modules:
  0.0 531.5 jit_solution(1233107373645498930)
XLA Ops:
  7.3 5.9 %shard_map.168 = (bf16[1024,1024]{1,0:T(8,128)(2,1)}, bf16[512,1024]{1,0:T(8,128)(2,1)}) custom-call(s32[1]{0:T(128)} %bitcast.3.flag_ref, f32[1536,1024]{1,0:T(8,128)} %weight_ref.1, f32[1536,1024]{1,0:T(8,128)} %weight_ref.1), custom_call_target="tpu_custom_call" | custom-call | flops 1 | bytes 1 | tf_op jit(solution)/shard_map/pallas_call | solution.py:123
  13.6 3.7 collective-permute-start.2
  19.6 5.3 shard_map.169
  24.8 5.0 collective-permute-done.2
  29.9 3.6 collective-permute-start.3
  34.7 15.8 %collective-permute-done.3 = bf16[400,1024]{1,0:T(8,128)(2,1)} collective-permute-done((bf16[400,1024]{1,0:T(8,128)(2,1)}, bf16[400,1024]{1,0:T(8,128)(2,1)}, u32[]{:S(2)}, u32[]{:S(2)}) %collective-permute-start.3) | collective-permute-done | bytes 819232 | tf_op jit(solution)/shard_map/ppermute | solution.py:281
  50.5 4.9 collective-permute-done.4
  61.4 13.2 %collective-permute-done.5.got_x = bf16[400,1024]{1,0:T(8,128)(2,1)S(1)} collective-permute-done((bf16[400,1024]{1,0:T(8,128)(2,1)S(1)}, bf16[400,1024]{1,0:T(8,128)(2,1)S(1)}, u32[]{:S(2)}, u32[]{:S(2)}) %collective-permute-start.5) | collective-permute-done | bytes 819232 | tf_op jit(solution)/shard_map/ppermute | solution.py:273
  75.8 8.1 %collective-permute-done.8 = bf16[400,1024]{1,0:T(8,128)(2,1)S(1)} collective-permute-done((bf16[400,1024]{1,0:T(8,128)(2,1)S(1)}, bf16[400,1024]{1,0:T(8,128)(2,1)S(1)}, u32[]{:S(2)}, u32[]{:S(2)}) %collective-permute-start.8) | collective-permute-done | bytes 819232 | tf_op jit(solution)/shard_map/ppermute | solution.py:281
  88.1 7.3 %collective-permute-done.10.far_b = bf16[400,512]{1,0:T(8,128)(2,1)} collective-permute-done((bf16[400,512]{1,0:T(8,128)(2,1)}, bf16[400,512]{1,0:T(8,128)(2,1)}, u32[]{:S(2)}, u32[]{:S(2)}) %collective-permute-start.10) | collective-permute-done | bytes 409632 | tf_op jit(solution)/shard_map/ppermute | solution.py:273
  103.4 4.8 shard_map.170.whole_in
  108.2 6.2 %collective-permute-done.12.got_x = bf16[400,1024]{1,0:T(8,128)(2,1)} collective-permute-done((bf16[400,1024]{1,0:T(8,128)(2,1)S(1)}, bf16[400,1024]{1,0:T(8,128)(2,1)}, u32[]{:S(2)}, u32[]{:S(2)}) %collective-permute-start.12) | collective-permute-done | bytes 819232 | tf_op jit(solution)/shard_map/ppermute | solution.py:273
  115.5 3.8 collective-permute-done.15
  123.6 5.8 %collective-permute-start.19 = (bf16[128,1024]{1,0:T(8,128)(2,1)S(1)}, bf16[128,1024]{1,0:T(8,128)(2,1)S(1)}, u32[]{:S(2)}, u32[]{:S(2)}) collective-permute-start(bf16[128,1024]{1,0:T(8,128)(2,1)S(1)} %get-tuple-element.308), channel_id=1, source_target_pairs={{0,6},{2,0},{4,2},{6,4},{1,7},{3,1},{5,3},{7,5},{8,14},{10,8},{12,... | collective-permute-start | bytes 786440 | tf_op jit(solution)/shard_map/ppermute | solution.py:68
  129.5 4.4 collective-permute-done.18
  141.7 4.8 shard_map.171.w_ref.whole_in
  151.4 8.0 %shard_map.172.q_ref.k_ref.v_ref = bf16[1024,1536]{1,0:T(8,128)(2,1)} custom-call(s32[1]{0:T(128)} %bitcast.2.core_ref, bf16[512,1024]{1,0:T(8,128)(2,1)} %copy-done.5, bf16[512,1024]{1,0:T(8,128)(2,1)} %collective-permute-done.22.x_other, bf16[16,400,1024]{2,1,0:T(8,128)(2,1)} %shard_map.171.w_ref.whole_in, f32[24,128]{1,0:T(8,128)} %reshape.324.vector_ref), custom_call_target="tpu_custom_call" | custom-call | flops 1 | bytes 1 | tf_op jit(solution)/shard_map/pallas_call | solution.py:466
  169.7 17.5 %shard_map.173 = (bf16[1024,512]{1,0:T(8,128)(2,1)}, bf16[1024,512]{1,0:T(8,128)(2,1)}) custom-call(bf16[1024,1536]{1,0:T(8,128)(2,1)} %shard_map.172.q_ref.k_ref.v_ref, bf16[1024,1536]{1,0:T(8,128)(2,1)} %shard_map.172.q_ref.k_ref.v_ref, bf16[1024,1536]{1,0:T(8,128)(2,1)} %shard_map.172.q_ref.k_ref.v_ref, bf16[1024,128]{1,0:T(8,128)(2,1)} %select_convert_fusion.key_ref), custom_call_target="tpu_custom_call" | custom-call | flops 1 | bytes 1 | tf_op jit(solution)/shard_map/pallas_call | solution.py:517
  187.3 4.8 shard_map.174.w0.w1.w2.w3.up0.up1.up2.down0.down1
  192.1 4.7 shard_map.175
  206.8 19.0 %shard_map.176 = (bf16[1024,2048]{1,0:T(8,128)(2,1)}, bf16[1024,2048]{1,0:T(8,128)(2,1)}, f32[512,1024]{1,0:T(8,128)}, bf16[512,1024]{1,0:T(8,128)(2,1)}) custom-call(s32[1]{0:T(128)} %bitcast.2.core_ref, bf16[512,1024]{1,0:T(8,128)(2,1)} %copy-done.4, bf16[512,1024]{1,0:T(8,128)(2,1)} %collective-permute-done.29.u_other, ...), custom_call_target="tpu_custom_call" | custom-call | flops 1 | bytes 1 | tf_op jit(solution)/shard_map/pallas_call | solution.py:652
  241.3 29.1 %shard_map.177 = (bf16[4,1024,1024]{2,1,0:T(8,128)(2,1)}, f32[1,2048]{1,0:T(1,128)}, f32[512,1024]{1,0:T(8,128)}, bf16[512,1024]{1,0:T(8,128)(2,1)}) custom-call(bf16[512,1024]{1,0:T(8,128)(2,1)} %copy-done.7, bf16[512,1024]{1,0:T(8,128)(2,1)} %copy-done.29, bf16[512,1024]{1,0:T(8,128)(2,1)} %copy-done.4, bf16[512,1024]{1,0:T(8,128)(2,1)} %collective-permute-done.29.u_other, ...), custom_call_target="tpu_custom_call" | custom-call | flops 1 | bytes 1 | tf_op jit(solution)/shard_map/pallas_call | solution.py:744
  273.5 4.7 multiply_reduce_fusion.1
  293.9 30.5 %shard_map.178 = bf16[1024,1536]{1,0:T(8,128)(2,1)} custom-call(bf16[1024,1536]{1,0:T(8,128)(2,1)} %shard_map.172.q_ref.k_ref.v_ref, bf16[1024,512]{1,0:T(8,128)(2,1)} %get-tuple-element.202.extra_ref, bf16[1024,1536]{1,0:T(8,128)(2,1)} %shard_map.172.q_ref.k_ref.v_ref, bf16[1024,1536]{1,0:T(8,128)(2,1)} %shard_map.172.q_ref.k_ref.v_ref, ...), custom_call_target="tpu_custom_call" | custom-call | flops 1 | bytes 1 | tf_op jit(solution)/shard_map/pallas_call | solution.py:581
  330.9 5.4 %convolution_convert_fusion = bf16[1536,1024]{1,0:T(8,128)(2,1)S(1)} fusion(bf16[1024,1536]{1,0:T(8,128)(2,1)S(1)} %copy-done.1, bf16[512,1024]{1,0:T(8,128)(2,1)} %collective-permute-done.22.x_other, bf16[512,1024]{1,0:T(8,128)(2,1)} %copy-done.5), kind=kOutput, calls=%fused_computation.4 | convolution fusion | flops 3226992640 | bytes 8388608 | tf_op jit(solution)/shard_map/dot_general | solution.py:35
  351.4 25.4 %collective-permute-done.38.got_b = bf16[2,528,512]{2,1,0:T(8,128)(2,1)} collective-permute-done((bf16[2,528,512]{2,1,0:T(8,128)(2,1)}, bf16[2,528,512]{2,1,0:T(8,128)(2,1)}, u32[]{:S(2)}, u32[]{:S(2)}) %collective-permute-start.38) | collective-permute-done | bytes 1081376 | tf_op jit(solution)/shard_map/ppermute | solution.py:273
  382.3 3.6 collective-permute-start.42
  395.6 5.8 %shard_map.179 = bf16[1600,1024]{1,0:T(8,128)(2,1)} custom-call(s32[2]{0:T(128)} %pad_add_fusion.4.where_ref, bf16[2,528,512]{2,1,0:T(8,128)(2,1)} %dynamic-slice_bitcast_fusion.1.a, bf16[2,528,512]{2,1,0:T(8,128)(2,1)} %collective-permute-done.37.got_a, bf16[528,512]{1,0:T(8,128)(2,1)} %copy-done.40, bf16[2,528,512]{2,1,0:T(8,128)(2,1)} %dynamic-slice_bitcast_fusion.b, ...), custom_call_target="tpu_custom_call" | custom-call | flops 1 | bytes 1 | tf_op jit(solution)/shard_map/pallas_call | solution.py:328
  401.4 62.3 %reduce-scatter.5.cloned.1.call-done.mine = bf16[400,1024]{1,0:T(8,128)(2,1)} async-done(((bf16[1600,1024]{1,0:T(8,128)(2,1)}), bf16[400,1024]{1,0:T(8,128)(2,1)}) %reduce-scatter.5.cloned.1.call-update) | async-done | bytes 819216 | tf_op jit(solution)/shard_map/reduce_scatter | solution.py:960
  470.4 16.8 %collective-permute-done.45 = bf16[128,1024]{1,0:T(8,128)(2,1)S(1)} collective-permute-done((bf16[128,1024]{1,0:T(8,128)(2,1)}, bf16[128,1024]{1,0:T(8,128)(2,1)S(1)}, u32[]{:S(2)}, u32[]{:S(2)}) %collective-permute-start.45) | collective-permute-done | bytes 262176 | tf_op jit(solution)/shard_map/ppermute | solution.py:80
  490.5 8.3 %collective-permute-done.47.far_a = bf16[400,512]{1,0:T(8,128)(2,1)S(1)} collective-permute-done((bf16[400,512]{1,0:T(8,128)(2,1)S(1)}, bf16[400,512]{1,0:T(8,128)(2,1)S(1)}, u32[]{:S(2)}, u32[]{:S(2)}) %collective-permute-start.47) | collective-permute-done | bytes 409632 | tf_op jit(solution)/shard_map/ppermute | solution.py:273
  505.6 18.8 %shard_map.180 = (f32[1536,1024]{1,0:T(8,128)}, f32[1536,1024]{1,0:T(8,128)}, f32[1536,1024]{1,0:T(8,128)}, f32[1536,1024]{1,0:T(8,128)}) custom-call(s32[3]{0:T(128)} %pad_add_fusion.5.where_ref, bf16[400,1024]{1,0:T(8,128)(2,1)} %reduce-scatter.5.cloned.1.call-done.mine, bf16[400,1024]{1,0:T(8,128)(2,1)} %copy-done.12, bf16[400,1024]{1,0:T(8,128)(2,1)} %copy-done.13, ...), custom_call_target="tpu_custom_call" | custom-call | flops 1 | bytes 1 | tf_op jit(solution)/shard_map/pallas_call | solution.py:415
  (342 shorter events, 149.1 us)
Async XLA Ops:
  7.2 369.7 %reduce-scatter.3.cloned.1.call-start = ((), (), s32[]{:S(2)}) async-start(), calls=%async_computation.2 | async-start | bytes 10485760 | tf_op jit(solution)/shard_map/reduce_scatter | solution.py:261
  13.6 16.2 %collective-permute-start.2 = (bf16[128,1024]{1,0:T(8,128)(2,1)S(1)}, bf16[128,1024]{1,0:T(8,128)(2,1)S(1)}, u32[]{:S(2)}, u32[]{:S(2)}) collective-permute-start(bf16[128,1024]{1,0:T(8,128)(2,1)S(1)} %get-tuple-element.310), channel_id=1, source_target_pairs={{0,4},{2,6},{4,0},{6,2},{1,5},{3,7},{5,1},{7,3},{8,12},{10,14},{12... | collective-permute-start | bytes 786440 | tf_op jit(solution)/shard_map/ppermute | solution.py:68
  29.9 20.7 %collective-permute-start.3 = (bf16[400,1024]{1,0:T(8,128)(2,1)}, bf16[400,1024]{1,0:T(8,128)(2,1)}, u32[]{:S(2)}, u32[]{:S(2)}) collective-permute-start(bf16[400,1024]{1,0:T(8,128)(2,1)} %get-tuple-element.143), channel_id=1, source_target_pairs={{0,2},{2,4},{4,6},{1,3},{3,5},{5,7},{8,10},{10,12},{12,14},{9,11},... | collective-permute-start | bytes 2457608 | tf_op jit(solution)/shard_map/ppermute | solution.py:281
  33.4 22.0 %collective-permute-start.4 = (bf16[400,1024]{1,0:T(8,128)(2,1)}, bf16[400,1024]{1,0:T(8,128)(2,1)S(1)}, u32[]{:S(2)}, u32[]{:S(2)}) collective-permute-start(bf16[400,1024]{1,0:T(8,128)(2,1)} %get-tuple-element.143), channel_id=1, source_target_pairs={{2,0},{4,2},{6,4},{3,1},{5,3},{7,5},{10,8},{12,10},{14,12},{11,9},... | collective-permute-start | bytes 2457608 | tf_op jit(solution)/shard_map/ppermute | solution.py:281
  55.5 19.1 %collective-permute-start.5 = (bf16[400,1024]{1,0:T(8,128)(2,1)S(1)}, bf16[400,1024]{1,0:T(8,128)(2,1)S(1)}, u32[]{:S(2)}, u32[]{:S(2)}) collective-permute-start(bf16[400,1024]{1,0:T(8,128)(2,1)S(1)} %broadcast_select_fusion.mine), channel_id=1, source_target_pairs={{0,8},{8,0},{16,24},{24,16},{1,9},{9,1},{17,25},{25,17},{2,10},{10... | collective-permute-start | bytes 2457608 | tf_op jit(solution)/shard_map/ppermute | solution.py:273
  57.1 18.7 %collective-permute-start.6 = (bf16[400,1024]{1,0:T(8,128)(2,1)S(1)}, bf16[400,1024]{1,0:T(8,128)(2,1)S(1)}, u32[]{:S(2)}, u32[]{:S(2)}) collective-permute-start(bf16[400,1024]{1,0:T(8,128)(2,1)S(1)} %broadcast_select_fusion.mine), channel_id=1, source_target_pairs={{0,16},{8,24},{16,0},{24,8},{1,17},{9,25},{17,1},{25,9},{2,18},{10... | collective-permute-start | bytes 2457608 | tf_op jit(solution)/shard_map/ppermute | solution.py:273
  58.6 17.2 %collective-permute-start.7 = (bf16[400,1024]{1,0:T(8,128)(2,1)}, bf16[400,1024]{1,0:T(8,128)(2,1)}, u32[]{:S(2)}, u32[]{:S(2)}) collective-permute-start(bf16[400,1024]{1,0:T(8,128)(2,1)} %collective-permute-done.3), channel_id=1, source_target_pairs={{2,4},{3,5},{10,12},{11,13},{18,20},{19,21},{26,28},{27,29}} | collective-permute-start | bytes 2457608 | tf_op jit(solution)/shard_map/ppermute | solution.py:281
  60.2 23.8 %collective-permute-start.8 = (bf16[400,1024]{1,0:T(8,128)(2,1)S(1)}, bf16[400,1024]{1,0:T(8,128)(2,1)S(1)}, u32[]{:S(2)}, u32[]{:S(2)}) collective-permute-start(bf16[400,1024]{1,0:T(8,128)(2,1)S(1)} %collective-permute-done.4), channel_id=1, source_target_pairs={{2,0},{4,2},{3,1},{5,3},{10,8},{12,10},{11,9},{13,11},{18,16},{20,... | collective-permute-start | bytes 2457608 | tf_op jit(solution)/shard_map/ppermute | solution.py:281
  97.8 16.6 %collective-permute-start.12 = (bf16[400,1024]{1,0:T(8,128)(2,1)S(1)}, bf16[400,1024]{1,0:T(8,128)(2,1)}, u32[]{:S(2)}, u32[]{:S(2)}) collective-permute-start(bf16[400,1024]{1,0:T(8,128)(2,1)S(1)} %select_select_fusion.1.mine), channel_id=1, source_target_pairs={{0,8},{8,0},{16,24},{24,16},{1,9},{9,1},{17,25},{25,17},{2,10},{10... | collective-permute-start | bytes 2457608 | tf_op jit(solution)/shard_map/ppermute | solution.py:273
  99.3 16.1 %collective-permute-start.13 = (bf16[400,1024]{1,0:T(8,128)(2,1)S(1)}, bf16[400,1024]{1,0:T(8,128)(2,1)S(1)}, u32[]{:S(2)}, u32[]{:S(2)}) collective-permute-start(bf16[400,1024]{1,0:T(8,128)(2,1)S(1)} %select_select_fusion.1.mine), channel_id=1, source_target_pairs={{0,16},{8,24},{16,0},{24,8},{1,17},{9,25},{17,1},{25,9},{2,18},{10... | collective-permute-start | bytes 2457608 | tf_op jit(solution)/shard_map/ppermute | solution.py:273
  99.9 15.6 %collective-permute-start.14 = (bf16[400,1024]{1,0:T(8,128)(2,1)}, bf16[400,1024]{1,0:T(8,128)(2,1)}, u32[]{:S(2)}, u32[]{:S(2)}) collective-permute-start(bf16[400,1024]{1,0:T(8,128)(2,1)} %collective-permute-done.3), channel_id=1, source_target_pairs={{4,6},{5,7},{12,14},{13,15},{20,22},{21,23},{28,30},{29,31}} | collective-permute-start | bytes 2457608 | tf_op jit(solution)/shard_map/ppermute | solution.py:281
  101.4 17.8 %collective-permute-start.15 = (bf16[400,1024]{1,0:T(8,128)(2,1)S(1)}, bf16[400,1024]{1,0:T(8,128)(2,1)}, u32[]{:S(2)}, u32[]{:S(2)}) collective-permute-start(bf16[400,1024]{1,0:T(8,128)(2,1)S(1)} %collective-permute-done.8), channel_id=1, source_target_pairs={{2,0},{3,1},{10,8},{11,9},{18,16},{19,17},{26,24},{27,25}} | collective-permute-start | bytes 2457608 | tf_op jit(solution)/shard_map/ppermute | solution.py:281
  120.2 14.9 %collective-permute-start.16 = (bf16[400,512]{1,0:T(8,128)(2,1)S(1)}, bf16[400,512]{1,0:T(8,128)(2,1)S(1)}, u32[]{:S(2)}, u32[]{:S(2)}) collective-permute-start(bf16[400,512]{1,0:T(8,128)(2,1)S(1)} %slice.156), channel_id=1, source_target_pairs={{0,16},{8,24},{16,0},{24,8},{1,17},{9,25},{17,1},{25,9},{2,18},{10... | collective-permute-start | bytes 1228808 | tf_op jit(solution)/shard_map/ppermute | solution.py:273
  136.0 15.4 %collective-permute-start.22 = (bf16[512,1024]{1,0:T(8,128)(2,1)S(1)}, bf16[512,1024]{1,0:T(8,128)(2,1)}, u32[]{:S(2)}, u32[]{:S(2)}) collective-permute-start(bf16[512,1024]{1,0:T(8,128)(2,1)S(1)} %constant_dynamic-update-slice_fusion.x_mine), channel_id=1, source_target_pairs={{0,1},{1,0},{2,3},{3,2},{4,5},{5,4},{6,7},{7,6},{8,9},{9,8},{10,11... | collective-permute-start | bytes 3145736 | tf_op jit(solution)/shard_map/ppermute | solution.py:43
  138.8 20.6 %collective-permute-start.20 = (bf16[400,1024]{1,0:T(8,128)(2,1)}, bf16[400,1024]{1,0:T(8,128)(2,1)S(1)}, u32[]{:S(2)}, u32[]{:S(2)}) collective-permute-start(bf16[400,1024]{1,0:T(8,128)(2,1)} %select_select_fusion.mine), channel_id=1, source_target_pairs={{0,8},{8,0},{16,24},{24,16},{1,9},{9,1},{17,25},{25,17},{2,10},{10... | collective-permute-start | bytes 2457608 | tf_op jit(solution)/shard_map/ppermute | solution.py:273
  139.4 20.2 %collective-permute-start.21 = (bf16[400,1024]{1,0:T(8,128)(2,1)}, bf16[400,1024]{1,0:T(8,128)(2,1)S(1)}, u32[]{:S(2)}, u32[]{:S(2)}) collective-permute-start(bf16[400,1024]{1,0:T(8,128)(2,1)} %select_select_fusion.mine), channel_id=1, source_target_pairs={{0,16},{8,24},{16,0},{24,8},{1,17},{9,25},{17,1},{25,9},{2,18},{10... | collective-permute-start | bytes 2457608 | tf_op jit(solution)/shard_map/ppermute | solution.py:273
  160.5 26.8 %collective-permute-start.24 = (bf16[400,512]{1,0:T(8,128)(2,1)}, bf16[400,512]{1,0:T(8,128)(2,1)}, u32[]{:S(2)}, u32[]{:S(2)}) collective-permute-start(bf16[400,512]{1,0:T(8,128)(2,1)} %slice.160), channel_id=1, source_target_pairs={{0,16},{8,24},{16,0},{24,8},{1,17},{9,25},{17,1},{25,9},{2,18},{10... | collective-permute-start | bytes 1228808 | tf_op jit(solution)/shard_map/ppermute | solution.py:273
  162.6 24.7 %collective-permute-start.25 = (bf16[400,512]{1,0:T(8,128)(2,1)}, bf16[400,512]{1,0:T(8,128)(2,1)}, u32[]{:S(2)}, u32[]{:S(2)}) collective-permute-start(bf16[400,512]{1,0:T(8,128)(2,1)} %slice.161), channel_id=1, source_target_pairs={{0,8},{8,0},{16,24},{24,16},{1,9},{9,1},{17,25},{25,17},{2,10},{10... | collective-permute-start | bytes 1228808 | tf_op jit(solution)/shard_map/ppermute | solution.py:273
  165.0 22.3 %collective-permute-start.26 = (bf16[128,1024]{1,0:T(8,128)(2,1)}, bf16[128,1024]{1,0:T(8,128)(2,1)S(1)}, u32[]{:S(2)}, u32[]{:S(2)}) collective-permute-start(bf16[128,1024]{1,0:T(8,128)(2,1)} %get-tuple-element.305), channel_id=1, source_target_pairs={{0,4},{2,6},{4,0},{6,2},{1,5},{3,7},{5,1},{7,3},{8,12},{10,14},{12... | collective-permute-start | bytes 786440 | tf_op jit(solution)/shard_map/ppermute | solution.py:68
  167.1 20.2 %collective-permute-start.27 = (bf16[128,1024]{1,0:T(8,128)(2,1)}, bf16[128,1024]{1,0:T(8,128)(2,1)S(1)}, u32[]{:S(2)}, u32[]{:S(2)}) collective-permute-start(bf16[128,1024]{1,0:T(8,128)(2,1)} %get-tuple-element.304), channel_id=1, source_target_pairs={{0,6},{2,0},{4,2},{6,4},{1,7},{3,1},{5,3},{7,5},{8,14},{10,8},{12,... | collective-permute-start | bytes 786440 | tf_op jit(solution)/shard_map/ppermute | solution.py:68
  270.5 193.2 %reduce-scatter.5.cloned.1.call-start = ((), (), s32[]{:S(2)}) async-start(), calls=%async_computation.3 | async-start | bytes 4096000 | tf_op jit(solution)/shard_map/reduce_scatter | solution.py:960
  286.0 38.5 %collective-permute-start.34 = (bf16[128,1024]{1,0:T(8,128)(2,1)S(1)}, bf16[128,1024]{1,0:T(8,128)(2,1)S(1)}, u32[]{:S(2)}, u32[]{:S(2)}) collective-permute-start(bf16[128,1024]{1,0:T(8,128)(2,1)S(1)} %get-tuple-element.303), channel_id=1, source_target_pairs={{0,6},{2,0},{4,2},{6,4},{1,7},{3,1},{5,3},{7,5},{8,14},{10,8},{12,... | collective-permute-start | bytes 786440 | tf_op jit(solution)/shard_map/ppermute | solution.py:80
  287.2 37.9 %collective-permute-start.35 = (bf16[128,1024]{1,0:T(8,128)(2,1)}, bf16[128,1024]{1,0:T(8,128)(2,1)}, u32[]{:S(2)}, u32[]{:S(2)}) collective-permute-start(bf16[128,1024]{1,0:T(8,128)(2,1)} %get-tuple-element.302), channel_id=1, source_target_pairs={{0,4},{2,6},{4,0},{6,2},{1,5},{3,7},{5,1},{7,3},{8,12},{10,14},{12... | collective-permute-start | bytes 786440 | tf_op jit(solution)/shard_map/ppermute | solution.py:80
  288.5 38.5 %collective-permute-start.36 = (bf16[128,1024]{1,0:T(8,128)(2,1)}, bf16[128,1024]{1,0:T(8,128)(2,1)S(1)}, u32[]{:S(2)}, u32[]{:S(2)}) collective-permute-start(bf16[128,1024]{1,0:T(8,128)(2,1)} %get-tuple-element.301), channel_id=1, source_target_pairs={{0,2},{2,4},{4,6},{6,0},{1,3},{3,5},{5,7},{7,1},{8,10},{10,12},{12... | collective-permute-start | bytes 786440 | tf_op jit(solution)/shard_map/ppermute | solution.py:80
  345.8 31.0 %collective-permute-start.38 = (bf16[2,528,512]{2,1,0:T(8,128)(2,1)}, bf16[2,528,512]{2,1,0:T(8,128)(2,1)}, u32[]{:S(2)}, u32[]{:S(2)}) collective-permute-start(bf16[2,528,512]{2,1,0:T(8,128)(2,1)} %dynamic-slice_bitcast_fusion.2), channel_id=1, source_target_pairs={{0,16},{8,24},{16,0},{24,8},{1,17},{9,25},{17,1},{25,9},{2,18},{10... | collective-permute-start | bytes 3244040 | tf_op jit(solution)/shard_map/ppermute | solution.py:273
  347.9 28.9 %collective-permute-start.37 = (bf16[2,528,512]{2,1,0:T(8,128)(2,1)}, bf16[2,528,512]{2,1,0:T(8,128)(2,1)}, u32[]{:S(2)}, u32[]{:S(2)}) collective-permute-start(bf16[2,528,512]{2,1,0:T(8,128)(2,1)} %dynamic-slice_bitcast_fusion.3), channel_id=1, source_target_pairs={{0,8},{8,0},{16,24},{24,16},{1,9},{9,1},{17,25},{25,17},{2,10},{10... | collective-permute-start | bytes 3244040 | tf_op jit(solution)/shard_map/ppermute | solution.py:273
  378.2 13.7 %collective-permute-start.41 = (bf16[528,512]{1,0:T(8,128)(2,1)S(1)}, bf16[528,512]{1,0:T(8,128)(2,1)S(1)}, u32[]{:S(2)}, u32[]{:S(2)}) collective-permute-start(bf16[528,512]{1,0:T(8,128)(2,1)S(1)} %fusion.10), channel_id=1, source_target_pairs={{0,8},{8,0},{16,24},{24,16},{1,9},{9,1},{17,25},{25,17},{2,10},{10... | collective-permute-start | bytes 1622024 | tf_op jit(solution)/shard_map/ppermute | solution.py:273
  381.1 13.7 %collective-permute-start.40 = (bf16[528,512]{1,0:T(8,128)(2,1)S(1)}, bf16[528,512]{1,0:T(8,128)(2,1)S(1)}, u32[]{:S(2)}, u32[]{:S(2)}) collective-permute-start(bf16[528,512]{1,0:T(8,128)(2,1)S(1)} %fusion.11), channel_id=1, source_target_pairs={{0,16},{8,24},{16,0},{24,8},{1,17},{9,25},{17,1},{25,9},{2,18},{10... | collective-permute-start | bytes 1622024 | tf_op jit(solution)/shard_map/ppermute | solution.py:273
  463.6 23.6 %collective-permute-start.43 = (bf16[400,1024]{1,0:T(8,128)(2,1)}, bf16[400,1024]{1,0:T(8,128)(2,1)S(1)}, u32[]{:S(2)}, u32[]{:S(2)}) collective-permute-start(bf16[400,1024]{1,0:T(8,128)(2,1)} %reduce-scatter.5.cloned.1.call-done.mine), channel_id=1, source_target_pairs={{0,8},{8,0},{16,24},{24,16},{1,9},{9,1},{17,25},{25,17},{2,10},{10... | collective-permute-start | bytes 2457608 | tf_op jit(solution)/shard_map/ppermute | solution.py:273
  465.1 22.1 %collective-permute-start.44 = (bf16[400,1024]{1,0:T(8,128)(2,1)}, bf16[400,1024]{1,0:T(8,128)(2,1)S(1)}, u32[]{:S(2)}, u32[]{:S(2)}) collective-permute-start(bf16[400,1024]{1,0:T(8,128)(2,1)} %reduce-scatter.5.cloned.1.call-done.mine), channel_id=1, source_target_pairs={{0,16},{8,24},{16,0},{24,8},{1,17},{9,25},{17,1},{25,9},{2,18},{10... | collective-permute-start | bytes 2457608 | tf_op jit(solution)/shard_map/ppermute | solution.py:273
  467.4 19.8 %collective-permute-start.45 = (bf16[128,1024]{1,0:T(8,128)(2,1)}, bf16[128,1024]{1,0:T(8,128)(2,1)S(1)}, u32[]{:S(2)}, u32[]{:S(2)}) collective-permute-start(bf16[128,1024]{1,0:T(8,128)(2,1)} %get-tuple-element.298), channel_id=1, source_target_pairs={{0,4},{2,6},{4,0},{6,2},{1,5},{3,7},{5,1},{7,3},{8,12},{10,14},{12... | collective-permute-start | bytes 786440 | tf_op jit(solution)/shard_map/ppermute | solution.py:80
  469.9 17.3 %collective-permute-start.46 = (bf16[128,1024]{1,0:T(8,128)(2,1)}, bf16[128,1024]{1,0:T(8,128)(2,1)S(1)}, u32[]{:S(2)}, u32[]{:S(2)}) collective-permute-start(bf16[128,1024]{1,0:T(8,128)(2,1)} %get-tuple-element.297), channel_id=1, source_target_pairs={{0,2},{2,4},{4,6},{6,0},{1,3},{3,5},{5,7},{7,1},{8,10},{10,12},{12... | collective-permute-start | bytes 786440 | tf_op jit(solution)/shard_map/ppermute | solution.py:80
  (79 other events, 573.5 us)
Sparse Core Ops, SparseCore 0:
  270.6 90.0 reduce-scatter.2
  401.5 62.1 reduce-scatter.4
